TPU v7x, 32 devices: a whole 2x2x4 slice. The times are simulated.
32 devices in a mesh: slab: 2 (over x), samp: 8 (over z, y), tgt: 2 (over core).
Axes of the slice: x: 2, y: 2, z: 4, core: 2. Of those that a mesh axis runs over, the one named last changes fastest.
Arguments:
- coverage: bfloat16 [2048, 1024], P('samp', ('slab', 'tgt')), parts along dimension 1, may hold values from 0.29882812 to 3
- neighbours: int32 [2048, 128], P('samp'), may hold values from 0 to 2047, as said below
- nbr_weight: bfloat16 [2048, 128], P('samp'), may hold values from 0.099609375 to 1
- ploidy: int32 [2048], P('samp'), may hold values from 1 to 2
- gc_bin: int32 [1024], P(('slab', 'tgt')), parts along dimension 0, may hold values from 0 to 7
Outputs:
- copy_number: float32 [2048, 1024], P('samp', ('slab', 'tgt')), parts along dimension 1
There are 2 independent parts, one for each index of `slab`. A program takes and returns all parts, laid end to end along the dimension named above; an argument that names none is the same for every part. Nothing has to cross between parts.
Inputs may be any that keep to these rules, and one draw needn't show every extreme that they name: `neighbours`: row s lists 128 distinct samples other than s. The rows of the 256 samples of one index of samp name, from the samples of each index of samp, only those of one block of 128 samples (block b holds local samples b*128 to b*128 + 127 of that index).
All inputs are finite; a program needn't handle non-finite values.
Results may differ from a plain program's by a relative error of at most 0.00065.
The roundings to bfloat16 on the way count: a program that leaves them out, or rounds other values in their place, can miss the bound.
Values may be sent and summed in bfloat16 or wider, within the bound.
No kernel may reach another device: no remote copies, remote signals or barrier semaphores. Data moves between devices by JAX's collectives and lax.ppermute only.
A program may use at most 64 MiB of HBM per device.

v0:
```python
import math

import jax
import jax.numpy as jnp
from jax import lax
from jax.sharding import PartitionSpec as P

TGT = 512
NGC = 8


LOG_PRIOR = (-4.6051702, -3.2188758, -0.1625189, -2.8134107, -3.5065579, -4.6051702)


def normalize_rows(covf, bin_sum, bin_count, onehot):
    sample_mean = jnp.sum(bin_sum, axis=1) / TGT
    bin_mean = bin_sum / jnp.maximum(bin_count, 1.0)[None, :]
    spread_mean = jnp.dot(bin_mean, onehot.T, precision=lax.Precision.HIGHEST)
    return (covf * (sample_mean[:, None] / spread_mean)).astype(jnp.bfloat16)


def spread_terms(first, second, third):
    ref_mean = second / first
    rel_var = (third / first - ref_mean * ref_mean) / (ref_mean * ref_mean)
    return (ref_mean, rel_var)


def copy_calls(normf, ref_mean, rel_var, plf):
    rel_total = lax.psum(jnp.sum(rel_var, axis=1), "tgt")
    level = 0.5 * rel_var + 0.5 * (rel_total / TGT)[:, None]
    ratio = normf / ref_mean
    scores = []
    for state in range(6):
        centre = max(state, 0.1) / plf
        vari = level * jnp.maximum(centre, 0.25) + 0.01
        delta = ratio - centre
        scores.append(LOG_PRIOR[state] - 0.5 * delta * delta / vari - 0.5 * jnp.log(vari))
    stacked = jnp.stack(scores)
    peak = jnp.max(stacked, axis=0)
    expo = jnp.exp(stacked - peak[None])
    states = jnp.arange(6, dtype=jnp.float32)[:, None, None]
    return jnp.sum(states * expo, axis=0) / jnp.sum(expo, axis=0)


def weighted(weight_map, table):
    return jnp.dot(weight_map, table, preferred_element_type=jnp.float32)


def squared(table):
    tablef = table.astype(jnp.float32)
    return (tablef * tablef).astype(jnp.bfloat16)


def build_map(places, nbr_weight, width):
    low_size = math.gcd(width, 128)
    high_size = width // low_size
    high = places // low_size
    low = places % low_size
    high_one = jnp.where(
        high[:, :, None] == jnp.arange(high_size, dtype=jnp.int32)[None, None, :],
        nbr_weight[:, :, None],
        jnp.zeros((), jnp.bfloat16),
    )
    low_one = (low[:, :, None] == jnp.arange(low_size, dtype=jnp.int32)[None, None, :]).astype(
        jnp.bfloat16
    )
    table = jnp.einsum("skg,skl->sgl", high_one, low_one, preferred_element_type=jnp.float32)
    return table.astype(jnp.bfloat16).reshape(places.shape[0], width)


def body(coverage, neighbours, nbr_weight, ploidy, gc_bin):
    samp_count = lax.axis_size("samp")
    samp_rows, tgt_cols = coverage.shape
    covf = coverage.astype(jnp.float32)
    onehot = (gc_bin[:, None] == jnp.arange(NGC, dtype=jnp.int32)[None, :]).astype(jnp.float32)
    bin_sum = jnp.dot(covf, onehot, precision=lax.Precision.HIGHEST)
    bin_count = jnp.sum(onehot, axis=0)
    bin_sum, bin_count = lax.psum((bin_sum, bin_count), "tgt")
    norm_cov = normalize_rows(covf, bin_sum, bin_count, onehot)
    normf = norm_cov.astype(jnp.float32)
    norm_sq = (normf * normf).astype(jnp.bfloat16)
    plf = ploidy.astype(jnp.float32)[:, None]
    width = samp_rows * samp_count
    near_cov = lax.all_gather(norm_cov, "samp", axis=0, tiled=True)
    near_sq = squared(near_cov)
    weight_map = build_map(neighbours, nbr_weight, width)
    first = jnp.sum(nbr_weight.astype(jnp.float32), axis=1)[:, None] * jnp.ones_like(normf)
    ref_mean, rel_var = spread_terms(
        first, weighted(weight_map, near_cov), weighted(weight_map, near_sq)
    )
    first_call = copy_calls(normf, ref_mean, rel_var, plf)
    offset = first_call - plf
    gate = (1.0 / (1.0 + 4.0 * offset * offset)).astype(jnp.bfloat16)
    gatef = gate.astype(jnp.float32)
    gated_cov = (gatef * normf).astype(jnp.bfloat16)
    gated_sq = (gatef * norm_sq.astype(jnp.float32)).astype(jnp.bfloat16)
    far_gate, far_cov, far_sq = (
        lax.all_gather(gate, "samp", axis=0, tiled=True),
        lax.all_gather(gated_cov, "samp", axis=0, tiled=True),
        lax.all_gather(gated_sq, "samp", axis=0, tiled=True),
    )
    ref_mean, rel_var = spread_terms(
        weighted(weight_map, far_gate), weighted(weight_map, far_cov), weighted(weight_map, far_sq)
    )
    return copy_calls(normf, ref_mean, rel_var, plf)


def solution(mesh):
    in_specs = (
        P("samp", ("slab", "tgt")),
        P("samp", None),
        P("samp", None),
        P("samp"),
        P(("slab", "tgt")),
    )
    out_specs = P("samp", ("slab", "tgt"))
    return jax.shard_map(body, mesh=mesh, in_specs=in_specs, out_specs=out_specs, check_vma=False)
```

profile of v0, /device:TPU:0, one launch (start us, length us, event | category | flops | bytes accessed | tf_op | source)
XLA Modules:
  0.0 199.3 jit_solution(11695038456067852352)
XLA Ops:
  6.5 0.8 convert_reduce_fusion.1
  7.4 1.1 convolution_bitcast_fusion
  8.4 2.6 %all-reduce = (f32[256,8]{0,1:T(8,128)S(1)}, f32[8]{0:T(128)S(1)}) all-reduce(f32[256,8]{0,1:T(8,128)S(1)} %convolution_bitcast_fusion, f32[8]{0:T(128)S(1)} %convert_reduce_fusion.1), channel_id=1, replica_groups=mesh['slab'=2,'samp'=8,'tgt'=2] {'tgt'}, use_global_device_ids=true, to_apply=%region_0.0 | all-reduce | flops 2056 | bytes 16448 | tf_op jit(solution)/shard_map/psum | solution.py:78
  11.1 2.0 fusion.11
  13.2 0.7 convert_element_type.52
  13.8 0.9 convert_reduce_fusion
  14.8 0.7 broadcast_maximum_fusion.4
  15.5 1.0 add_select_fusion.1
  16.5 7.4 %fusion.3 = bf16[256,16,128]{2,1,0:T(8,128)(2,1)S(1)} fusion(s32[256,128]{1,0:T(8,128)S(1)} %get-tuple-element.30, s32[256,128]{1,0:T(8,128)S(1)} %get-tuple-element.29, bf16[256,128]{1,0:T(8,128)(2,1)S(1)} %copy-done.1), kind=kOutput, calls=%fused_computation.10 | convolution fusion | flops 139984896 | bytes 1376256 | tf_op jit(solution)/shard_map/skg,skl->sgl/dot_general | solution.py:67
  24.0 32.2 %all-gather.5.cloned.1.call-done = bf16[2048,256]{1,0:T(8,128)(2,1)} async-done(((bf16[256,256]{1,0:T(8,128)(2,1)}), bf16[2048,256]{1,0:T(8,128)(2,1)}) %all-gather.5.cloned.1.call-update) | async-done | bytes 1048592 | tf_op jit(solution)/shard_map/all_gather | solution.py:84
  56.1 1.8 fusion.19
  58.5 2.5 %psum.30 = f32[256]{0:T(256)S(1)} all-reduce(f32[256]{0:T(256)S(1)} %get-tuple-element.41), channel_id=1, replica_groups=mesh['slab'=2,'samp'=8,'tgt'=2] {'tgt'}, use_global_device_ids=true, to_apply=%region_6.7 | all-reduce | flops 256 | bytes 2048 | tf_op jit(solution)/shard_map/psum | solution.py:29
  61.0 0.9 maximum_maximum_fusion.1
  63.4 0.8 fusion.70
  65.0 1.6 fusion.29
  66.7 36.7 %all-gather.7.cloned.1.call-done = bf16[2048,256]{1,0:T(8,128)(2,1)} async-done(((bf16[256,256]{1,0:T(8,128)(2,1)}), bf16[2048,256]{1,0:T(8,128)(2,1)}) %all-gather.7.cloned.1.call-update) | async-done | bytes 1048592 | tf_op jit(solution)/shard_map/all_gather | solution.py:98
  103.4 1.7 fusion.16
  105.1 39.4 %all-gather.9.cloned.1.call-done = bf16[2048,256]{1,0:T(8,128)(2,1)} async-done(((bf16[256,256]{1,0:T(8,128)(2,1)}), bf16[2048,256]{1,0:T(8,128)(2,1)}) %all-gather.9.cloned.1.call-update) | async-done | bytes 1048592 | tf_op jit(solution)/shard_map/all_gather | solution.py:99
  144.5 1.7 fusion.14
  146.1 39.2 %all-gather.11.cloned.1.call-done = bf16[2048,256]{1,0:T(8,128)(2,1)} async-done(((bf16[256,256]{1,0:T(8,128)(2,1)}), bf16[2048,256]{1,0:T(8,128)(2,1)}) %all-gather.11.cloned.1.call-update) | async-done | bytes 1048592 | tf_op jit(solution)/shard_map/all_gather | solution.py:100
  185.4 1.7 fusion.84
  187.1 2.5 %psum.31 = f32[256]{0:T(256)S(1)} all-reduce(f32[256]{0:T(256)S(1)} %get-tuple-element.43), channel_id=1, replica_groups=mesh['slab'=2,'samp'=8,'tgt'=2] {'tgt'}, use_global_device_ids=true, to_apply=%region_10.11 | all-reduce | flops 256 | bytes 2048 | tf_op jit(solution)/shard_map/psum | solution.py:29
  189.6 0.9 maximum_maximum_fusion
  192.0 0.7 div.169
  (34 shorter events, 4.4 us)
Async XLA Ops:
  6.5 10.0 %copy-start.1 = (bf16[256,128]{1,0:T(8,128)(2,1)S(1)}, bf16[256,128]{1,0:T(8,128)(2,1)}, u32[]{:S(2)}) copy-start(bf16[256,128]{1,0:T(8,128)(2,1)} %param.7) | copy-start | bytes 196612
  6.5 49.6 %all-gather.5.cloned.1.call-start = ((), (), s32[]{:S(2)}) async-start(), calls=%async_computation | async-start | bytes 1179648 | tf_op jit(solution)/shard_map/all_gather | solution.py:84
  13.1 90.3 %all-gather.7.cloned.1.call-start = ((), (), s32[]{:S(2)}) async-start(), calls=%async_computation.1 | async-start | bytes 1179648 | tf_op jit(solution)/shard_map/all_gather | solution.py:98
  56.1 1.8 copy-start.2
  57.9 3.1 %copy-start = (bf16[256,256]{1,0:T(8,128)(2,1)S(1)}, bf16[256,256]{1,0:T(8,128)(2,1)}, u32[]{:S(2)}) copy-start(bf16[256,256]{1,0:T(8,128)(2,1)} %fusion.11) | copy-start | bytes 393220
  64.3 80.2 %all-gather.9.cloned.1.call-start = ((), (), s32[]{:S(2)}) async-start(), calls=%async_computation.2 | async-start | bytes 1179648 | tf_op jit(solution)/shard_map/all_gather | solution.py:99
  65.0 120.4 %all-gather.11.cloned.1.call-start = ((), (), s32[]{:S(2)}) async-start(), calls=%async_computation.3 | async-start | bytes 1179648 | tf_op jit(solution)/shard_map/all_gather | solution.py:100
Sparse Core Ops, SparseCore 0:
  13.2 42.8 all-gather.4
  64.4 38.9 all-gather.6
  105.5 38.8 all-gather.8
  146.4 38.8 all-gather.10
where the time goes:
time: 200 us; the launch traced here: 199 us
  waiting for transfers between devices  148 us (74%)
  matrix products  17.9 us (9%)
  between operations  13.3 us (7%)
  other arithmetic  12.1 us (6%)
  blocking collectives  7.57 us (4%)
    all_gather x1, waiting for transfers between devices, body(): lax.all_gather(gated_cov, 'samp', axis=0, tiled=True)  39.4 us
    all_gather x1, waiting for transfers between devices, body(): lax.all_gather(gated_sq, 'samp', axis=0, tiled=True)  39.2 us
    all_gather x1, waiting for transfers between devices, body(): lax.all_gather(gate, 'samp', axis=0, tiled=True)  36.7 us
    all_gather x1, waiting for transfers between devices, body(): near_cov = lax.all_gather(norm_cov, 'samp', axis=0, tiled=True)  32.2 us
    dot_general x1, matrix products, build_map(): jnp.einsum('skg,skl->sgl', high_one, low_one, preferred_element_type=jnp....  7.45 us
    dot_general x5, matrix products, weighted(): return jnp.dot(weight_map, table, preferred_element_type=jnp.float32)  7.39 us
    psum x2, blocking collectives, copy_calls(): rel_total = lax.psum(jnp.sum(rel_var, axis=1), 'tgt')  4.94 us
  transfers between devices with their start and end apart: 4, of which 4 were waited for; matrix products, arithmetic and copies ran while one was open for 8% of the time, Pallas kernels for 0%

commit v1 on v0

v1 whole, which is shorter than its diff:
```python
import jax
import jax.numpy as jnp
from jax import lax
from jax.sharding import PartitionSpec as P

TGT = 512
NGC = 8
RBLK = 128
EXTRA = 16


LOG_PRIOR = (-4.6051702, -3.2188758, -0.1625189, -2.8134107, -3.5065579, -4.6051702)


def swap_tgt(value):
    return lax.ppermute(value, "tgt", [(0, 1), (1, 0)])


def send(value, step, count):
    return lax.ppermute(value, "samp", [(i, i ^ step) for i in range(count)])


def pick(block, which):
    return lax.dynamic_slice_in_dim(block, which * RBLK, RBLK, axis=0)


def spread_terms(first, second, third):
    ref_mean = second / first
    rel_var = (third / first - ref_mean * ref_mean) / (ref_mean * ref_mean)
    return (ref_mean, rel_var)


def copy_calls(normf, ref_mean, rel_var, plf):
    part = jnp.sum(rel_var, axis=1)
    rel_total = part + swap_tgt(part)
    level = 0.5 * rel_var + 0.5 * (rel_total / TGT)[:, None]
    ratio = normf / ref_mean
    scores = []
    for state in range(6):
        centre = max(state, 0.1) / plf
        vari = level * jnp.maximum(centre, 0.25) + 0.01
        delta = ratio - centre
        scores.append(LOG_PRIOR[state] - 0.5 * delta * delta / vari - 0.5 * jnp.log(vari))
    peak = scores[0]
    for score in scores[1:]:
        peak = jnp.maximum(peak, score)
    expo = [jnp.exp(score - peak) for score in scores]
    top = sum(state * expo[state] for state in range(1, 6))
    return top / sum(expo)


def weighted(weight_map, table):
    return jnp.dot(weight_map, table, preferred_element_type=jnp.float32)


def squared(table):
    tablef = table.astype(jnp.float32)
    return (tablef * tablef).astype(jnp.bfloat16)


def build_map(position, low, nbr_weight, count):
    high_one = jnp.where(
        position[:, :, None] == jnp.arange(count, dtype=jnp.int32)[None, None, :],
        nbr_weight[:, :, None],
        jnp.zeros((), jnp.bfloat16),
    )
    low_one = (low[:, :, None] == jnp.arange(RBLK, dtype=jnp.int32)[None, None, :]).astype(
        jnp.bfloat16
    )
    table = jnp.einsum("skg,skl->sgl", high_one, low_one, preferred_element_type=jnp.float32)
    return table.astype(jnp.bfloat16).reshape(position.shape[0], count * RBLK)


def body(coverage, neighbours, nbr_weight, ploidy, gc_bin):
    count = lax.axis_size("samp")
    half = count // 2
    me = lax.axis_index("samp")
    rows, cols = coverage.shape
    covf = coverage.astype(jnp.float32)
    onehot = gc_bin[:, None] == jnp.arange(NGC, dtype=jnp.int32)[None, :]
    bin_sum = jnp.dot(coverage, onehot.astype(jnp.bfloat16), preferred_element_type=jnp.float32)
    onehot = onehot.astype(jnp.float32)
    stats = jnp.concatenate([bin_sum, jnp.sum(onehot, axis=0)[None, :]], axis=0)
    stats = stats + swap_tgt(stats)
    bin_sum, bin_count = stats[:rows], stats[rows]
    sample_mean = jnp.sum(bin_sum, axis=1) / TGT
    bin_mean = bin_sum / jnp.maximum(bin_count, 1.0)[None, :]
    spread_mean = jnp.dot(bin_mean, onehot.T, precision=lax.Precision.HIGHEST)
    norm_cov = (covf * (sample_mean[:, None] / spread_mean)).astype(jnp.bfloat16)
    normf = norm_cov.astype(jnp.float32)
    plf = ploidy.astype(jnp.float32)[:, None]

    position = (neighbours // rows) ^ me
    block = (neighbours // RBLK) % (rows // RBLK)
    low = neighbours % RBLK
    lanes = jnp.arange(count, dtype=jnp.int32)
    choice = jnp.max(
        jnp.where(position[:, :, None] == lanes[None, None, :], block[:, :, None], 0), axis=(0, 1)
    )
    note = jnp.zeros((EXTRA, cols), jnp.bfloat16).at[:, :count].set(
        jnp.broadcast_to(choice.astype(jnp.bfloat16)[None, :], (EXTRA, count))
    )

    noted = jnp.concatenate([norm_cov, note], axis=0)
    across = send(norm_cov, half, count)
    direct = {k: send(noted, k, count) for k in range(1, half)}
    wants = {
        k: (direct[k][rows, k].astype(jnp.int32), direct[k][rows, k ^ half].astype(jnp.int32))
        for k in direct
    }
    passed = {k: send(pick(across, wants[k][1]), k, count) for k in direct}
    near = [pick(norm_cov, choice[0])]
    near += [pick(direct[k], choice[k]) for k in direct]
    near += [pick(across, choice[half])]
    near += [passed[k] for k in direct]
    near_cov = jnp.concatenate(near, axis=0)
    near_sq = squared(near_cov)

    weight_map = build_map(position, low, nbr_weight, count)
    first = jnp.sum(nbr_weight.astype(jnp.float32), axis=1)[:, None] * jnp.ones_like(normf)
    ref_mean, rel_var = spread_terms(
        first, weighted(weight_map, near_cov), weighted(weight_map, near_sq)
    )
    first_call = copy_calls(normf, ref_mean, rel_var, plf)
    offset = first_call - plf
    gate = (1.0 / (1.0 + 4.0 * offset * offset)).astype(jnp.bfloat16)

    across = send(gate, half, count)
    direct = {k: send(pick(gate, wants[k][0]), k, count) for k in wants}
    passed = {k: send(pick(across, wants[k][1]), k, count) for k in wants}
    far = [pick(gate, choice[0])]
    far += [direct[k] for k in wants]
    far += [pick(across, choice[half])]
    far += [passed[k] for k in wants]
    far_gate = jnp.concatenate(far, axis=0)
    far_f = far_gate.astype(jnp.float32)
    far_cov = (far_f * near_cov.astype(jnp.float32)).astype(jnp.bfloat16)
    far_sq = (far_f * near_sq.astype(jnp.float32)).astype(jnp.bfloat16)
    ref_mean, rel_var = spread_terms(
        weighted(weight_map, far_gate), weighted(weight_map, far_cov), weighted(weight_map, far_sq)
    )
    return copy_calls(normf, ref_mean, rel_var, plf)


def solution(mesh):
    in_specs = (
        P("samp", ("slab", "tgt")),
        P("samp", None),
        P("samp", None),
        P("samp"),
        P(("slab", "tgt")),
    )
    out_specs = P("samp", ("slab", "tgt"))
    return jax.shard_map(body, mesh=mesh, in_specs=in_specs, out_specs=out_specs, check_vma=False)
```

time: 200 us -> 70.6 us (0.35)
  waiting for transfers between devices: 148 us -> 21.4 us
  starting transfers between devices: 0.12 us -> 20.1 us
  blocking collectives: 7.57 us -> 0 us
  matrix products: 17.9 us -> 10.7 us
  between operations: 13.3 us -> 7.35 us
  other arithmetic: 12.1 us -> 7.84 us
  local copies, waits for them, and re-layouts: 0.01 us -> 2.88 us
    all_gather x4 -> x0, waiting for transfers between devices: 148 us -> none  [the longest x1 39.4 us: body(): lax.all_gather(gated_cov, 'samp', axis=0, tiled=True)]
    ppermute x0 -> x17, waiting for transfers between devices: none -> 21.4 us  [the longest x14 20.3 us: send(): return lax.ppermute(value, 'samp', [(i, i ^ step) for i in range(count)])]
    ppermute x0 -> x17, starting transfers between devices: none -> 20.1 us  [the longest x14 19.5 us: send(): return lax.ppermute(value, 'samp', [(i, i ^ step) for i in range(count)])]
    psum x3 -> x0, blocking collectives: 7.57 us -> none  [the longest x2 4.94 us: copy_calls(): rel_total = lax.psum(jnp.sum(rel_var, axis=1), 'tgt')]
    dot_general x5, matrix products: 7.39 us -> 1.82 us  [weighted(): return jnp.dot(weight_map, table, preferred_element_type=jnp.float32)]
    slice x0 -> x4, local copies, waits for them, and re-layouts: none -> 2.59 us  [the longest x3 1.94 us: body(): direct[k][rows, k].astype(jnp.int32)]
  transfers between devices with their start and end apart: 4 -> 17, of which waited for: 4 -> 8; matrix products, arithmetic and copies ran while one was open for 8% -> 19% of each run, Pallas kernels for 0% -> 0%
where the time goes in v1:
time: 70.6 us; the launch traced here: 70.3 us
  waiting for transfers between devices  21.4 us (30%)
  starting transfers between devices  20.1 us (28%)
  matrix products  10.7 us (15%)
  other arithmetic  7.84 us (11%)
  between operations  7.35 us (10%)
  local copies, waits for them, and re-layouts  2.88 us (4%)
    ppermute x14, waiting for transfers between devices, send(): return lax.ppermute(value, 'samp', [(i, i ^ step) for i in range(count)])  20.3 us
    ppermute x14, starting transfers between devices, send(): return lax.ppermute(value, 'samp', [(i, i ^ step) for i in range(count)])  19.5 us
    dot_general x1, matrix products, build_map(): jnp.einsum('skg,skl->sgl', high_one, low_one, preferred_element_type=jnp....  7.37 us
    slice x3, local copies, waits for them, and re-layouts, body(): direct[k][rows, k].astype(jnp.int32)  1.94 us
    div x1, other arithmetic, copy_calls(): return top / sum(expo)  1.88 us
    dot_general x5, matrix products, weighted(): return jnp.dot(weight_map, table, preferred_element_type=jnp.float32)  1.82 us
  transfers between devices with their start and end apart: 17, of which 8 were waited for; matrix products, arithmetic and copies ran while one was open for 19% of the time, Pallas kernels for 0%

profile of v1, /device:TPU:0, one launch (start us, length us, event | category | flops | bytes accessed | tf_op | source)
XLA Modules:
  0.0 70.3 jit_solution(750486232887869271)
XLA Ops:
  0.0 0.8 %convert_reduce_fusion.1 = f32[8]{0:T(128)S(1)} fusion(s32[256]{0:T(256)} %param.11), kind=kLoop, calls=%fused_computation.132 | loop fusion | flops 6136 | bytes 1056 | tf_op jit(solution)/shard_map/reduce_sum | solution.py:83
  0.9 1.1 %convolution_bitcast_fusion = f32[256,8]{0,1:T(8,128)S(1)} fusion(bf16[256,256]{1,0:T(8,128)(2,1)} %param.7, s32[256]{0:T(256)} %param.11), kind=kOutput, calls=%fused_computation.13 | convolution fusion | flops 1050624 | bytes 140288 | tf_op jit(solution)/shard_map/dot_general | solution.py:81
  3.8 1.1 %add_select_fusion.2 = (s32[256,128]{1,0:T(8,128)S(1)}, s32[256,128]{1,0:T(8,128)S(1)}, s32[256,128]{1,0:T(8,128)S(1)}) fusion(s32[256,128]{1,0:T(8,128)} %param.8, s32[]{:T(128)S(6)} %axis_index.15), kind=kLoop, calls=%fused_computation.99 | loop fusion | flops 1343488 | bytes 524292 | tf_op jit(solution)/shard_map/jit(remainder)/select_n | solution.py:95
  5.3 7.4 %fusion.2 = bf16[256,8,128]{2,1,0:T(8,128)(2,1)S(1)} fusion(s32[256,128]{1,0:T(8,128)S(1)} %get-tuple-element.43, s32[256,128]{1,0:T(8,128)S(1)} %get-tuple-element.45, bf16[256,128]{1,0:T(8,128)(2,1)S(1)} %copy-done.1), kind=kOutput, calls=%fused_computation.6 | convolution fusion | flops 72089600 | bytes 851968 | tf_op jit(solution)/shard_map/skg,skl->sgl/dot_general | solution.py:70
  14.0 2.6 %collective-permute-start.1 = (bf16[272,256]{1,0:T(8,128)(2,1)S(1)}, bf16[272,256]{1,0:T(8,128)(2,1)S(1)}, u32[]{:S(2)}, u32[]{:S(2)}) collective-permute-start(bf16[272,256]{1,0:T(8,128)(2,1)S(1)} %pad_maximum_fusion), channel_id=1, source_target_pairs={{0,2},{2,0},{4,6},{6,4},{8,10},{10,8},{12,14},{14,12},{1,3},{3,1},... | collective-permute-start | bytes 417800 | tf_op jit(solution)/shard_map/ppermute | solution.py:20
  20.5 2.7 %collective-permute-start.4 = (bf16[256,256]{1,0:T(8,128)(2,1)S(1)}, bf16[256,256]{1,0:T(8,128)(2,1)S(1)}, u32[]{:S(2)}, u32[]{:S(2)}) collective-permute-start(bf16[256,256]{1,0:T(8,128)(2,1)S(1)} %multiply_convert_fusion), channel_id=1, source_target_pairs={{0,8},{2,10},{4,12},{6,14},{8,0},{10,2},{12,4},{14,6},{1,9},{3,11}... | collective-permute-start | bytes 393224 | tf_op jit(solution)/shard_map/ppermute | solution.py:20
  23.1 1.5 %collective-permute-start.3 = (bf16[272,256]{1,0:T(8,128)(2,1)S(1)}, bf16[272,256]{1,0:T(8,128)(2,1)S(1)}, u32[]{:S(2)}, u32[]{:S(2)}) collective-permute-start(bf16[272,256]{1,0:T(8,128)(2,1)S(1)} %pad_maximum_fusion), channel_id=1, source_target_pairs={{0,6},{2,4},{4,2},{6,0},{8,14},{10,12},{12,10},{14,8},{1,7},{3,5},... | collective-permute-start | bytes 417800 | tf_op jit(solution)/shard_map/ppermute | solution.py:20
  25.8 7.5 %collective-permute-done.2 = bf16[272,256]{1,0:T(8,128)(2,1)S(1)} collective-permute-done((bf16[272,256]{1,0:T(8,128)(2,1)S(1)}, bf16[272,256]{1,0:T(8,128)(2,1)S(1)}, u32[]{:S(2)}, u32[]{:S(2)}) %collective-permute-start.2) | collective-permute-done | bytes 139296 | tf_op jit(solution)/shard_map/ppermute | solution.py:20
  36.6 1.5 %collective-permute-start.5 = (bf16[128,256]{1,0:T(8,128)(2,1)S(1)}, bf16[128,256]{1,0:T(8,128)(2,1)S(1)}, u32[]{:S(2)}, u32[]{:S(2)}) collective-permute-start(bf16[128,256]{1,0:T(8,128)(2,1)S(1)} %get-tuple-element.48), channel_id=1, source_target_pairs={{0,2},{2,0},{4,6},{6,4},{8,10},{10,8},{12,14},{14,12},{1,3},{3,1},... | collective-permute-start | bytes 196616 | tf_op jit(solution)/shard_map/ppermute | solution.py:20
  38.2 1.6 %collective-permute-start.7 = (bf16[128,256]{1,0:T(8,128)(2,1)S(1)}, bf16[128,256]{1,0:T(8,128)(2,1)S(1)}, u32[]{:S(2)}, u32[]{:S(2)}) collective-permute-start(bf16[128,256]{1,0:T(8,128)(2,1)S(1)} %get-tuple-element.46), channel_id=1, source_target_pairs={{0,6},{2,4},{4,2},{6,0},{8,14},{10,12},{12,10},{14,8},{1,7},{3,5},... | collective-permute-start | bytes 196616 | tf_op jit(solution)/shard_map/ppermute | solution.py:20
  40.3 1.3 %collective-permute-done.5 = bf16[128,256]{1,0:T(8,128)(2,1)S(1)} collective-permute-done((bf16[128,256]{1,0:T(8,128)(2,1)S(1)}, bf16[128,256]{1,0:T(8,128)(2,1)S(1)}, u32[]{:S(2)}, u32[]{:S(2)}) %collective-permute-start.5) | collective-permute-done | bytes 65568 | tf_op jit(solution)/shard_map/ppermute | solution.py:20
  41.6 2.4 %collective-permute-done.6 = bf16[128,256]{1,0:T(8,128)(2,1)S(1)} collective-permute-done((bf16[128,256]{1,0:T(8,128)(2,1)S(1)}, bf16[128,256]{1,0:T(8,128)(2,1)S(1)}, u32[]{:S(2)}, u32[]{:S(2)}) %collective-permute-start.6) | collective-permute-done | bytes 65568 | tf_op jit(solution)/shard_map/ppermute | solution.py:20
  46.8 1.4 %fusion.72 = bf16[256,256]{1,0:T(8,128)(2,1)S(1)} fusion(f32[256,256]{1,0:T(8,128)S(1)} %get-tuple-element.66, f32[256,256]{1,0:T(8,128)S(1)} %fusion.20, bf16[256,256]{1,0:T(8,128)(2,1)S(1)} %multiply_convert_fusion, f32[256]{0:T(256)S(1)} %convert_element_type.86, f32[256]{0:T(256)S(1)} %get-tuple-element.58, f32[256]{0:T(256)S(1)} %get-tuple-element.59, ...), kind=kLoop, calls=%fused_computation.93 | loop fusion | flops 5898240 | bytes 801792 | tf_op jit(solution)/shard_map/convert_element_type | solution.py:126
  49.0 2.4 %collective-permute-start.12 = (bf16[256,256]{1,0:T(8,128)(2,1)S(1)}, bf16[256,256]{1,0:T(8,128)(2,1)S(1)}, u32[]{:S(2)}, u32[]{:S(2)}) collective-permute-start(bf16[256,256]{1,0:T(8,128)(2,1)S(1)} %fusion.72), channel_id=1, source_target_pairs={{0,8},{2,10},{4,12},{6,14},{8,0},{10,2},{12,4},{14,6},{1,9},{3,11}... | collective-permute-start | bytes 393224 | tf_op jit(solution)/shard_map/ppermute | solution.py:20
  51.4 0.9 %collective-permute-start.11 = (bf16[128,256]{1,0:T(8,128)(2,1)S(1)}, bf16[128,256]{1,0:T(8,128)(2,1)S(1)}, u32[]{:S(2)}, u32[]{:S(2)}) collective-permute-start(bf16[128,256]{1,0:T(8,128)(2,1)S(1)} %get-tuple-element.39), channel_id=1, source_target_pairs={{0,6},{2,4},{4,2},{6,0},{8,14},{10,12},{12,10},{14,8},{1,7},{3,5},... | collective-permute-start | bytes 196616 | tf_op jit(solution)/shard_map/ppermute | solution.py:20
  52.3 1.1 %collective-permute-start.10 = (bf16[128,256]{1,0:T(8,128)(2,1)S(1)}, bf16[128,256]{1,0:T(8,128)(2,1)S(1)}, u32[]{:S(2)}, u32[]{:S(2)}) collective-permute-start(bf16[128,256]{1,0:T(8,128)(2,1)S(1)} %get-tuple-element.40), channel_id=1, source_target_pairs={{0,4},{2,6},{4,0},{6,2},{8,12},{10,14},{12,8},{14,10},{1,5},{3,7},... | collective-permute-start | bytes 196616 | tf_op jit(solution)/shard_map/ppermute | solution.py:20
  53.4 5.3 %collective-permute-done.10 = bf16[128,256]{1,0:T(8,128)(2,1)S(1)} collective-permute-done((bf16[128,256]{1,0:T(8,128)(2,1)S(1)}, bf16[128,256]{1,0:T(8,128)(2,1)S(1)}, u32[]{:S(2)}, u32[]{:S(2)}) %collective-permute-start.10) | collective-permute-done | bytes 65568 | tf_op jit(solution)/shard_map/ppermute | solution.py:20
  58.6 0.9 %collective-permute-done.11 = bf16[128,256]{1,0:T(8,128)(2,1)S(1)} collective-permute-done((bf16[128,256]{1,0:T(8,128)(2,1)S(1)}, bf16[128,256]{1,0:T(8,128)(2,1)S(1)}, u32[]{:S(2)}, u32[]{:S(2)}) %collective-permute-start.11) | collective-permute-done | bytes 65568 | tf_op jit(solution)/shard_map/ppermute | solution.py:20
  59.5 1.4 %collective-permute-start.13 = (bf16[128,256]{1,0:T(8,128)(2,1)S(1)}, bf16[128,256]{1,0:T(8,128)(2,1)S(1)}, u32[]{:S(2)}, u32[]{:S(2)}) collective-permute-start(bf16[128,256]{1,0:T(8,128)(2,1)S(1)} %get-tuple-element.37), channel_id=1, source_target_pairs={{0,2},{2,0},{4,6},{6,4},{8,10},{10,8},{12,14},{14,12},{1,3},{3,1},... | collective-permute-start | bytes 196616 | tf_op jit(solution)/shard_map/ppermute | solution.py:20
  61.5 1.6 %collective-permute-start.14 = (bf16[128,256]{1,0:T(8,128)(2,1)S(1)}, bf16[128,256]{1,0:T(8,128)(2,1)S(1)}, u32[]{:S(2)}, u32[]{:S(2)}) collective-permute-start(bf16[128,256]{1,0:T(8,128)(2,1)S(1)} %get-tuple-element.36), channel_id=1, source_target_pairs={{0,4},{2,6},{4,0},{6,2},{8,12},{10,14},{12,8},{14,10},{1,5},{3,7},... | collective-permute-start | bytes 196616 | tf_op jit(solution)/shard_map/ppermute | solution.py:20
  63.1 1.2 %collective-permute-done.13 = bf16[128,256]{1,0:T(8,128)(2,1)S(1)} collective-permute-done((bf16[128,256]{1,0:T(8,128)(2,1)S(1)}, bf16[128,256]{1,0:T(8,128)(2,1)S(1)}, u32[]{:S(2)}, u32[]{:S(2)}) %collective-permute-start.13) | collective-permute-done | bytes 65568 | tf_op jit(solution)/shard_map/ppermute | solution.py:20
  64.3 1.7 %collective-permute-done.14 = bf16[128,256]{1,0:T(8,128)(2,1)S(1)} collective-permute-done((bf16[128,256]{1,0:T(8,128)(2,1)S(1)}, bf16[128,256]{1,0:T(8,128)(2,1)S(1)}, u32[]{:S(2)}, u32[]{:S(2)}) %collective-permute-start.14) | collective-permute-done | bytes 65568 | tf_op jit(solution)/shard_map/ppermute | solution.py:20
  67.3 1.1 %collective-permute-done.16 = f32[256]{0:T(256)S(1)} collective-permute-done((f32[256]{0:T(256)S(1)}, f32[256]{0:T(256)S(1)}, u32[]{:S(2)}, u32[]{:S(2)}) %collective-permute-start.16) | collective-permute-done | bytes 1056 | tf_op jit(solution)/shard_map/ppermute | solution.py:16
  68.4 1.9 %add_divide_fusion = f32[256,256]{1,0:T(8,128)} fusion(f32[256,256]{1,0:T(8,128)S(1)} %get-tuple-element.68, f32[256,256]{1,0:T(8,128)S(1)} %fusion.13, f32[256,256]{1,0:T(8,128)S(1)} %fusion.17, bf16[256,256]{1,0:T(8,128)(2,1)S(1)} %multiply_convert_fusion, f32[256]{0:T(256)S(1)} %add_multiply_fusion, f32[256]{0:T(256)S(1)} %get-tuple-element.58, ...), kind=kLoop, calls=%fused_computation.89 | loop fusion | flops 5505024 | bytes 1192960 | tf_op jit(solution)/shard_map/div | solution.py:49
  (67 shorter events, 10.7 us)
Async XLA Ops:
  0.0 5.3 %copy-start.1 = (bf16[256,128]{1,0:T(8,128)(2,1)S(1)}, bf16[256,128]{1,0:T(8,128)(2,1)}, u32[]{:S(2)}) copy-start(bf16[256,128]{1,0:T(8,128)(2,1)} %param.9) | copy-start | bytes 196612
  2.0 11.4 %collective-permute-start = (f32[257,8]{0,1:T(8,128)S(1)}, f32[257,8]{0,1:T(8,128)S(1)}, u32[]{:S(2)}, u32[]{:S(2)}) collective-permute-start(f32[257,8]{0,1:T(8,128)S(1)} %pad_maximum_fusion.1), channel_id=1, source_target_pairs={{0,1},{1,0},{2,3},{3,2},{4,5},{5,4},{6,7},{7,6},{8,9},{9,8},{10,11... | collective-permute-start | bytes 24680 | tf_op jit(solution)/shard_map/ppermute | solution.py:16
  5.3 8.2 %copy-start = (bf16[256,256]{1,0:T(8,128)(2,1)S(1)}, bf16[256,256]{1,0:T(8,128)(2,1)}, u32[]{:S(2)}) copy-start(bf16[256,256]{1,0:T(8,128)(2,1)} %param.7) | copy-start | bytes 393220
  5.3 8.2 %copy-start.3 = (s32[256]{0:T(256)S(1)}, s32[256]{0:T(256)}, u32[]{:S(2)}) copy-start(s32[256]{0:T(256)} %param.11) | copy-start | bytes 3076
  13.6 3.7 %copy-start.2 = (s32[256]{0:T(256)S(1)}, s32[256]{0:T(256)}, u32[]{:S(2)}) copy-start(s32[256]{0:T(256)} %param.10) | copy-start | bytes 3076
  14.0 11.1 %collective-permute-start.1 = (bf16[272,256]{1,0:T(8,128)(2,1)S(1)}, bf16[272,256]{1,0:T(8,128)(2,1)S(1)}, u32[]{:S(2)}, u32[]{:S(2)}) collective-permute-start(bf16[272,256]{1,0:T(8,128)(2,1)S(1)} %pad_maximum_fusion), channel_id=1, source_target_pairs={{0,2},{2,0},{4,6},{6,4},{8,10},{10,8},{12,14},{14,12},{1,3},{3,1},... | collective-permute-start | bytes 417800 | tf_op jit(solution)/shard_map/ppermute | solution.py:20
  20.5 16.1 %collective-permute-start.4 = (bf16[256,256]{1,0:T(8,128)(2,1)S(1)}, bf16[256,256]{1,0:T(8,128)(2,1)S(1)}, u32[]{:S(2)}, u32[]{:S(2)}) collective-permute-start(bf16[256,256]{1,0:T(8,128)(2,1)S(1)} %multiply_convert_fusion), channel_id=1, source_target_pairs={{0,8},{2,10},{4,12},{6,14},{8,0},{10,2},{12,4},{14,6},{1,9},{3,11}... | collective-permute-start | bytes 393224 | tf_op jit(solution)/shard_map/ppermute | solution.py:20
  23.1 10.8 %collective-permute-start.3 = (bf16[272,256]{1,0:T(8,128)(2,1)S(1)}, bf16[272,256]{1,0:T(8,128)(2,1)S(1)}, u32[]{:S(2)}, u32[]{:S(2)}) collective-permute-start(bf16[272,256]{1,0:T(8,128)(2,1)S(1)} %pad_maximum_fusion), channel_id=1, source_target_pairs={{0,6},{2,4},{4,2},{6,0},{8,14},{10,12},{12,10},{14,8},{1,7},{3,5},... | collective-permute-start | bytes 417800 | tf_op jit(solution)/shard_map/ppermute | solution.py:20
  24.6 8.6 %collective-permute-start.2 = (bf16[272,256]{1,0:T(8,128)(2,1)S(1)}, bf16[272,256]{1,0:T(8,128)(2,1)S(1)}, u32[]{:S(2)}, u32[]{:S(2)}) collective-permute-start(bf16[272,256]{1,0:T(8,128)(2,1)S(1)} %pad_maximum_fusion), channel_id=1, source_target_pairs={{0,4},{2,6},{4,0},{6,2},{8,12},{10,14},{12,8},{14,10},{1,5},{3,7},... | collective-permute-start | bytes 417800 | tf_op jit(solution)/shard_map/ppermute | solution.py:20
  36.6 5.0 %collective-permute-start.5 = (bf16[128,256]{1,0:T(8,128)(2,1)S(1)}, bf16[128,256]{1,0:T(8,128)(2,1)S(1)}, u32[]{:S(2)}, u32[]{:S(2)}) collective-permute-start(bf16[128,256]{1,0:T(8,128)(2,1)S(1)} %get-tuple-element.48), channel_id=1, source_target_pairs={{0,2},{2,0},{4,6},{6,4},{8,10},{10,8},{12,14},{14,12},{1,3},{3,1},... | collective-permute-start | bytes 196616 | tf_op jit(solution)/shard_map/ppermute | solution.py:20
  38.2 5.8 %collective-permute-start.7 = (bf16[128,256]{1,0:T(8,128)(2,1)S(1)}, bf16[128,256]{1,0:T(8,128)(2,1)S(1)}, u32[]{:S(2)}, u32[]{:S(2)}) collective-permute-start(bf16[128,256]{1,0:T(8,128)(2,1)S(1)} %get-tuple-element.46), channel_id=1, source_target_pairs={{0,6},{2,4},{4,2},{6,0},{8,14},{10,12},{12,10},{14,8},{1,7},{3,5},... | collective-permute-start | bytes 196616 | tf_op jit(solution)/shard_map/ppermute | solution.py:20
  39.8 4.3 %collective-permute-start.6 = (bf16[128,256]{1,0:T(8,128)(2,1)S(1)}, bf16[128,256]{1,0:T(8,128)(2,1)S(1)}, u32[]{:S(2)}, u32[]{:S(2)}) collective-permute-start(bf16[128,256]{1,0:T(8,128)(2,1)S(1)} %get-tuple-element.47), channel_id=1, source_target_pairs={{0,4},{2,6},{4,0},{6,2},{8,12},{10,14},{12,8},{14,10},{1,5},{3,7},... | collective-permute-start | bytes 196616 | tf_op jit(solution)/shard_map/ppermute | solution.py:20
  44.8 2.1 %collective-permute-start.8 = (f32[256]{0:T(256)S(1)}, f32[256]{0:T(256)S(1)}, u32[]{:S(2)}, u32[]{:S(2)}) collective-permute-start(f32[256]{0:T(256)S(1)} %get-tuple-element.65), channel_id=1, source_target_pairs={{0,1},{1,0},{2,3},{3,2},{4,5},{5,4},{6,7},{7,6},{8,9},{9,8},{10,11... | collective-permute-start | bytes 3080 | tf_op jit(solution)/shard_map/ppermute | solution.py:16
  48.3 5.1 %collective-permute-start.9 = (bf16[128,256]{1,0:T(8,128)(2,1)S(1)}, bf16[128,256]{1,0:T(8,128)(2,1)S(1)}, u32[]{:S(2)}, u32[]{:S(2)}) collective-permute-start(bf16[128,256]{1,0:T(8,128)(2,1)S(1)} %get-tuple-element.41), channel_id=1, source_target_pairs={{0,2},{2,0},{4,6},{6,4},{8,10},{10,8},{12,14},{14,12},{1,3},{3,1},... | collective-permute-start | bytes 196616 | tf_op jit(solution)/shard_map/ppermute | solution.py:20
  49.0 10.5 %collective-permute-start.12 = (bf16[256,256]{1,0:T(8,128)(2,1)S(1)}, bf16[256,256]{1,0:T(8,128)(2,1)S(1)}, u32[]{:S(2)}, u32[]{:S(2)}) collective-permute-start(bf16[256,256]{1,0:T(8,128)(2,1)S(1)} %fusion.72), channel_id=1, source_target_pairs={{0,8},{2,10},{4,12},{6,14},{8,0},{10,2},{12,4},{14,6},{1,9},{3,11}... | collective-permute-start | bytes 393224 | tf_op jit(solution)/shard_map/ppermute | solution.py:20
  51.4 8.1 %collective-permute-start.11 = (bf16[128,256]{1,0:T(8,128)(2,1)S(1)}, bf16[128,256]{1,0:T(8,128)(2,1)S(1)}, u32[]{:S(2)}, u32[]{:S(2)}) collective-permute-start(bf16[128,256]{1,0:T(8,128)(2,1)S(1)} %get-tuple-element.39), channel_id=1, source_target_pairs={{0,6},{2,4},{4,2},{6,0},{8,14},{10,12},{12,10},{14,8},{1,7},{3,5},... | collective-permute-start | bytes 196616 | tf_op jit(solution)/shard_map/ppermute | solution.py:20
  52.3 6.4 %collective-permute-start.10 = (bf16[128,256]{1,0:T(8,128)(2,1)S(1)}, bf16[128,256]{1,0:T(8,128)(2,1)S(1)}, u32[]{:S(2)}, u32[]{:S(2)}) collective-permute-start(bf16[128,256]{1,0:T(8,128)(2,1)S(1)} %get-tuple-element.40), channel_id=1, source_target_pairs={{0,4},{2,6},{4,0},{6,2},{8,12},{10,14},{12,8},{14,10},{1,5},{3,7},... | collective-permute-start | bytes 196616 | tf_op jit(solution)/shard_map/ppermute | solution.py:20
  59.5 4.8 %collective-permute-start.13 = (bf16[128,256]{1,0:T(8,128)(2,1)S(1)}, bf16[128,256]{1,0:T(8,128)(2,1)S(1)}, u32[]{:S(2)}, u32[]{:S(2)}) collective-permute-start(bf16[128,256]{1,0:T(8,128)(2,1)S(1)} %get-tuple-element.37), channel_id=1, source_target_pairs={{0,2},{2,0},{4,6},{6,4},{8,10},{10,8},{12,14},{14,12},{1,3},{3,1},... | collective-permute-start | bytes 196616 | tf_op jit(solution)/shard_map/ppermute | solution.py:20
  60.9 5.2 %collective-permute-start.15 = (bf16[128,256]{1,0:T(8,128)(2,1)S(1)}, bf16[128,256]{1,0:T(8,128)(2,1)S(1)}, u32[]{:S(2)}, u32[]{:S(2)}) collective-permute-start(bf16[128,256]{1,0:T(8,128)(2,1)S(1)} %get-tuple-element.35), channel_id=1, source_target_pairs={{0,6},{2,4},{4,2},{6,0},{8,14},{10,12},{12,10},{14,8},{1,7},{3,5},... | collective-permute-start | bytes 196616 | tf_op jit(solution)/shard_map/ppermute | solution.py:20
  61.5 4.6 %collective-permute-start.14 = (bf16[128,256]{1,0:T(8,128)(2,1)S(1)}, bf16[128,256]{1,0:T(8,128)(2,1)S(1)}, u32[]{:S(2)}, u32[]{:S(2)}) collective-permute-start(bf16[128,256]{1,0:T(8,128)(2,1)S(1)} %get-tuple-element.36), channel_id=1, source_target_pairs={{0,4},{2,6},{4,0},{6,2},{8,12},{10,14},{12,8},{14,10},{1,5},{3,7},... | collective-permute-start | bytes 196616 | tf_op jit(solution)/shard_map/ppermute | solution.py:20
  67.2 1.2 %collective-permute-start.16 = (f32[256]{0:T(256)S(1)}, f32[256]{0:T(256)S(1)}, u32[]{:S(2)}, u32[]{:S(2)}) collective-permute-start(f32[256]{0:T(256)S(1)} %get-tuple-element.67), channel_id=1, source_target_pairs={{0,1},{1,0},{2,3},{3,2},{4,5},{5,4},{6,7},{7,6},{8,9},{9,8},{10,11... | collective-permute-start | bytes 3080 | tf_op jit(solution)/shard_map/ppermute | solution.py:16

commit v2 on v0

v2 whole, which is shorter than its diff:
```python
import functools

import jax
import jax.numpy as jnp
from jax import lax
from jax.experimental import pallas as pl
from jax.experimental.pallas import tpu as pltpu
from jax.sharding import PartitionSpec as P

NGC = 8
RBLK = 128
LANE = 128
CHUNK = 32
GROUP = 8

LOG_PRIOR = (-4.6051702, -3.2188758, -0.1625189, -2.8134107, -3.5065579, -4.6051702)

F32 = jnp.float32
BF16 = jnp.bfloat16
EXACT = lax.Precision.HIGHEST


def swap_tgt(value):
    return lax.ppermute(value, "tgt", [(0, 1), (1, 0)])


def send(value, step, count):
    return lax.ppermute(value, "samp", [(i, i ^ step) for i in range(count)])


def call(body, name, outs, *args, scratch=()):
    return pl.pallas_call(
        body,
        out_shape=[jax.ShapeDtypeStruct(shape, dtype) for shape, dtype in outs],
        in_specs=[pl.BlockSpec(memory_space=pltpu.VMEM)] * len(args),
        out_specs=[pl.BlockSpec(memory_space=pltpu.VMEM)] * len(outs),
        scratch_shapes=list(scratch),
        compiler_params=pltpu.CompilerParams(vmem_limit_bytes=16 * 2**20),
        name=name,
    )(*args)


def dot(left, right, left_dim, right_dim, precision=None):
    return lax.dot_general(
        left,
        right,
        (((left_dim,), (right_dim,)), ((), ())),
        precision=precision,
        preferred_element_type=F32,
    )


def pick(ref, ask, parts):
    chosen = ref[0:RBLK]
    for part in range(1, parts):
        chosen = jnp.where(ask == part, ref[part * RBLK : (part + 1) * RBLK], chosen)
    return chosen


def ask_kernel(neighbours, coverage, noted, ask):
    rows, cols = coverage.shape
    index = neighbours[...]
    position = lax.div(index, rows) ^ lax.axis_index("samp")
    block = lax.div(lax.rem(index, rows), RBLK)
    count = lax.axis_size("samp")
    best = [
        jnp.max(jnp.where(position == p, block, 0), axis=0, keepdims=True) for p in range(count)
    ]
    best += [jnp.zeros_like(best[0])] * (ask.shape[0] - count)
    best = jnp.max(jnp.concatenate(best, axis=0), axis=1, keepdims=True)
    wide = jnp.broadcast_to(best.astype(F32), ask.shape).astype(BF16)
    ask[...] = wide
    noted[0:rows] = coverage[...]
    noted[rows:] = wide


def map_kernel(neighbours, weight, ask, out, total, wide):
    rows = neighbours.shape[0]
    listed = neighbours.shape[1]
    count = lax.axis_size("samp")
    me = lax.axis_index("samp")
    sample = lax.broadcasted_iota(jnp.int32, (RBLK, listed), 0).astype(F32).astype(BF16)
    device = lax.broadcasted_iota(jnp.int32, (count, listed), 0)
    one, zero = jnp.ones((), BF16), jnp.zeros((), BF16)

    def step(i, carry):
        start = pl.multiple_of(i * GROUP, GROUP)
        index = neighbours[pl.ds(start, GROUP), :]
        heavy = weight[pl.ds(start, GROUP), :].astype(F32)
        position = lax.div(index, rows) ^ me
        low = lax.rem(index, RBLK).astype(F32).astype(BF16)
        for r in range(0, GROUP, 2):
            low_one = jnp.concatenate(
                [jnp.where(sample == low[q : q + 1], one, zero) for q in (r, r + 1)], axis=1
            )
            high = [
                jnp.where(device == position[q : q + 1], heavy[q : q + 1], 0.0) for q in (r, r + 1)
            ]
            none = jnp.zeros_like(high[0])
            high_one = jnp.concatenate(
                [jnp.concatenate([high[0], none], axis=1), jnp.concatenate([none, high[1]], axis=1)],
                axis=0,
            ).astype(BF16)
            both = dot(high_one, low_one, 1, 1)
            wide[:, pl.ds(start + r, 1), :] = both[:count].reshape(count, 1, RBLK)
            wide[:, pl.ds(start + r + 1, 1), :] = both[count:].reshape(count, 1, RBLK)
        return carry

    lax.fori_loop(0, rows // GROUP, step, 0, unroll=8)
    for p in range(count):
        out[:, p * RBLK : (p + 1) * RBLK] = wide[p].astype(BF16)
    summed = jnp.sum(weight[...].astype(F32), axis=1, keepdims=True)
    total[...] = jnp.broadcast_to(summed, total.shape)


def bin_rows(gc):
    return (lax.broadcasted_iota(jnp.int32, (NGC, gc.shape[1]), 0) == gc[...]).astype(F32)


def bin_sums(onehot, block):
    return dot(onehot.astype(BF16), block, 1, 1)


def factors(sums, number, targets):
    mean = jnp.sum(sums, axis=0, keepdims=True) / targets
    scale = mean / (sums / jnp.maximum(number, 1.0))
    return jnp.where(sums > 0, scale, 0.0)


def normal(block, scale, onehot):
    return (block.astype(F32) * dot(scale, onehot, 0, 0, EXACT)).astype(BF16)


def stats_kernel(coverage, across, gc, stats):
    rows = coverage.shape[0]
    onehot = bin_rows(gc)
    stats[:, 0:rows] = bin_sums(onehot, coverage[...])
    stats[:, rows : 2 * rows] = bin_sums(onehot, across[0:rows])
    number = jnp.sum(onehot, axis=1, keepdims=True)
    stats[:, 2 * rows :] = jnp.broadcast_to(number, (NGC, LANE))


def norm_kernel(half, coverage, across, mine, theirs, gc, ask, *refs):
    noted, refs = refs[: half - 1], refs[half - 1 :]
    own, near, far, raw, sums = refs[:5]
    passed = refs[5:]
    rows, cols = coverage.shape
    parts = rows // RBLK
    targets = cols * lax.axis_size("tgt")
    onehot = bin_rows(gc)
    number = mine[:, 2 * rows : 2 * rows + 1] + theirs[:, 2 * rows : 2 * rows + 1]
    scale = factors(mine[:, 0 : 2 * rows] + theirs[:, 0 : 2 * rows], number, targets)
    own[...] = normal(coverage[...], scale[:, 0:rows], onehot)
    far[...] = normal(across[0:rows], scale[:, rows : 2 * rows], onehot)
    near[0:RBLK] = pick(own, ask[0:1], parts)
    near[RBLK : 2 * RBLK] = pick(far, ask[half : half + 1], parts)
    for k in range(1, half):
        note = noted[k - 1]
        other = k ^ half
        passed[k - 1][0:RBLK] = pick(far, note[rows + other : rows + other + 1], parts)
        passed[k - 1][RBLK:] = across[rows:]
        place = pl.ds((k - 1) * RBLK, RBLK)
        raw[place, :] = pick(note, ask[k : k + 1], parts)
        sums[:, (k - 1) * RBLK : k * RBLK] = bin_sums(onehot, raw[place, :])


def spread(first, second, third, normf, ratio, rel, part):
    mean = second / first
    inverse = 1.0 / mean
    ratio[...] = normf * inverse
    relative = (third / first) * (inverse * inverse) - 1.0
    rel[...] = relative
    part[...] = dot(jnp.ones((NGC, relative.shape[1]), F32), relative, 1, 1, EXACT)


def squared(block):
    wide = block.astype(F32)
    return (wide * wide).astype(BF16)


def first_kernel(half, weight, total, own, near, raw, sums, sums_two, mine, theirs, gc, *refs):
    passed, refs = refs[: half - 1], refs[half - 1 :]
    table, ratio, rel, part = refs
    rows, cols = own.shape
    onehot = bin_rows(gc)
    number = mine[:, 2 * rows : 2 * rows + 1] + theirs[:, 2 * rows : 2 * rows + 1]
    scale = factors(sums[...] + sums_two[...], number, cols * lax.axis_size("tgt"))
    table[0:RBLK] = near[0:RBLK]
    table[half * RBLK : (half + 1) * RBLK] = near[RBLK : 2 * RBLK]
    table[RBLK : half * RBLK] = normal(raw[...], scale, onehot)
    for k in range(1, half):
        other = k ^ half
        table[other * RBLK : (other + 1) * RBLK] = passed[k - 1][0:RBLK]
    second = dot(weight[...], table[...], 1, 0)
    third = dot(weight[...], squared(table[...]), 1, 0)
    first = jnp.concatenate([total[...]] * (cols // LANE), axis=1)
    spread(first, second, third, own[...].astype(F32), ratio, rel, part)


def second_kernel(count, weight, table, own, gate, ask, *refs):
    arrived, refs = refs[: count - 1], refs[count - 1 :]
    ratio, rel, part = refs
    rows, cols = own.shape
    gates = [pick(gate, ask[0:1], rows // RBLK)] + [ref[...] for ref in arrived]
    gates = jnp.concatenate(gates, axis=0)
    wide = gates.astype(F32)
    covs = (wide * table[...].astype(F32)).astype(BF16)
    squares = (wide * squared(table[...]).astype(F32)).astype(BF16)
    first = dot(weight[...], gates, 1, 0)
    second = dot(weight[...], covs, 1, 0)
    third = dot(weight[...], squares, 1, 0)
    spread(first, second, third, own[...].astype(F32), ratio, rel, part)


def called(ratio, rel, part, part_two, plf, finish):
    rows, cols = ratio.shape
    targets = cols * lax.axis_size("tgt")
    at_top = (lax.broadcasted_iota(jnp.int32, (NGC, LANE), 0) == 0).astype(F32)
    level_part = dot((part[...] + part_two[...]) * (0.5 / targets), at_top, 0, 0, EXACT)
    for start in range(0, rows, CHUNK):
        here = slice(start, start + CHUNK)
        shared = level_part[here]
        ploidy = plf[here]
        for lane in range(0, cols, LANE):
            there = slice(lane, lane + LANE)
            level = 0.5 * rel[here, there] + shared
            copies = ratio[here, there]
            scores, roots = [], []
            for state, prior in enumerate(LOG_PRIOR):
                centre = max(state, 0.1) / ploidy
                root = lax.rsqrt(level * jnp.maximum(centre, 0.25) + 0.01)
                delta = (copies - centre) * root
                scores.append(prior - 0.5 * (delta * delta))
                roots.append(root)
            peak = functools.reduce(jnp.maximum, scores)
            expo = [jnp.exp(s - peak) * root for s, root in zip(scores, roots)]
            top = expo[1]
            for state in range(2, 6):
                top = top + float(state) * expo[state]
            finish(here, there, top / functools.reduce(jnp.add, expo), ploidy)


def gate_kernel(half, parts, ratio, rel, part, part_two, plf, across, *refs):
    count = 2 * half
    rows = ratio.shape[0]
    noted, passed, refs = refs[: half - 1], refs[half - 1 : 2 * half - 2], refs[2 * half - 2 :]
    gate, out = refs[0], refs[1:]

    def finish(here, there, value, ploidy):
        offset = value - ploidy
        gate[here, there] = (1.0 / (1.0 + 4.0 * (offset * offset))).astype(BF16)

    called(ratio, rel, part, part_two, plf, finish)
    for p in range(1, count):
        if p < half:
            ask = noted[p - 1][rows + p : rows + p + 1]
        elif p == half:
            ask = across[rows + p : rows + p + 1]
        else:
            ask = passed[(p ^ half) - 1][RBLK + p : RBLK + p + 1]
        out[p - 1][...] = pick(gate, ask, parts)


def final_kernel(ratio, rel, part, part_two, plf, out):
    def finish(here, there, value, ploidy):
        out[here, there] = value

    called(ratio, rel, part, part_two, plf, finish)


def body(coverage, neighbours, nbr_weight, ploidy, gc_bin):
    count = lax.axis_size("samp")
    half = count // 2
    mates = range(1, half)
    rows, cols = coverage.shape
    listed = neighbours.shape[1]
    parts = rows // RBLK
    extra = -(-count // 16) * 16
    gc = gc_bin.reshape(1, cols)
    plf = jnp.broadcast_to(ploidy.astype(F32)[:, None], (rows, LANE))

    noted, ask = call(
        ask_kernel, "choices", [((rows + extra, cols), BF16), ((extra, cols), BF16)],
        neighbours, coverage,
    )
    across = send(noted, half, count)
    noted = [send(noted, k, count) for k in mates]
    weight, total = call(
        map_kernel, "weight_map", [((rows, count * RBLK), BF16), ((rows, LANE), F32)],
        neighbours, nbr_weight, ask, scratch=[pltpu.VMEM((count, rows, RBLK), F32)],
    )
    (mine,) = call(
        stats_kernel, "bin_sums", [((NGC, 2 * rows + LANE), F32)], coverage, across, gc
    )
    theirs = swap_tgt(mine)
    own, near, _, raw, sums, *passed = call(
        functools.partial(norm_kernel, half), "normalise",
        [
            ((rows, cols), BF16),
            ((2 * RBLK, cols), BF16),
            ((rows, cols), BF16),
            ((len(mates) * RBLK, cols), BF16),
            ((NGC, len(mates) * RBLK), F32),
        ] + [((RBLK + extra, cols), BF16)] * len(mates),
        coverage, across, mine, theirs, gc, ask, *noted,
    )
    passed = [send(block, k, count) for k, block in zip(mates, passed)]
    sums_two = swap_tgt(sums)
    table, ratio, rel, part = call(
        functools.partial(first_kernel, half), "moments_one",
        [
            ((count * RBLK, cols), BF16),
            ((rows, cols), F32),
            ((rows, cols), F32),
            ((NGC, rows), F32),
        ],
        weight, total, own, near, raw, sums, sums_two, mine, theirs, gc, *passed,
    )
    gate, *gates = call(
        functools.partial(gate_kernel, half, parts), "gate",
        [((rows, cols), BF16)] + [((RBLK, cols), BF16)] * (count - 1),
        ratio, rel, part, swap_tgt(part), plf, across, *noted, *passed,
    )
    gates = [send(block, p, count) for p, block in enumerate(gates, 1)]
    ratio, rel, part = call(
        functools.partial(second_kernel, count), "moments_two",
        [((rows, cols), F32), ((rows, cols), F32), ((NGC, rows), F32)],
        weight, table, own, gate, ask, *gates,
    )
    (out,) = call(
        final_kernel, "copy_number", [((rows, cols), F32)], ratio, rel, part, swap_tgt(part), plf
    )
    return out


def solution(mesh):
    in_specs = (
        P("samp", ("slab", "tgt")),
        P("samp", None),
        P("samp", None),
        P("samp"),
        P(("slab", "tgt")),
    )
    out_specs = P("samp", ("slab", "tgt"))
    return jax.shard_map(body, mesh=mesh, in_specs=in_specs, out_specs=out_specs, check_vma=False)
```

time: 200 us -> 50.5 us (0.25)
  waiting for transfers between devices: 148 us -> 14.6 us
  starting transfers between devices: 0.12 us -> 22.2 us
  matrix products: 17.9 us -> 0 us
  between operations: 13.3 us -> 0.09 us
  other arithmetic: 12.1 us -> 0.01 us
  Pallas kernels: 0 us -> 10.7 us
  blocking collectives: 7.57 us -> 0 us
  local copies, waits for them, and re-layouts: 0.01 us -> 2.63 us
    all_gather x4 -> x0, waiting for transfers between devices: 148 us -> none  [the longest x1 39.4 us: body(): lax.all_gather(gated_cov, 'samp', axis=0, tiled=True)]
    ppermute x0 -> x18, starting transfers between devices: none -> 22.2 us  [the longest x14 22.2 us: send(): return lax.ppermute(value, 'samp', [(i, i ^ step) for i in range(count)])]
    dot_general x8 -> x0, matrix products: 17.9 us -> none  [the longest x1 7.45 us: build_map(): jnp.einsum('skg,skl->sgl', high_one, low_one, preferred_element_type=jnp....]
    ppermute x0 -> x18, waiting for transfers between devices: none -> 14.6 us  [the longest x14 12.9 us: send(): return lax.ppermute(value, 'samp', [(i, i ^ step) for i in range(count)])]
    pallas_call x0 -> x8, Pallas kernels: none -> 10.7 us  [call(): pl.pallas_call(body, out_shape=[jax.ShapeDtypeStruct(shape, dtype) for sh...]
    psum x3 -> x0, blocking collectives: 7.57 us -> none  [the longest x2 4.94 us: copy_calls(): rel_total = lax.psum(jnp.sum(rel_var, axis=1), 'tgt')]
    convert_element_type x3 -> x1, other arithmetic: 3.12 us -> 0.01 us  [body(): plf = jnp.broadcast_to(ploidy.astype(F32)[:, None], (rows, LANE))]
    unnamed x6 -> x14, local copies, waits for them, and re-layouts: 0.01 us -> 2.54 us
  transfers between devices with their start and end apart: 4 -> 18, of which waited for: 4 -> 8; matrix products, arithmetic and copies ran while one was open for 8% -> 0% of each run, Pallas kernels for 0% -> 6%
where the time goes in v2:
time: 50.5 us; the launch traced here: 50.2 us
  starting transfers between devices  22.2 us (44%)
  waiting for transfers between devices  14.6 us (29%)
  Pallas kernels  10.7 us (21%)
  local copies, waits for them, and re-layouts  2.63 us (5%)
    ppermute x14, starting transfers between devices, send(): return lax.ppermute(value, 'samp', [(i, i ^ step) for i in range(count)])  22.2 us
    ppermute x14, waiting for transfers between devices, send(): return lax.ppermute(value, 'samp', [(i, i ^ step) for i in range(count)])  12.9 us
    pallas_call x8, Pallas kernels, call(): pl.pallas_call(body, out_shape=[jax.ShapeDtypeStruct(shape, dtype) for sh...  10.7 us
    unnamed x14, local copies, waits for them, and re-layouts  2.54 us
    ppermute x4, waiting for transfers between devices, swap_tgt(): return lax.ppermute(value, 'tgt', [(0, 1), (1, 0)])  1.7 us
  transfers between devices with their start and end apart: 18, of which 8 were waited for; matrix products, arithmetic and copies ran while one was open for 0% of the time, Pallas kernels for 6%

profile of v2, /device:TPU:0, one launch (start us, length us, event | category | flops | bytes accessed | tf_op | source)
XLA Modules:
  0.0 50.2 jit_solution(17066361426549980505)
XLA Ops:
  0.0 0.9 %copy-done = bf16[256,256]{1,0:T(8,128)(2,1)S(1)} copy-done((bf16[256,256]{1,0:T(8,128)(2,1)S(1)}, bf16[256,256]{1,0:T(8,128)(2,1)}, u32[]{:S(2)}) %copy-start) | copy-done | bytes 131096
  0.9 0.9 %copy-done.2 = s32[256,128]{1,0:T(8,128)S(1)} copy-done((s32[256,128]{1,0:T(8,128)S(1)}, s32[256,128]{1,0:T(8,128)}, u32[]{:S(2)}) %copy-start.2) | copy-done | bytes 131096
  2.2 4.1 %collective-permute-start = (bf16[272,256]{1,0:T(8,128)(2,1)S(1)}, bf16[272,256]{1,0:T(8,128)(2,1)S(1)}, u32[]{:S(2)}, u32[]{:S(2)}) collective-permute-start(bf16[272,256]{1,0:T(8,128)(2,1)S(1)} %get-tuple-element.34), channel_id=1, source_target_pairs={{0,8},{2,10},{4,12},{6,14},{8,0},{10,2},{12,4},{14,6},{1,9},{3,11}... | collective-permute-start | bytes 417800 | tf_op jit(solution)/shard_map/ppermute | solution.py:28
  6.3 2.5 %collective-permute-start.4 = (bf16[272,256]{1,0:T(8,128)(2,1)S(1)}, bf16[272,256]{1,0:T(8,128)(2,1)S(1)}, u32[]{:S(2)}, u32[]{:S(2)}) collective-permute-start(bf16[272,256]{1,0:T(8,128)(2,1)S(1)} %get-tuple-element.34), channel_id=1, source_target_pairs={{0,6},{2,4},{4,2},{6,0},{8,14},{10,12},{12,10},{14,8},{1,7},{3,5},... | collective-permute-start | bytes 417800 | tf_op jit(solution)/shard_map/ppermute | solution.py:28
  9.7 3.3 %collective-permute-done.across = bf16[272,256]{1,0:T(8,128)(2,1)S(1)} collective-permute-done((bf16[272,256]{1,0:T(8,128)(2,1)S(1)}, bf16[272,256]{1,0:T(8,128)(2,1)S(1)}, u32[]{:S(2)}, u32[]{:S(2)}) %collective-permute-start) | collective-permute-done | bytes 139296 | tf_op jit(solution)/shard_map/ppermute | solution.py:28
  13.2 2.4 %collective-permute-done.4.refs_2_ = bf16[272,256]{1,0:T(8,128)(2,1)S(1)} collective-permute-done((bf16[272,256]{1,0:T(8,128)(2,1)S(1)}, bf16[272,256]{1,0:T(8,128)(2,1)S(1)}, u32[]{:S(2)}, u32[]{:S(2)}) %collective-permute-start.4) | collective-permute-done | bytes 139296 | tf_op jit(solution)/shard_map/ppermute | solution.py:28
  15.6 1.5 %collective-permute-done.3.refs_1_ = bf16[272,256]{1,0:T(8,128)(2,1)S(1)} collective-permute-done((bf16[272,256]{1,0:T(8,128)(2,1)S(1)}, bf16[272,256]{1,0:T(8,128)(2,1)S(1)}, u32[]{:S(2)}, u32[]{:S(2)}) %collective-permute-start.3) | collective-permute-done | bytes 139296 | tf_op jit(solution)/shard_map/ppermute | solution.py:28
  17.2 1.4 %normalise.1 = (bf16[256,256]{1,0:T(8,128)(2,1)S(1)}, bf16[256,256]{1,0:T(8,128)(2,1)S(1)}, bf16[256,256]{1,0:T(8,128)(2,1)}, bf16[384,256]{1,0:T(8,128)(2,1)S(1...) custom-call(bf16[256,256]{1,0:T(8,128)(2,1)S(1)} %copy-done.1, ...), custom_call_target="tpu_custom_call" | custom-call | tf_op jit(solution)/shard_map/normalise/pallas_call | solution.py:32
  19.1 1.5 %collective-permute-start.7 = (bf16[144,256]{1,0:T(8,128)(2,1)S(1)}, bf16[144,256]{1,0:T(8,128)(2,1)S(1)}, u32[]{:S(2)}, u32[]{:S(2)}) collective-permute-start(bf16[144,256]{1,0:T(8,128)(2,1)S(1)} %get-tuple-element.40), channel_id=1, source_target_pairs={{0,4},{2,6},{4,0},{6,2},{8,12},{10,14},{12,8},{14,10},{1,5},{3,7},... | collective-permute-start | bytes 221192 | tf_op jit(solution)/shard_map/ppermute | solution.py:28
  20.6 1.5 %collective-permute-start.8 = (bf16[144,256]{1,0:T(8,128)(2,1)S(1)}, bf16[144,256]{1,0:T(8,128)(2,1)S(1)}, u32[]{:S(2)}, u32[]{:S(2)}) collective-permute-start(bf16[144,256]{1,0:T(8,128)(2,1)S(1)} %get-tuple-element.41), channel_id=1, source_target_pairs={{0,6},{2,4},{4,2},{6,0},{8,14},{10,12},{12,10},{14,8},{1,7},{3,5},... | collective-permute-start | bytes 221192 | tf_op jit(solution)/shard_map/ppermute | solution.py:28
  22.1 2.9 %weight_map.1 = (bf16[256,1024]{1,0:T(8,128)(2,1)S(1)}, f32[256,128]{1,0:T(8,128)S(1)}) custom-call(s32[256,128]{1,0:T(8,128)S(1)} %copy-done.3, bf16[256,128]{1,0:T(8,128)(2,1)S(1)} %copy-done.4, bf16[16,256]{1,0:T(8,128)(2,1)S(1)} %get-tuple-element.31.ask), custom_call_target="tpu_custom_call" | custom-call | tf_op jit(solution)/shard_map/weight_map/pallas_call | solution.py:32
  25.0 0.8 %collective-permute-done.8.refs_2_.refs_5_ = bf16[144,256]{1,0:T(8,128)(2,1)S(1)} collective-permute-done((bf16[144,256]{1,0:T(8,128)(2,1)S(1)}, bf16[144,256]{1,0:T(8,128)(2,1)S(1)}, u32[]{:S(2)}, u32[]{:S(2)}) %collective-permute-start.8) | collective-permute-done | bytes 73760 | tf_op jit(solution)/shard_map/ppermute | solution.py:28
  25.9 1.6 %moments_one.1 = (bf16[1024,256]{1,0:T(8,128)(2,1)S(1)}, f32[256,256]{1,0:T(8,128)S(1)}, f32[256,256]{1,0:T(8,128)S(1)}, f32[8,256]{1,0:T(8,128)S(1)}) custom-call(bf16[256,1024]{1,0:T(8,128)(2,1)S(1)} %get-tuple-element.32.weight, f32[256,128]{1,0:T(8,128)S(1)} %get-tuple-element.33.total, bf16[256,256]{1,0:T(8,128)(2,1)S(1)} %get-tuple-element.35.own, ...), custom_call_target="tpu_custom_call" | custom-call | tf_op jit(solution)/shard_map/moments_one/pallas_call | solution.py:32
  28.7 1.3 %gate.1 = (bf16[256,256]{1,0:T(8,128)(2,1)S(1)}, bf16[128,256]{1,0:T(8,128)(2,1)S(1)}, bf16[128,256]{1,0:T(8,128)(2,1)S(1)}, bf16[128,256]{1,0:T(8,128)(2,1)S(1)...) custom-call(f32[256,256]{1,0:T(8,128)S(1)} %get-tuple-element.43.rat, ...), custom_call_target="tpu_custom_call" | custom-call | tf_op jit(solution)/shard_map/gate/pallas_call | solution.py:32
  30.8 1.3 %collective-permute-start.11 = (bf16[128,256]{1,0:T(8,128)(2,1)S(1)}, bf16[128,256]{1,0:T(8,128)(2,1)S(1)}, u32[]{:S(2)}, u32[]{:S(2)}) collective-permute-start(bf16[128,256]{1,0:T(8,128)(2,1)S(1)} %get-tuple-element.48), channel_id=1, source_target_pairs={{0,4},{2,6},{4,0},{6,2},{8,12},{10,14},{12,8},{14,10},{1,5},{3,7},... | collective-permute-start | bytes 196616 | tf_op jit(solution)/shard_map/ppermute | solution.py:28
  32.1 1.5 %collective-permute-start.12 = (bf16[128,256]{1,0:T(8,128)(2,1)S(1)}, bf16[128,256]{1,0:T(8,128)(2,1)S(1)}, u32[]{:S(2)}, u32[]{:S(2)}) collective-permute-start(bf16[128,256]{1,0:T(8,128)(2,1)S(1)} %get-tuple-element.49), channel_id=1, source_target_pairs={{0,6},{2,4},{4,2},{6,0},{8,14},{10,12},{12,10},{14,8},{1,7},{3,5},... | collective-permute-start | bytes 196616 | tf_op jit(solution)/shard_map/ppermute | solution.py:28
  33.6 1.6 %collective-permute-start.13 = (bf16[128,256]{1,0:T(8,128)(2,1)S(1)}, bf16[128,256]{1,0:T(8,128)(2,1)S(1)}, u32[]{:S(2)}, u32[]{:S(2)}) collective-permute-start(bf16[128,256]{1,0:T(8,128)(2,1)S(1)} %get-tuple-element.50), channel_id=1, source_target_pairs={{0,8},{2,10},{4,12},{6,14},{8,0},{10,2},{12,4},{14,6},{1,9},{3,11}... | collective-permute-start | bytes 196616 | tf_op jit(solution)/shard_map/ppermute | solution.py:28
  35.2 1.5 %collective-permute-start.14 = (bf16[128,256]{1,0:T(8,128)(2,1)S(1)}, bf16[128,256]{1,0:T(8,128)(2,1)S(1)}, u32[]{:S(2)}, u32[]{:S(2)}) collective-permute-start(bf16[128,256]{1,0:T(8,128)(2,1)S(1)} %get-tuple-element.51), channel_id=1, source_target_pairs={{0,10},{2,8},{4,14},{6,12},{8,2},{10,0},{12,6},{14,4},{1,11},{3,9}... | collective-permute-start | bytes 196616 | tf_op jit(solution)/shard_map/ppermute | solution.py:28
  36.7 1.8 %collective-permute-start.15 = (bf16[128,256]{1,0:T(8,128)(2,1)S(1)}, bf16[128,256]{1,0:T(8,128)(2,1)S(1)}, u32[]{:S(2)}, u32[]{:S(2)}) collective-permute-start(bf16[128,256]{1,0:T(8,128)(2,1)S(1)} %get-tuple-element.52), channel_id=1, source_target_pairs={{0,12},{2,14},{4,8},{6,10},{8,4},{10,6},{12,0},{14,2},{1,13},{3,15... | collective-permute-start | bytes 196616 | tf_op jit(solution)/shard_map/ppermute | solution.py:28
  38.5 2.8 %collective-permute-start.16 = (bf16[128,256]{1,0:T(8,128)(2,1)S(1)}, bf16[128,256]{1,0:T(8,128)(2,1)S(1)}, u32[]{:S(2)}, u32[]{:S(2)}) collective-permute-start(bf16[128,256]{1,0:T(8,128)(2,1)S(1)} %get-tuple-element.53), channel_id=1, source_target_pairs={{0,14},{2,12},{4,10},{6,8},{8,6},{10,4},{12,2},{14,0},{1,15},{3,13... | collective-permute-start | bytes 196616 | tf_op jit(solution)/shard_map/ppermute | solution.py:28
  42.0 4.0 %collective-permute-done.14.refs_4_ = bf16[128,256]{1,0:T(8,128)(2,1)S(1)} collective-permute-done((bf16[128,256]{1,0:T(8,128)(2,1)S(1)}, bf16[128,256]{1,0:T(8,128)(2,1)S(1)}, u32[]{:S(2)}, u32[]{:S(2)}) %collective-permute-start.14) | collective-permute-done | bytes 65568 | tf_op jit(solution)/shard_map/ppermute | solution.py:28
  46.0 1.1 %moments_two.1 = (f32[256,256]{1,0:T(8,128)S(1)}, f32[256,256]{1,0:T(8,128)S(1)}, f32[8,256]{1,0:T(8,128)S(1)}) custom-call(bf16[256,1024]{1,0:T(8,128)(2,1)S(1)} %get-tuple-element.32.weight, bf16[1024,256]{1,0:T(8,128)(2,1)S(1)} %get-tuple-element.42.table, bf16[256,256]{1,0:T(8,128)(2,1)S(1)} %get-tuple-element.35.own, ...), custom_call_target="tpu_custom_call" | custom-call | tf_op jit(solution)/shard_map/moments_two/pallas_call | solution.py:32
  47.1 1.2 %collective-permute-done.17.part_two = f32[8,256]{1,0:T(8,128)S(1)} collective-permute-done((f32[8,256]{1,0:T(8,128)S(1)}, f32[8,256]{1,0:T(8,128)S(1)}, u32[]{:S(2)}, u32[]{:S(2)}) %collective-permute-start.17) | collective-permute-done | bytes 8224 | tf_op jit(solution)/shard_map/ppermute | solution.py:24
  48.3 1.9 %copy_number.1 = f32[256,256]{1,0:T(8,128)} custom-call(f32[256,256]{1,0:T(8,128)S(1)} %get-tuple-element.54.ratio, f32[256,256]{1,0:T(8,128)S(1)} %get-tuple-element.55.rel, f32[8,256]{1,0:T(8,128)S(1)} %get-tuple-element.56.part, f32[8,256]{1,0:T(8,128)S(1)} %collective-permute-done.17.part_two, f32[256,128]{1,0:T(8,128)S(1)} %broadcast_in_dim.2.plf), custom_call_target="tpu_custom_call" | custom-call | tf_op jit(solution)/shard_map/copy_number/pallas_call | solution.py:32
  (36 shorter events, 5.0 us)
Async XLA Ops:
  0.0 0.9 %copy-start = (bf16[256,256]{1,0:T(8,128)(2,1)S(1)}, bf16[256,256]{1,0:T(8,128)(2,1)}, u32[]{:S(2)}) copy-start(bf16[256,256]{1,0:T(8,128)(2,1)} %coverage.5) | copy-start | bytes 393220
  0.9 0.9 %copy-start.2 = (s32[256,128]{1,0:T(8,128)S(1)}, s32[256,128]{1,0:T(8,128)}, u32[]{:S(2)}) copy-start(s32[256,128]{1,0:T(8,128)} %neighbours.3) | copy-start | bytes 393220
  2.2 10.8 %copy-start.5 = (s32[256]{0:T(256)S(1)}, s32[256]{0:T(256)}, u32[]{:S(2)}) copy-start(s32[256]{0:T(256)} %param.9) | copy-start | bytes 3076
  2.2 10.8 %collective-permute-start = (bf16[272,256]{1,0:T(8,128)(2,1)S(1)}, bf16[272,256]{1,0:T(8,128)(2,1)S(1)}, u32[]{:S(2)}, u32[]{:S(2)}) collective-permute-start(bf16[272,256]{1,0:T(8,128)(2,1)S(1)} %get-tuple-element.34), channel_id=1, source_target_pairs={{0,8},{2,10},{4,12},{6,14},{8,0},{10,2},{12,4},{14,6},{1,9},{3,11}... | collective-permute-start | bytes 417800 | tf_op jit(solution)/shard_map/ppermute | solution.py:28
  6.3 9.4 %collective-permute-start.4 = (bf16[272,256]{1,0:T(8,128)(2,1)S(1)}, bf16[272,256]{1,0:T(8,128)(2,1)S(1)}, u32[]{:S(2)}, u32[]{:S(2)}) collective-permute-start(bf16[272,256]{1,0:T(8,128)(2,1)S(1)} %get-tuple-element.34), channel_id=1, source_target_pairs={{0,6},{2,4},{4,2},{6,0},{8,14},{10,12},{12,10},{14,8},{1,7},{3,5},... | collective-permute-start | bytes 417800 | tf_op jit(solution)/shard_map/ppermute | solution.py:28
  8.8 8.4 %collective-permute-start.3 = (bf16[272,256]{1,0:T(8,128)(2,1)S(1)}, bf16[272,256]{1,0:T(8,128)(2,1)S(1)}, u32[]{:S(2)}, u32[]{:S(2)}) collective-permute-start(bf16[272,256]{1,0:T(8,128)(2,1)S(1)} %get-tuple-element.34), channel_id=1, source_target_pairs={{0,4},{2,6},{4,0},{6,2},{8,12},{10,14},{12,8},{14,10},{1,5},{3,7},... | collective-permute-start | bytes 417800 | tf_op jit(solution)/shard_map/ppermute | solution.py:28
  9.2 7.9 %collective-permute-start.2 = (bf16[272,256]{1,0:T(8,128)(2,1)S(1)}, bf16[272,256]{1,0:T(8,128)(2,1)S(1)}, u32[]{:S(2)}, u32[]{:S(2)}) collective-permute-start(bf16[272,256]{1,0:T(8,128)(2,1)S(1)} %get-tuple-element.34), channel_id=1, source_target_pairs={{0,2},{2,0},{4,6},{6,4},{8,10},{10,8},{12,14},{14,12},{1,3},{3,1},... | collective-permute-start | bytes 417800 | tf_op jit(solution)/shard_map/ppermute | solution.py:28
  13.0 4.1 %copy-start.1 = (bf16[256,256]{1,0:T(8,128)(2,1)S(1)}, bf16[256,256]{1,0:T(8,128)(2,1)}, u32[]{:S(2)}) copy-start(bf16[256,256]{1,0:T(8,128)(2,1)} %coverage.5) | copy-start | bytes 393220
  13.2 4.0 %collective-permute-start.1 = (f32[8,640]{1,0:T(8,128)S(1)}, f32[8,640]{1,0:T(8,128)S(1)}, u32[]{:S(2)}, u32[]{:S(2)}) collective-permute-start(f32[8,640]{1,0:T(8,128)S(1)} %bin_sums.1.mine), channel_id=1, source_target_pairs={{0,1},{1,0},{2,3},{3,2},{4,5},{5,4},{6,7},{7,6},{8,9},{9,8},{10,11... | collective-permute-start | bytes 61448 | tf_op jit(solution)/shard_map/ppermute | solution.py:24
  17.2 4.9 %copy-start.3 = (s32[256,128]{1,0:T(8,128)S(1)}, s32[256,128]{1,0:T(8,128)}, u32[]{:S(2)}) copy-start(s32[256,128]{1,0:T(8,128)} %neighbours.3) | copy-start | bytes 393220
  17.2 4.9 %copy-start.4 = (bf16[256,128]{1,0:T(8,128)(2,1)S(1)}, bf16[256,128]{1,0:T(8,128)(2,1)}, u32[]{:S(2)}) copy-start(bf16[256,128]{1,0:T(8,128)(2,1)} %weight.1) | copy-start | bytes 196612
  18.6 6.4 %collective-permute-start.6 = (bf16[144,256]{1,0:T(8,128)(2,1)S(1)}, bf16[144,256]{1,0:T(8,128)(2,1)S(1)}, u32[]{:S(2)}, u32[]{:S(2)}) collective-permute-start(bf16[144,256]{1,0:T(8,128)(2,1)S(1)} %get-tuple-element.39), channel_id=1, source_target_pairs={{0,2},{2,0},{4,6},{6,4},{8,10},{10,8},{12,14},{14,12},{1,3},{3,1},... | collective-permute-start | bytes 221192 | tf_op jit(solution)/shard_map/ppermute | solution.py:28
  19.1 5.9 %collective-permute-start.7 = (bf16[144,256]{1,0:T(8,128)(2,1)S(1)}, bf16[144,256]{1,0:T(8,128)(2,1)S(1)}, u32[]{:S(2)}, u32[]{:S(2)}) collective-permute-start(bf16[144,256]{1,0:T(8,128)(2,1)S(1)} %get-tuple-element.40), channel_id=1, source_target_pairs={{0,4},{2,6},{4,0},{6,2},{8,12},{10,14},{12,8},{14,10},{1,5},{3,7},... | collective-permute-start | bytes 221192 | tf_op jit(solution)/shard_map/ppermute | solution.py:28
  20.6 5.3 %collective-permute-start.8 = (bf16[144,256]{1,0:T(8,128)(2,1)S(1)}, bf16[144,256]{1,0:T(8,128)(2,1)S(1)}, u32[]{:S(2)}, u32[]{:S(2)}) collective-permute-start(bf16[144,256]{1,0:T(8,128)(2,1)S(1)} %get-tuple-element.41), channel_id=1, source_target_pairs={{0,6},{2,4},{4,2},{6,0},{8,14},{10,12},{12,10},{14,8},{1,7},{3,5},... | collective-permute-start | bytes 221192 | tf_op jit(solution)/shard_map/ppermute | solution.py:28
  22.1 2.9 %collective-permute-start.5 = (f32[8,384]{1,0:T(8,128)S(1)}, f32[8,384]{1,0:T(8,128)S(1)}, u32[]{:S(2)}, u32[]{:S(2)}) collective-permute-start(f32[8,384]{1,0:T(8,128)S(1)} %get-tuple-element.38.sums), channel_id=1, source_target_pairs={{0,1},{1,0},{2,3},{3,2},{4,5},{5,4},{6,7},{7,6},{8,9},{9,8},{10,11... | collective-permute-start | bytes 36872 | tf_op jit(solution)/shard_map/ppermute | solution.py:24
  27.4 1.2 %collective-permute-start.9 = (f32[8,256]{1,0:T(8,128)S(1)}, f32[8,256]{1,0:T(8,128)S(1)}, u32[]{:S(2)}, u32[]{:S(2)}) collective-permute-start(f32[8,256]{1,0:T(8,128)S(1)} %get-tuple-element.45.part), channel_id=1, source_target_pairs={{0,1},{1,0},{2,3},{3,2},{4,5},{5,4},{6,7},{7,6},{8,9},{9,8},{10,11... | collective-permute-start | bytes 24584 | tf_op jit(solution)/shard_map/ppermute | solution.py:24
  30.0 6.7 %collective-permute-start.10 = (bf16[128,256]{1,0:T(8,128)(2,1)S(1)}, bf16[128,256]{1,0:T(8,128)(2,1)S(1)}, u32[]{:S(2)}, u32[]{:S(2)}) collective-permute-start(bf16[128,256]{1,0:T(8,128)(2,1)S(1)} %get-tuple-element.47), channel_id=1, source_target_pairs={{0,2},{2,0},{4,6},{6,4},{8,10},{10,8},{12,14},{14,12},{1,3},{3,1},... | collective-permute-start | bytes 196616 | tf_op jit(solution)/shard_map/ppermute | solution.py:28
  30.8 7.6 %collective-permute-start.11 = (bf16[128,256]{1,0:T(8,128)(2,1)S(1)}, bf16[128,256]{1,0:T(8,128)(2,1)S(1)}, u32[]{:S(2)}, u32[]{:S(2)}) collective-permute-start(bf16[128,256]{1,0:T(8,128)(2,1)S(1)} %get-tuple-element.48), channel_id=1, source_target_pairs={{0,4},{2,6},{4,0},{6,2},{8,12},{10,14},{12,8},{14,10},{1,5},{3,7},... | collective-permute-start | bytes 196616 | tf_op jit(solution)/shard_map/ppermute | solution.py:28
  32.1 9.1 %collective-permute-start.12 = (bf16[128,256]{1,0:T(8,128)(2,1)S(1)}, bf16[128,256]{1,0:T(8,128)(2,1)S(1)}, u32[]{:S(2)}, u32[]{:S(2)}) collective-permute-start(bf16[128,256]{1,0:T(8,128)(2,1)S(1)} %get-tuple-element.49), channel_id=1, source_target_pairs={{0,6},{2,4},{4,2},{6,0},{8,14},{10,12},{12,10},{14,8},{1,7},{3,5},... | collective-permute-start | bytes 196616 | tf_op jit(solution)/shard_map/ppermute | solution.py:28
  33.6 8.4 %collective-permute-start.13 = (bf16[128,256]{1,0:T(8,128)(2,1)S(1)}, bf16[128,256]{1,0:T(8,128)(2,1)S(1)}, u32[]{:S(2)}, u32[]{:S(2)}) collective-permute-start(bf16[128,256]{1,0:T(8,128)(2,1)S(1)} %get-tuple-element.50), channel_id=1, source_target_pairs={{0,8},{2,10},{4,12},{6,14},{8,0},{10,2},{12,4},{14,6},{1,9},{3,11}... | collective-permute-start | bytes 196616 | tf_op jit(solution)/shard_map/ppermute | solution.py:28
  35.2 10.9 %collective-permute-start.14 = (bf16[128,256]{1,0:T(8,128)(2,1)S(1)}, bf16[128,256]{1,0:T(8,128)(2,1)S(1)}, u32[]{:S(2)}, u32[]{:S(2)}) collective-permute-start(bf16[128,256]{1,0:T(8,128)(2,1)S(1)} %get-tuple-element.51), channel_id=1, source_target_pairs={{0,10},{2,8},{4,14},{6,12},{8,2},{10,0},{12,6},{14,4},{1,11},{3,9}... | collective-permute-start | bytes 196616 | tf_op jit(solution)/shard_map/ppermute | solution.py:28
  36.7 9.3 %collective-permute-start.15 = (bf16[128,256]{1,0:T(8,128)(2,1)S(1)}, bf16[128,256]{1,0:T(8,128)(2,1)S(1)}, u32[]{:S(2)}, u32[]{:S(2)}) collective-permute-start(bf16[128,256]{1,0:T(8,128)(2,1)S(1)} %get-tuple-element.52), channel_id=1, source_target_pairs={{0,12},{2,14},{4,8},{6,10},{8,4},{10,6},{12,0},{14,2},{1,13},{3,15... | collective-permute-start | bytes 196616 | tf_op jit(solution)/shard_map/ppermute | solution.py:28
  38.5 7.6 %collective-permute-start.16 = (bf16[128,256]{1,0:T(8,128)(2,1)S(1)}, bf16[128,256]{1,0:T(8,128)(2,1)S(1)}, u32[]{:S(2)}, u32[]{:S(2)}) collective-permute-start(bf16[128,256]{1,0:T(8,128)(2,1)S(1)} %get-tuple-element.53), channel_id=1, source_target_pairs={{0,14},{2,12},{4,10},{6,8},{8,6},{10,4},{12,2},{14,0},{1,15},{3,13... | collective-permute-start | bytes 196616 | tf_op jit(solution)/shard_map/ppermute | solution.py:28
  47.1 1.2 %collective-permute-start.17 = (f32[8,256]{1,0:T(8,128)S(1)}, f32[8,256]{1,0:T(8,128)S(1)}, u32[]{:S(2)}, u32[]{:S(2)}) collective-permute-start(f32[8,256]{1,0:T(8,128)S(1)} %get-tuple-element.56.part), channel_id=1, source_target_pairs={{0,1},{1,0},{2,3},{3,2},{4,5},{5,4},{6,7},{7,6},{8,9},{9,8},{10,11... | collective-permute-start | bytes 24584 | tf_op jit(solution)/shard_map/ppermute | solution.py:24
  (1 other events, 0.7 us)

commit v3 on v2

--- a/solution.py
+++ b/solution.py
@@ -57,8 +57,7 @@
     return chosen
 
 
-def ask_kernel(neighbours, coverage, noted, ask):
-    rows, cols = coverage.shape
+def ask_kernel(rows, neighbours, ask):
     index = neighbours[...]
     position = lax.div(index, rows) ^ lax.axis_index("samp")
     block = lax.div(lax.rem(index, rows), RBLK)
@@ -68,13 +67,10 @@
     ]
     best += [jnp.zeros_like(best[0])] * (ask.shape[0] - count)
     best = jnp.max(jnp.concatenate(best, axis=0), axis=1, keepdims=True)
-    wide = jnp.broadcast_to(best.astype(F32), ask.shape).astype(BF16)
-    ask[...] = wide
-    noted[0:rows] = coverage[...]
-    noted[rows:] = wide
-
-
-def map_kernel(neighbours, weight, ask, out, total, wide):
+    ask[...] = jnp.broadcast_to(best.astype(F32), ask.shape).astype(BF16)
+
+
+def map_kernel(neighbours, weight, plf, noted, out, total, wide):
     rows = neighbours.shape[0]
     listed = neighbours.shape[1]
     count = lax.axis_size("samp")
@@ -117,51 +113,42 @@
     return (lax.broadcasted_iota(jnp.int32, (NGC, gc.shape[1]), 0) == gc[...]).astype(F32)
 
 
-def bin_sums(onehot, block):
-    return dot(onehot.astype(BF16), block, 1, 1)
-
-
-def factors(sums, number, targets):
-    mean = jnp.sum(sums, axis=0, keepdims=True) / targets
-    scale = mean / (sums / jnp.maximum(number, 1.0))
-    return jnp.where(sums > 0, scale, 0.0)
-
-
-def normal(block, scale, onehot):
-    return (block.astype(F32) * dot(scale, onehot, 0, 0, EXACT)).astype(BF16)
-
-
-def stats_kernel(coverage, across, gc, stats):
+def stats_kernel(coverage, gc, stats):
     rows = coverage.shape[0]
     onehot = bin_rows(gc)
-    stats[:, 0:rows] = bin_sums(onehot, coverage[...])
-    stats[:, rows : 2 * rows] = bin_sums(onehot, across[0:rows])
+    stats[:, 0:rows] = dot(onehot.astype(BF16), coverage[...], 1, 1)
     number = jnp.sum(onehot, axis=1, keepdims=True)
-    stats[:, 2 * rows :] = jnp.broadcast_to(number, (NGC, LANE))
-
-
-def norm_kernel(half, coverage, across, mine, theirs, gc, ask, *refs):
-    noted, refs = refs[: half - 1], refs[half - 1 :]
-    own, near, far, raw, sums = refs[:5]
-    passed = refs[5:]
+    stats[:, rows:] = jnp.broadcast_to(number, (NGC, LANE))
+
+
+def norm_kernel(coverage, mine, theirs, gc, ask, noted):
     rows, cols = coverage.shape
+    onehot = bin_rows(gc)
+    sums = mine[:, 0:rows] + theirs[:, 0:rows]
+    number = mine[:, rows : rows + 1] + theirs[:, rows : rows + 1]
+    mean = jnp.sum(sums, axis=0, keepdims=True) / (cols * lax.axis_size("tgt"))
+    scale = mean / (sums / jnp.maximum(number, 1.0))
+    scale = dot(jnp.where(sums > 0, scale, 0.0), onehot, 0, 0, EXACT)
+    noted[0:rows] = (coverage[...].astype(F32) * scale).astype(BF16)
+    noted[rows:] = ask[...]
+
+
+def pass_kernel(relay, asked, total, across, *refs):
+    mates = len(refs) // 2
+    half = mates + 1
+    noted, out = refs[:mates], refs[mates:]
+    rows = across.shape[0] - asked
     parts = rows // RBLK
-    targets = cols * lax.axis_size("tgt")
-    onehot = bin_rows(gc)
-    number = mine[:, 2 * rows : 2 * rows + 1] + theirs[:, 2 * rows : 2 * rows + 1]
-    scale = factors(mine[:, 0 : 2 * rows] + theirs[:, 0 : 2 * rows], number, targets)
-    own[...] = normal(coverage[...], scale[:, 0:rows], onehot)
-    far[...] = normal(across[0:rows], scale[:, rows : 2 * rows], onehot)
-    near[0:RBLK] = pick(own, ask[0:1], parts)
-    near[RBLK : 2 * RBLK] = pick(far, ask[half : half + 1], parts)
     for k in range(1, half):
         note = noted[k - 1]
-        other = k ^ half
-        passed[k - 1][0:RBLK] = pick(far, note[rows + other : rows + other + 1], parts)
-        passed[k - 1][RBLK:] = across[rows:]
-        place = pl.ds((k - 1) * RBLK, RBLK)
-        raw[place, :] = pick(note, ask[k : k + 1], parts)
-        sums[:, (k - 1) * RBLK : k * RBLK] = bin_sums(onehot, raw[place, :])
+        base = note.shape[0] - asked
+        other = base + (k ^ half)
+        out[k - 1][0:RBLK] = pick(across, note[other : other + 1], parts)
+        last = RBLK
+        if relay and k == 1:
+            out[0][RBLK : 2 * RBLK] = pick(noted[1], note[base + 3 : base + 4], parts)
+            last = 2 * RBLK
+        out[k - 1][last:] = across[rows:]
 
 
 def spread(first, second, third, normf, ratio, rel, part):
@@ -178,29 +165,34 @@
     return (wide * wide).astype(BF16)
 
 
-def first_kernel(half, weight, total, own, near, raw, sums, sums_two, mine, theirs, gc, *refs):
-    passed, refs = refs[: half - 1], refs[half - 1 :]
-    table, ratio, rel, part = refs
-    rows, cols = own.shape
-    onehot = bin_rows(gc)
-    number = mine[:, 2 * rows : 2 * rows + 1] + theirs[:, 2 * rows : 2 * rows + 1]
-    scale = factors(sums[...] + sums_two[...], number, cols * lax.axis_size("tgt"))
-    table[0:RBLK] = near[0:RBLK]
-    table[half * RBLK : (half + 1) * RBLK] = near[RBLK : 2 * RBLK]
-    table[RBLK : half * RBLK] = normal(raw[...], scale, onehot)
+def first_kernel(relay, rows, weight, total, own, across, ask, *refs):
+    mates = (len(refs) - 4) // 2
+    half = mates + 1
+    noted, passed, (table, ratio, rel, part) = refs[:mates], refs[mates : 2 * mates], refs[2 * mates :]
+    cols = own.shape[1]
+    parts = rows // RBLK
+    table[0:RBLK] = pick(own, ask[0:1], parts)
+    table[half * RBLK : (half + 1) * RBLK] = pick(across, ask[half : half + 1], parts)
     for k in range(1, half):
+        if relay and k == 3:
+            here = passed[0][RBLK : 2 * RBLK]
+        else:
+            here = pick(noted[k - 1], ask[k : k + 1], parts)
+        table[k * RBLK : (k + 1) * RBLK] = here
         other = k ^ half
         table[other * RBLK : (other + 1) * RBLK] = passed[k - 1][0:RBLK]
     second = dot(weight[...], table[...], 1, 0)
     third = dot(weight[...], squared(table[...]), 1, 0)
     first = jnp.concatenate([total[...]] * (cols // LANE), axis=1)
-    spread(first, second, third, own[...].astype(F32), ratio, rel, part)
-
-
-def second_kernel(count, weight, table, own, gate, ask, *refs):
-    arrived, refs = refs[: count - 1], refs[count - 1 :]
+    spread(first, second, third, own[0:rows].astype(F32), ratio, rel, part)
+
+
+def second_kernel(order, weight, table, own, gate, ask, *refs):
+    count = len(order) + 1
+    arrived = [refs[order.index(p)] for p in range(1, count)]
+    refs = refs[count - 1 :]
     ratio, rel, part = refs
-    rows, cols = own.shape
+    rows, cols = gate.shape
     gates = [pick(gate, ask[0:1], rows // RBLK)] + [ref[...] for ref in arrived]
     gates = jnp.concatenate(gates, axis=0)
     wide = gates.astype(F32)
@@ -209,7 +201,7 @@
     first = dot(weight[...], gates, 1, 0)
     second = dot(weight[...], covs, 1, 0)
     third = dot(weight[...], squares, 1, 0)
-    spread(first, second, third, own[...].astype(F32), ratio, rel, part)
+    spread(first, second, third, own[0:rows].astype(F32), ratio, rel, part)
 
 
 def called(ratio, rel, part, part_two, plf, finish):
@@ -240,25 +232,26 @@
             finish(here, there, top / functools.reduce(jnp.add, expo), ploidy)
 
 
-def gate_kernel(half, parts, ratio, rel, part, part_two, plf, across, *refs):
-    count = 2 * half
+def gate_kernel(asked, ratio, rel, part, part_two, plf, across, *refs):
     rows = ratio.shape[0]
-    noted, passed, refs = refs[: half - 1], refs[half - 1 : 2 * half - 2], refs[2 * half - 2 :]
-    gate, out = refs[0], refs[1:]
+    mates = (len(refs) - 2) // 4
+    half = mates + 1
+    noted, passed, gate, out = refs[:mates], refs[mates : 2 * mates], refs[2 * mates], refs[2 * mates + 1 :]
 
     def finish(here, there, value, ploidy):
         offset = value - ploidy
         gate[here, there] = (1.0 / (1.0 + 4.0 * (offset * offset))).astype(BF16)
 
     called(ratio, rel, part, part_two, plf, finish)
-    for p in range(1, count):
+    for p in range(1, 2 * half):
         if p < half:
-            ask = noted[p - 1][rows + p : rows + p + 1]
+            source = noted[p - 1]
         elif p == half:
-            ask = across[rows + p : rows + p + 1]
+            source = across
         else:
-            ask = passed[(p ^ half) - 1][RBLK + p : RBLK + p + 1]
-        out[p - 1][...] = pick(gate, ask, parts)
+            source = passed[(p ^ half) - 1]
+        place = source.shape[0] - asked + p
+        out[p - 1][...] = pick(gate, source[place : place + 1], rows // RBLK)
 
 
 def final_kernel(ratio, rel, part, part_two, plf, out):
@@ -273,57 +266,51 @@
     half = count // 2
     mates = range(1, half)
     rows, cols = coverage.shape
-    listed = neighbours.shape[1]
-    parts = rows // RBLK
     extra = -(-count // 16) * 16
+    relay = half > 3
     gc = gc_bin.reshape(1, cols)
     plf = jnp.broadcast_to(ploidy.astype(F32)[:, None], (rows, LANE))
 
-    noted, ask = call(
-        ask_kernel, "choices", [((rows + extra, cols), BF16), ((extra, cols), BF16)],
-        neighbours, coverage,
-    )
-    across = send(noted, half, count)
-    noted = [send(noted, k, count) for k in mates]
+    (mine,) = call(stats_kernel, "bin_sums", [((NGC, rows + LANE), F32)], coverage, gc)
+    theirs = swap_tgt(mine)
+    (ask,) = call(
+        functools.partial(ask_kernel, rows), "choices", [((extra, cols), BF16)], neighbours
+    )
+    (own,) = call(
+        norm_kernel, "normalise", [((rows + extra, cols), BF16)], coverage, mine, theirs, gc, ask
+    )
+    across = send(own, half, count)
+    noted = [send(ask if relay and k == 3 else own, k, count) for k in mates]
     weight, total = call(
         map_kernel, "weight_map", [((rows, count * RBLK), BF16), ((rows, LANE), F32)],
-        neighbours, nbr_weight, ask, scratch=[pltpu.VMEM((count, rows, RBLK), F32)],
-    )
-    (mine,) = call(
-        stats_kernel, "bin_sums", [((NGC, 2 * rows + LANE), F32)], coverage, across, gc
-    )
-    theirs = swap_tgt(mine)
-    own, near, _, raw, sums, *passed = call(
-        functools.partial(norm_kernel, half), "normalise",
-        [
-            ((rows, cols), BF16),
-            ((2 * RBLK, cols), BF16),
-            ((rows, cols), BF16),
-            ((len(mates) * RBLK, cols), BF16),
-            ((NGC, len(mates) * RBLK), F32),
-        ] + [((RBLK + extra, cols), BF16)] * len(mates),
-        coverage, across, mine, theirs, gc, ask, *noted,
+        neighbours, nbr_weight, plf, own, scratch=[pltpu.VMEM((count, rows, RBLK), F32)],
+    )
+    passed = call(
+        functools.partial(pass_kernel, relay, extra), "pass_on",
+        [(((2 if relay and k == 1 else 1) * RBLK + extra, cols), BF16) for k in mates],
+        total, across, *noted,
     )
     passed = [send(block, k, count) for k, block in zip(mates, passed)]
-    sums_two = swap_tgt(sums)
     table, ratio, rel, part = call(
-        functools.partial(first_kernel, half), "moments_one",
+        functools.partial(first_kernel, relay, rows), "moments_one",
         [
             ((count * RBLK, cols), BF16),
             ((rows, cols), F32),
             ((rows, cols), F32),
             ((NGC, rows), F32),
         ],
-        weight, total, own, near, raw, sums, sums_two, mine, theirs, gc, *passed,
+        weight, total, own, across, ask, *noted, *passed,
     )
     gate, *gates = call(
-        functools.partial(gate_kernel, half, parts), "gate",
+        functools.partial(gate_kernel, extra), "gate",
         [((rows, cols), BF16)] + [((RBLK, cols), BF16)] * (count - 1),
         ratio, rel, part, swap_tgt(part), plf, across, *noted, *passed,
     )
-    gates = [send(block, p, count) for p, block in enumerate(gates, 1)]
+    order = [(half - 1 - i // 2) ^ (half if i % 2 == 0 else 0) for i in range(count)]
+    order = [p for p in order if p]
+    gates = [send(gates[p - 1], p, count) for p in order]
     ratio, rel, part = call(
-        functools.partial(second_kernel, count), "moments_two",
+        functools.partial(second_kernel, order), "moments_two",
         [((rows, cols), F32), ((rows, cols), F32), ((NGC, rows), F32)],
         weight, table, own, gate, ask, *gates,
     )

time: 50.5 us -> 47.3 us (0.937)
  waiting for transfers between devices: 14.6 us -> 12.6 us
  Pallas kernels: 10.7 us -> 9.16 us
  starting transfers between devices: 22.2 us -> 22.9 us
    ppermute x14, waiting for transfers between devices: 12.9 us -> 9.72 us  [send(): return lax.ppermute(value, 'samp', [(i, i ^ step) for i in range(count)])]
    pallas_call x8 -> x9, Pallas kernels: 10.7 us -> 9.16 us  [call(): pl.pallas_call(body, out_shape=[jax.ShapeDtypeStruct(shape, dtype) for sh...]
    ppermute x4 -> x3, waiting for transfers between devices: 1.7 us -> 2.86 us  [swap_tgt(): return lax.ppermute(value, 'tgt', [(0, 1), (1, 0)])]
    unnamed x14 -> x10, local copies, waits for them, and re-layouts: 2.54 us -> 2.37 us
  transfers between devices with their start and end apart: 18 -> 17, of which waited for: 8 -> 9; matrix products, arithmetic and copies ran while one was open for 0% -> 0% of each run, Pallas kernels for 6% -> 7%
where the time goes in v3:
time: 47.3 us; the launch traced here: 47.1 us
  starting transfers between devices  22.9 us (48%)
  waiting for transfers between devices  12.6 us (27%)
  Pallas kernels  9.16 us (19%)
  local copies, waits for them, and re-layouts  2.46 us (5%)
    ppermute x14, starting transfers between devices, send(): return lax.ppermute(value, 'samp', [(i, i ^ step) for i in range(count)])  22.4 us
    ppermute x14, waiting for transfers between devices, send(): return lax.ppermute(value, 'samp', [(i, i ^ step) for i in range(count)])  9.72 us
    pallas_call x9, Pallas kernels, call(): pl.pallas_call(body, out_shape=[jax.ShapeDtypeStruct(shape, dtype) for sh...  9.16 us
    ppermute x3, waiting for transfers between devices, swap_tgt(): return lax.ppermute(value, 'tgt', [(0, 1), (1, 0)])  2.86 us
    unnamed x10, local copies, waits for them, and re-layouts  2.37 us
  transfers between devices with their start and end apart: 17, of which 9 were waited for; matrix products, arithmetic and copies ran while one was open for 0% of the time, Pallas kernels for 7%

profile of v3, /device:TPU:0, one launch (start us, length us, event | category | flops | bytes accessed | tf_op | source)
XLA Modules:
  0.0 47.1 jit_solution(8759814061522130955)
XLA Ops:
  0.0 0.9 %copy-done.1 = bf16[256,256]{1,0:T(8,128)(2,1)S(1)} copy-done((bf16[256,256]{1,0:T(8,128)(2,1)S(1)}, bf16[256,256]{1,0:T(8,128)(2,1)}, u32[]{:S(2)}) %copy-start.1) | copy-done | bytes 131096
  0.9 0.7 %copy-done.3 = s32[256]{0:T(256)S(1)} copy-done((s32[256]{0:T(256)S(1)}, s32[256]{0:T(256)}, u32[]{:S(2)}) %copy-start.3) | copy-done | bytes 1048
  3.6 3.0 %collective-permute-start.3 = (bf16[272,256]{1,0:T(8,128)(2,1)S(1)}, bf16[272,256]{1,0:T(8,128)(2,1)S(1)}, u32[]{:S(2)}, u32[]{:S(2)}) collective-permute-start(bf16[272,256]{1,0:T(8,128)(2,1)S(1)} %normalise.1.noted.own), channel_id=1, source_target_pairs={{0,4},{2,6},{4,0},{6,2},{8,12},{10,14},{12,8},{14,10},{1,5},{3,7},... | collective-permute-start | bytes 417800 | tf_op jit(solution)/shard_map/ppermute | solution.py:28
  6.6 1.5 %collective-permute-start.2 = (bf16[272,256]{1,0:T(8,128)(2,1)S(1)}, bf16[272,256]{1,0:T(8,128)(2,1)S(1)}, u32[]{:S(2)}, u32[]{:S(2)}) collective-permute-start(bf16[272,256]{1,0:T(8,128)(2,1)S(1)} %normalise.1.noted.own), channel_id=1, source_target_pairs={{0,2},{2,0},{4,6},{6,4},{8,10},{10,8},{12,14},{14,12},{1,3},{3,1},... | collective-permute-start | bytes 417800 | tf_op jit(solution)/shard_map/ppermute | solution.py:28
  8.1 2.6 %collective-permute-start.1 = (bf16[272,256]{1,0:T(8,128)(2,1)S(1)}, bf16[272,256]{1,0:T(8,128)(2,1)S(1)}, u32[]{:S(2)}, u32[]{:S(2)}) collective-permute-start(bf16[272,256]{1,0:T(8,128)(2,1)S(1)} %normalise.1.noted.own), channel_id=1, source_target_pairs={{0,8},{2,10},{4,12},{6,14},{8,0},{10,2},{12,4},{14,6},{1,9},{3,11}... | collective-permute-start | bytes 417800 | tf_op jit(solution)/shard_map/ppermute | solution.py:28
  11.2 0.7 %copy-done.2 = bf16[256,128]{1,0:T(8,128)(2,1)S(1)} copy-done((bf16[256,128]{1,0:T(8,128)(2,1)S(1)}, bf16[256,128]{1,0:T(8,128)(2,1)}, u32[]{:S(2)}) %copy-start.2) | copy-done | bytes 65560
  11.9 2.9 %weight_map.1 = (bf16[256,1024]{1,0:T(8,128)(2,1)S(1)}, f32[256,128]{1,0:T(8,128)S(1)}) custom-call(s32[256,128]{1,0:T(8,128)S(1)} %copy-done, bf16[256,128]{1,0:T(8,128)(2,1)S(1)} %copy-done.2, f32[256,128]{1,0:T(8,128)S(1)} %broadcast_in_dim.2.plf, bf16[272,256]{1,0:T(8,128)(2,1)S(1)} %normalise.1.noted.own), custom_call_target="tpu_custom_call" | custom-call | tf_op jit(solution)/shard_map/weight_map/pallas_call | solution.py:32
  15.2 1.9 %collective-permute-done.1.across = bf16[272,256]{1,0:T(8,128)(2,1)S(1)} collective-permute-done((bf16[272,256]{1,0:T(8,128)(2,1)S(1)}, bf16[272,256]{1,0:T(8,128)(2,1)S(1)}, u32[]{:S(2)}, u32[]{:S(2)}) %collective-permute-start.1) | collective-permute-done | bytes 139296 | tf_op jit(solution)/shard_map/ppermute | solution.py:28
  18.1 2.7 %collective-permute-start.7 = (bf16[144,256]{1,0:T(8,128)(2,1)S(1)}, bf16[144,256]{1,0:T(8,128)(2,1)S(1)}, u32[]{:S(2)}, u32[]{:S(2)}) collective-permute-start(bf16[144,256]{1,0:T(8,128)(2,1)S(1)} %get-tuple-element.29), channel_id=1, source_target_pairs={{0,6},{2,4},{4,2},{6,0},{8,14},{10,12},{12,10},{14,8},{1,7},{3,5},... | collective-permute-start | bytes 221192 | tf_op jit(solution)/shard_map/ppermute | solution.py:28
  20.8 1.4 %collective-permute-done.6.refs_4_ = bf16[144,256]{1,0:T(8,128)(2,1)S(1)} collective-permute-done((bf16[144,256]{1,0:T(8,128)(2,1)S(1)}, bf16[144,256]{1,0:T(8,128)(2,1)S(1)}, u32[]{:S(2)}, u32[]{:S(2)}) %collective-permute-start.6) | collective-permute-done | bytes 73760 | tf_op jit(solution)/shard_map/ppermute | solution.py:28
  22.2 1.7 %collective-permute-done.7.refs_5_ = bf16[144,256]{1,0:T(8,128)(2,1)S(1)} collective-permute-done((bf16[144,256]{1,0:T(8,128)(2,1)S(1)}, bf16[144,256]{1,0:T(8,128)(2,1)S(1)}, u32[]{:S(2)}, u32[]{:S(2)}) %collective-permute-start.7) | collective-permute-done | bytes 73760 | tf_op jit(solution)/shard_map/ppermute | solution.py:28
  23.9 1.0 %moments_one.1 = (bf16[1024,256]{1,0:T(8,128)(2,1)S(1)}, f32[256,256]{1,0:T(8,128)S(1)}, f32[256,256]{1,0:T(8,128)S(1)}, f32[8,256]{1,0:T(8,128)S(1)}) custom-call(bf16[256,1024]{1,0:T(8,128)(2,1)S(1)} %get-tuple-element.25.weight, f32[256,128]{1,0:T(8,128)S(1)} %get-tuple-element.26.total, bf16[272,256]{1,0:T(8,128)(2,1)S(1)} %normalise.1.noted.own, ...), custom_call_target="tpu_custom_call" | custom-call | tf_op jit(solution)/shard_map/moments_one/pallas_call | solution.py:32
  24.9 1.2 %collective-permute-done.8.part_two = f32[8,256]{1,0:T(8,128)S(1)} collective-permute-done((f32[8,256]{1,0:T(8,128)S(1)}, f32[8,256]{1,0:T(8,128)S(1)}, u32[]{:S(2)}, u32[]{:S(2)}) %collective-permute-start.8) | collective-permute-done | bytes 8224 | tf_op jit(solution)/shard_map/ppermute | solution.py:24
  26.1 1.3 %gate.1 = (bf16[256,256]{1,0:T(8,128)(2,1)S(1)}, bf16[128,256]{1,0:T(8,128)(2,1)S(1)}, bf16[128,256]{1,0:T(8,128)(2,1)S(1)}, bf16[128,256]{1,0:T(8,128)(2,1)S(1)...) custom-call(f32[256,256]{1,0:T(8,128)S(1)} %get-tuple-element.31.rat, ...), custom_call_target="tpu_custom_call" | custom-call | tf_op jit(solution)/shard_map/gate/pallas_call | solution.py:32
  27.4 2.7 %collective-permute-start.9 = (bf16[128,256]{1,0:T(8,128)(2,1)S(1)}, bf16[128,256]{1,0:T(8,128)(2,1)S(1)}, u32[]{:S(2)}, u32[]{:S(2)}) collective-permute-start(bf16[128,256]{1,0:T(8,128)(2,1)S(1)} %get-tuple-element.35), channel_id=1, source_target_pairs={{0,14},{2,12},{4,10},{6,8},{8,6},{10,4},{12,2},{14,0},{1,15},{3,13... | collective-permute-start | bytes 196616 | tf_op jit(solution)/shard_map/ppermute | solution.py:28
  30.0 1.1 %collective-permute-start.10 = (bf16[128,256]{1,0:T(8,128)(2,1)S(1)}, bf16[128,256]{1,0:T(8,128)(2,1)S(1)}, u32[]{:S(2)}, u32[]{:S(2)}) collective-permute-start(bf16[128,256]{1,0:T(8,128)(2,1)S(1)} %get-tuple-element.36), channel_id=1, source_target_pairs={{0,6},{2,4},{4,2},{6,0},{8,14},{10,12},{12,10},{14,8},{1,7},{3,5},... | collective-permute-start | bytes 196616 | tf_op jit(solution)/shard_map/ppermute | solution.py:28
  31.1 1.3 %collective-permute-start.11 = (bf16[128,256]{1,0:T(8,128)(2,1)S(1)}, bf16[128,256]{1,0:T(8,128)(2,1)S(1)}, u32[]{:S(2)}, u32[]{:S(2)}) collective-permute-start(bf16[128,256]{1,0:T(8,128)(2,1)S(1)} %get-tuple-element.37), channel_id=1, source_target_pairs={{0,12},{2,14},{4,8},{6,10},{8,4},{10,6},{12,0},{14,2},{1,13},{3,15... | collective-permute-start | bytes 196616 | tf_op jit(solution)/shard_map/ppermute | solution.py:28
  32.4 0.8 %collective-permute-start.12 = (bf16[128,256]{1,0:T(8,128)(2,1)S(1)}, bf16[128,256]{1,0:T(8,128)(2,1)S(1)}, u32[]{:S(2)}, u32[]{:S(2)}) collective-permute-start(bf16[128,256]{1,0:T(8,128)(2,1)S(1)} %get-tuple-element.38), channel_id=1, source_target_pairs={{0,4},{2,6},{4,0},{6,2},{8,12},{10,14},{12,8},{14,10},{1,5},{3,7},... | collective-permute-start | bytes 196616 | tf_op jit(solution)/shard_map/ppermute | solution.py:28
  33.3 3.2 %collective-permute-start.13 = (bf16[128,256]{1,0:T(8,128)(2,1)S(1)}, bf16[128,256]{1,0:T(8,128)(2,1)S(1)}, u32[]{:S(2)}, u32[]{:S(2)}) collective-permute-start(bf16[128,256]{1,0:T(8,128)(2,1)S(1)} %get-tuple-element.39), channel_id=1, source_target_pairs={{0,10},{2,8},{4,14},{6,12},{8,2},{10,0},{12,6},{14,4},{1,11},{3,9}... | collective-permute-start | bytes 196616 | tf_op jit(solution)/shard_map/ppermute | solution.py:28
  37.0 1.8 %collective-permute-start.15 = (bf16[128,256]{1,0:T(8,128)(2,1)S(1)}, bf16[128,256]{1,0:T(8,128)(2,1)S(1)}, u32[]{:S(2)}, u32[]{:S(2)}) collective-permute-start(bf16[128,256]{1,0:T(8,128)(2,1)S(1)} %get-tuple-element.41), channel_id=1, source_target_pairs={{0,8},{2,10},{4,12},{6,14},{8,0},{10,2},{12,4},{14,6},{1,9},{3,11}... | collective-permute-start | bytes 196616 | tf_op jit(solution)/shard_map/ppermute | solution.py:28
  38.7 3.9 %collective-permute-done.13.refs_4_ = bf16[128,256]{1,0:T(8,128)(2,1)S(1)} collective-permute-done((bf16[128,256]{1,0:T(8,128)(2,1)S(1)}, bf16[128,256]{1,0:T(8,128)(2,1)S(1)}, u32[]{:S(2)}, u32[]{:S(2)}) %collective-permute-start.13) | collective-permute-done | bytes 65568 | tf_op jit(solution)/shard_map/ppermute | solution.py:28
  43.0 1.1 %moments_two.1 = (f32[256,256]{1,0:T(8,128)S(1)}, f32[256,256]{1,0:T(8,128)S(1)}, f32[8,256]{1,0:T(8,128)S(1)}) custom-call(bf16[256,1024]{1,0:T(8,128)(2,1)S(1)} %get-tuple-element.25.weight, bf16[1024,256]{1,0:T(8,128)(2,1)S(1)} %get-tuple-element.30.table, bf16[272,256]{1,0:T(8,128)(2,1)S(1)} %normalise.1.noted.own, ...), custom_call_target="tpu_custom_call" | custom-call | tf_op jit(solution)/shard_map/moments_two/pallas_call | solution.py:32
  44.1 1.2 %collective-permute-done.16.part_two = f32[8,256]{1,0:T(8,128)S(1)} collective-permute-done((f32[8,256]{1,0:T(8,128)S(1)}, f32[8,256]{1,0:T(8,128)S(1)}, u32[]{:S(2)}, u32[]{:S(2)}) %collective-permute-start.16) | collective-permute-done | bytes 8224 | tf_op jit(solution)/shard_map/ppermute | solution.py:24
  45.3 1.9 %copy_number.1 = f32[256,256]{1,0:T(8,128)} custom-call(f32[256,256]{1,0:T(8,128)S(1)} %get-tuple-element.42.ratio, f32[256,256]{1,0:T(8,128)S(1)} %get-tuple-element.43.rel, f32[8,256]{1,0:T(8,128)S(1)} %get-tuple-element.44.part, f32[8,256]{1,0:T(8,128)S(1)} %collective-permute-done.16.part_two, f32[256,128]{1,0:T(8,128)S(1)} %broadcast_in_dim.2.plf), custom_call_target="tpu_custom_call" | custom-call | tf_op jit(solution)/shard_map/copy_number/pallas_call | solution.py:32
  (31 shorter events, 4.6 us)
Async XLA Ops:
  0.0 2.3 %copy-start = (s32[256,128]{1,0:T(8,128)S(1)}, s32[256,128]{1,0:T(8,128)}, u32[]{:S(2)}) copy-start(s32[256,128]{1,0:T(8,128)} %neighbours.3) | copy-start | bytes 393220
  0.0 0.9 %copy-start.1 = (bf16[256,256]{1,0:T(8,128)(2,1)S(1)}, bf16[256,256]{1,0:T(8,128)(2,1)}, u32[]{:S(2)}) copy-start(bf16[256,256]{1,0:T(8,128)(2,1)} %coverage.3) | copy-start | bytes 393220
  0.9 0.7 %copy-start.3 = (s32[256]{0:T(256)S(1)}, s32[256]{0:T(256)}, u32[]{:S(2)}) copy-start(s32[256]{0:T(256)} %param.9) | copy-start | bytes 3076
  1.8 1.3 %collective-permute-start = (f32[8,384]{1,0:T(8,128)S(1)}, f32[8,384]{1,0:T(8,128)S(1)}, u32[]{:S(2)}, u32[]{:S(2)}) collective-permute-start(f32[8,384]{1,0:T(8,128)S(1)} %bin_sums.1.mine), channel_id=1, source_target_pairs={{0,1},{1,0},{2,3},{3,2},{4,5},{5,4},{6,7},{7,6},{8,9},{9,8},{10,11... | collective-permute-start | bytes 36872 | tf_op jit(solution)/shard_map/ppermute | solution.py:24
  2.6 8.4 %copy-start.4 = (s32[256]{0:T(256)S(1)}, s32[256]{0:T(256)}, u32[]{:S(2)}) copy-start(s32[256]{0:T(256)} %param.8) | copy-start | bytes 3076
  3.6 11.6 %collective-permute-start.3 = (bf16[272,256]{1,0:T(8,128)(2,1)S(1)}, bf16[272,256]{1,0:T(8,128)(2,1)S(1)}, u32[]{:S(2)}, u32[]{:S(2)}) collective-permute-start(bf16[272,256]{1,0:T(8,128)(2,1)S(1)} %normalise.1.noted.own), channel_id=1, source_target_pairs={{0,4},{2,6},{4,0},{6,2},{8,12},{10,14},{12,8},{14,10},{1,5},{3,7},... | collective-permute-start | bytes 417800 | tf_op jit(solution)/shard_map/ppermute | solution.py:28
  6.6 8.7 %collective-permute-start.2 = (bf16[272,256]{1,0:T(8,128)(2,1)S(1)}, bf16[272,256]{1,0:T(8,128)(2,1)S(1)}, u32[]{:S(2)}, u32[]{:S(2)}) collective-permute-start(bf16[272,256]{1,0:T(8,128)(2,1)S(1)} %normalise.1.noted.own), channel_id=1, source_target_pairs={{0,2},{2,0},{4,6},{6,4},{8,10},{10,8},{12,14},{14,12},{1,3},{3,1},... | collective-permute-start | bytes 417800 | tf_op jit(solution)/shard_map/ppermute | solution.py:28
  8.1 9.1 %collective-permute-start.1 = (bf16[272,256]{1,0:T(8,128)(2,1)S(1)}, bf16[272,256]{1,0:T(8,128)(2,1)S(1)}, u32[]{:S(2)}, u32[]{:S(2)}) collective-permute-start(bf16[272,256]{1,0:T(8,128)(2,1)S(1)} %normalise.1.noted.own), channel_id=1, source_target_pairs={{0,8},{2,10},{4,12},{6,14},{8,0},{10,2},{12,4},{14,6},{1,9},{3,11}... | collective-permute-start | bytes 417800 | tf_op jit(solution)/shard_map/ppermute | solution.py:28
  10.7 4.5 %collective-permute-start.4 = (bf16[16,256]{1,0:T(8,128)(2,1)S(1)}, bf16[16,256]{1,0:T(8,128)(2,1)S(1)}, u32[]{:S(2)}, u32[]{:S(2)}) collective-permute-start(bf16[16,256]{1,0:T(8,128)(2,1)S(1)} %choices.1.ask), channel_id=1, source_target_pairs={{0,6},{2,4},{4,2},{6,0},{8,14},{10,12},{12,10},{14,8},{1,7},{3,5},... | collective-permute-start | bytes 24584 | tf_op jit(solution)/shard_map/ppermute | solution.py:28
  11.1 0.8 %copy-start.2 = (bf16[256,128]{1,0:T(8,128)(2,1)S(1)}, bf16[256,128]{1,0:T(8,128)(2,1)}, u32[]{:S(2)}) copy-start(bf16[256,128]{1,0:T(8,128)(2,1)} %weight.1) | copy-start | bytes 196612
  17.2 6.7 %collective-permute-start.5 = (bf16[272,256]{1,0:T(8,128)(2,1)S(1)}, bf16[272,256]{1,0:T(8,128)(2,1)S(1)}, u32[]{:S(2)}, u32[]{:S(2)}) collective-permute-start(bf16[272,256]{1,0:T(8,128)(2,1)S(1)} %get-tuple-element.27), channel_id=1, source_target_pairs={{0,2},{2,0},{4,6},{6,4},{8,10},{10,8},{12,14},{14,12},{1,3},{3,1},... | collective-permute-start | bytes 417800 | tf_op jit(solution)/shard_map/ppermute | solution.py:28
  17.8 4.4 %collective-permute-start.6 = (bf16[144,256]{1,0:T(8,128)(2,1)S(1)}, bf16[144,256]{1,0:T(8,128)(2,1)S(1)}, u32[]{:S(2)}, u32[]{:S(2)}) collective-permute-start(bf16[144,256]{1,0:T(8,128)(2,1)S(1)} %get-tuple-element.28), channel_id=1, source_target_pairs={{0,4},{2,6},{4,0},{6,2},{8,12},{10,14},{12,8},{14,10},{1,5},{3,7},... | collective-permute-start | bytes 221192 | tf_op jit(solution)/shard_map/ppermute | solution.py:28
  18.1 5.8 %collective-permute-start.7 = (bf16[144,256]{1,0:T(8,128)(2,1)S(1)}, bf16[144,256]{1,0:T(8,128)(2,1)S(1)}, u32[]{:S(2)}, u32[]{:S(2)}) collective-permute-start(bf16[144,256]{1,0:T(8,128)(2,1)S(1)} %get-tuple-element.29), channel_id=1, source_target_pairs={{0,6},{2,4},{4,2},{6,0},{8,14},{10,12},{12,10},{14,8},{1,7},{3,5},... | collective-permute-start | bytes 221192 | tf_op jit(solution)/shard_map/ppermute | solution.py:28
  24.9 1.2 %collective-permute-start.8 = (f32[8,256]{1,0:T(8,128)S(1)}, f32[8,256]{1,0:T(8,128)S(1)}, u32[]{:S(2)}, u32[]{:S(2)}) collective-permute-start(f32[8,256]{1,0:T(8,128)S(1)} %get-tuple-element.33.part), channel_id=1, source_target_pairs={{0,1},{1,0},{2,3},{3,2},{4,5},{5,4},{6,7},{7,6},{8,9},{9,8},{10,11... | collective-permute-start | bytes 24584 | tf_op jit(solution)/shard_map/ppermute | solution.py:24
  27.4 9.1 %collective-permute-start.9 = (bf16[128,256]{1,0:T(8,128)(2,1)S(1)}, bf16[128,256]{1,0:T(8,128)(2,1)S(1)}, u32[]{:S(2)}, u32[]{:S(2)}) collective-permute-start(bf16[128,256]{1,0:T(8,128)(2,1)S(1)} %get-tuple-element.35), channel_id=1, source_target_pairs={{0,14},{2,12},{4,10},{6,8},{8,6},{10,4},{12,2},{14,0},{1,15},{3,13... | collective-permute-start | bytes 196616 | tf_op jit(solution)/shard_map/ppermute | solution.py:28
  30.0 6.9 %collective-permute-start.10 = (bf16[128,256]{1,0:T(8,128)(2,1)S(1)}, bf16[128,256]{1,0:T(8,128)(2,1)S(1)}, u32[]{:S(2)}, u32[]{:S(2)}) collective-permute-start(bf16[128,256]{1,0:T(8,128)(2,1)S(1)} %get-tuple-element.36), channel_id=1, source_target_pairs={{0,6},{2,4},{4,2},{6,0},{8,14},{10,12},{12,10},{14,8},{1,7},{3,5},... | collective-permute-start | bytes 196616 | tf_op jit(solution)/shard_map/ppermute | solution.py:28
  31.1 7.6 %collective-permute-start.11 = (bf16[128,256]{1,0:T(8,128)(2,1)S(1)}, bf16[128,256]{1,0:T(8,128)(2,1)S(1)}, u32[]{:S(2)}, u32[]{:S(2)}) collective-permute-start(bf16[128,256]{1,0:T(8,128)(2,1)S(1)} %get-tuple-element.37), channel_id=1, source_target_pairs={{0,12},{2,14},{4,8},{6,10},{8,4},{10,6},{12,0},{14,2},{1,13},{3,15... | collective-permute-start | bytes 196616 | tf_op jit(solution)/shard_map/ppermute | solution.py:28
  32.4 6.3 %collective-permute-start.12 = (bf16[128,256]{1,0:T(8,128)(2,1)S(1)}, bf16[128,256]{1,0:T(8,128)(2,1)S(1)}, u32[]{:S(2)}, u32[]{:S(2)}) collective-permute-start(bf16[128,256]{1,0:T(8,128)(2,1)S(1)} %get-tuple-element.38), channel_id=1, source_target_pairs={{0,4},{2,6},{4,0},{6,2},{8,12},{10,14},{12,8},{14,10},{1,5},{3,7},... | collective-permute-start | bytes 196616 | tf_op jit(solution)/shard_map/ppermute | solution.py:28
  33.3 9.4 %collective-permute-start.13 = (bf16[128,256]{1,0:T(8,128)(2,1)S(1)}, bf16[128,256]{1,0:T(8,128)(2,1)S(1)}, u32[]{:S(2)}, u32[]{:S(2)}) collective-permute-start(bf16[128,256]{1,0:T(8,128)(2,1)S(1)} %get-tuple-element.39), channel_id=1, source_target_pairs={{0,10},{2,8},{4,14},{6,12},{8,2},{10,0},{12,6},{14,4},{1,11},{3,9}... | collective-permute-start | bytes 196616 | tf_op jit(solution)/shard_map/ppermute | solution.py:28
  36.4 6.2 %collective-permute-start.14 = (bf16[128,256]{1,0:T(8,128)(2,1)S(1)}, bf16[128,256]{1,0:T(8,128)(2,1)S(1)}, u32[]{:S(2)}, u32[]{:S(2)}) collective-permute-start(bf16[128,256]{1,0:T(8,128)(2,1)S(1)} %get-tuple-element.40), channel_id=1, source_target_pairs={{0,2},{2,0},{4,6},{6,4},{8,10},{10,8},{12,14},{14,12},{1,3},{3,1},... | collective-permute-start | bytes 196616 | tf_op jit(solution)/shard_map/ppermute | solution.py:28
  37.0 6.0 %collective-permute-start.15 = (bf16[128,256]{1,0:T(8,128)(2,1)S(1)}, bf16[128,256]{1,0:T(8,128)(2,1)S(1)}, u32[]{:S(2)}, u32[]{:S(2)}) collective-permute-start(bf16[128,256]{1,0:T(8,128)(2,1)S(1)} %get-tuple-element.41), channel_id=1, source_target_pairs={{0,8},{2,10},{4,12},{6,14},{8,0},{10,2},{12,4},{14,6},{1,9},{3,11}... | collective-permute-start | bytes 196616 | tf_op jit(solution)/shard_map/ppermute | solution.py:28
  44.1 1.2 %collective-permute-start.16 = (f32[8,256]{1,0:T(8,128)S(1)}, f32[8,256]{1,0:T(8,128)S(1)}, u32[]{:S(2)}, u32[]{:S(2)}) collective-permute-start(f32[8,256]{1,0:T(8,128)S(1)} %get-tuple-element.44.part), channel_id=1, source_target_pairs={{0,1},{1,0},{2,3},{3,2},{4,5},{5,4},{6,7},{7,6},{8,9},{9,8},{10,11... | collective-permute-start | bytes 24584 | tf_op jit(solution)/shard_map/ppermute | solution.py:24

commit v4 on v3

v4 whole, which is shorter than its diff:
```python
import functools
import math

import jax
import jax.numpy as jnp
from jax import lax
from jax.experimental import pallas as pl
from jax.experimental.pallas import tpu as pltpu
from jax.sharding import PartitionSpec as P

NGC = 8
RBLK = 128
LANE = 128
CHUNK = 32
GROUP = 8

LOG_PRIOR = (-4.6051702, -3.2188758, -0.1625189, -2.8134107, -3.5065579, -4.6051702)

F32 = jnp.float32
BF16 = jnp.bfloat16
EXACT = lax.Precision.HIGHEST


def swap_tgt(value):
    return lax.ppermute(value, "tgt", [(0, 1), (1, 0)])


def send(value, step, count):
    return lax.ppermute(value, "samp", [(i, i ^ step) for i in range(count)])


def call(body, name, outs, *args, scratch=(), cost=1):
    return pl.pallas_call(
        body,
        out_shape=[jax.ShapeDtypeStruct(shape, dtype) for shape, dtype in outs],
        in_specs=[pl.BlockSpec(memory_space=pltpu.VMEM)] * len(args),
        out_specs=[pl.BlockSpec(memory_space=pltpu.VMEM)] * len(outs),
        scratch_shapes=list(scratch),
        compiler_params=pltpu.CompilerParams(vmem_limit_bytes=16 * 2**20),
        cost_estimate=pl.CostEstimate(flops=cost, bytes_accessed=cost, transcendentals=0),
        name=name,
    )(*args)


def dot(left, right, left_dim, right_dim, precision=None):
    return lax.dot_general(
        left,
        right,
        (((left_dim,), (right_dim,)), ((), ())),
        precision=precision,
        preferred_element_type=F32,
    )


def pick(ref, ask, parts):
    chosen = ref[0:RBLK]
    for part in range(1, parts):
        chosen = jnp.where(ask == part, ref[part * RBLK : (part + 1) * RBLK], chosen)
    return chosen


def ask_kernel(rows, neighbours, ask):
    index = neighbours[...]
    position = lax.div(index, rows) ^ lax.axis_index("samp")
    block = lax.div(lax.rem(index, rows), RBLK)
    count = lax.axis_size("samp")
    best = [
        jnp.max(jnp.where(position == p, block, 0), axis=0, keepdims=True) for p in range(count)
    ]
    best += [jnp.zeros_like(best[0])] * (ask.shape[0] - count)
    best = jnp.max(jnp.concatenate(best, axis=0), axis=1, keepdims=True)
    ask[...] = jnp.broadcast_to(best.astype(F32), ask.shape).astype(BF16)


def map_kernel(neighbours, weight, plf, noted, out, total, wide):
    rows = neighbours.shape[0]
    listed = neighbours.shape[1]
    count = lax.axis_size("samp")
    me = lax.axis_index("samp")
    sample = lax.broadcasted_iota(jnp.int32, (RBLK, listed), 0).astype(F32).astype(BF16)
    device = lax.broadcasted_iota(jnp.int32, (count, listed), 0)
    one, zero = jnp.ones((), BF16), jnp.zeros((), BF16)

    def step(i, carry):
        start = pl.multiple_of(i * GROUP, GROUP)
        index = neighbours[pl.ds(start, GROUP), :]
        heavy = weight[pl.ds(start, GROUP), :].astype(F32)
        position = lax.div(index, rows) ^ me
        low = lax.rem(index, RBLK).astype(F32).astype(BF16)
        for r in range(0, GROUP, 2):
            low_one = jnp.concatenate(
                [jnp.where(sample == low[q : q + 1], one, zero) for q in (r, r + 1)], axis=1
            )
            high = [
                jnp.where(device == position[q : q + 1], heavy[q : q + 1], 0.0) for q in (r, r + 1)
            ]
            none = jnp.zeros_like(high[0])
            high_one = jnp.concatenate(
                [jnp.concatenate([high[0], none], axis=1), jnp.concatenate([none, high[1]], axis=1)],
                axis=0,
            ).astype(BF16)
            both = dot(high_one, low_one, 1, 1)
            wide[:, pl.ds(start + r, 1), :] = both[:count].reshape(count, 1, RBLK)
            wide[:, pl.ds(start + r + 1, 1), :] = both[count:].reshape(count, 1, RBLK)
        return carry

    lax.fori_loop(0, rows // GROUP, step, 0, unroll=8)
    for p in range(count):
        out[:, p * RBLK : (p + 1) * RBLK] = wide[p].astype(BF16)
    summed = jnp.sum(weight[...].astype(F32), axis=1, keepdims=True)
    total[...] = jnp.broadcast_to(summed, total.shape)


def stats_kernel(coverage, onehot, stats):
    rows = coverage.shape[0]
    stats[:, 0:rows] = dot(onehot[...].astype(BF16), coverage[...], 1, 1)
    number = jnp.sum(onehot[...], axis=1, keepdims=True)
    stats[:, rows:] = jnp.broadcast_to(number, (NGC, LANE))


def norm_kernel(coverage, mine, theirs, onehot, ask, noted, wide):
    rows, cols = coverage.shape
    extra = ask.shape[0]
    sums = mine[:, 0:rows] + theirs[:, 0:rows]
    number = mine[:, rows : rows + 1] + theirs[:, rows : rows + 1]
    mean = jnp.sum(sums, axis=0, keepdims=True) / (cols * lax.axis_size("tgt"))
    scale = mean / (sums / jnp.maximum(number, 1.0))
    scale = dot(jnp.where(sums > 0, scale, 0.0), onehot[...], 0, 0, EXACT)
    block = (coverage[...].astype(F32) * scale).astype(BF16)
    for out in (noted, wide):
        out[0:rows] = block
        out[rows : rows + extra] = ask[...]
    wide[rows + extra :] = ask[...]


def pass_kernel(late, asked, total, own, across, *refs):
    mates = len(refs) // 2
    half = mates + 1
    noted, out = refs[:mates], refs[mates:]
    rows = own.shape[0] - asked
    parts = rows // RBLK
    for k in range(1, half):
        note = noted[k - 1]
        base = note.shape[0] - asked
        other = base + (k ^ half)
        out[k - 1][0:RBLK] = pick(across, note[other : other + 1], parts)
        if k in late:
            out[k - 1][RBLK : 2 * RBLK] = pick(own, note[base + k : base + k + 1], parts)
        out[k - 1][out[k - 1].shape[0] - asked :] = across[rows : rows + asked]


def spread(first, second, third, normf, ratio, rel, own_sum, part):
    inverse = 1.0 / second
    scaled = first * inverse
    ratio[...] = normf * scaled
    relative = (third * inverse) * scaled - 1.0
    rel[...] = relative
    own_sum[...] = jnp.broadcast_to(jnp.sum(relative, axis=1, keepdims=True), own_sum.shape)
    for start in range(0, own_sum.shape[0], LANE):
        block = jnp.where(diagonal(), own_sum[start : start + LANE], 0.0)
        part[:, start : start + LANE] = jnp.sum(block, axis=0, keepdims=True)


def diagonal():
    row = lax.broadcasted_iota(jnp.int32, (LANE, LANE), 0)
    return row == lax.broadcasted_iota(jnp.int32, (LANE, LANE), 1)


def squared(block):
    wide = block.astype(F32)
    return (wide * wide).astype(BF16)


def columns(weight, positions):
    return jnp.concatenate([weight[:, p * RBLK : (p + 1) * RBLK] for p in positions], axis=1)


def place(table, positions):
    return jnp.concatenate([table[p * RBLK : (p + 1) * RBLK] for p in positions], axis=0)


def early_one_kernel(early, rows, weight, own, across, ask, *refs):
    noted, (table, partial) = refs[:-2], refs[-2:]
    parts = rows // RBLK
    half = len(noted) + 1
    for p in early:
        source = own if p == 0 else across if p == half else noted[p - 1]
        table[p * RBLK : (p + 1) * RBLK] = pick(source, ask[p : p + 1], parts)
    mine, block = columns(weight, early), place(table, early)
    partial[0] = dot(mine, block, 1, 0)
    partial[1] = dot(mine, squared(block), 1, 0)


def first_kernel(late, rows, weight, total, own, early, partial, *refs):
    mates = len(refs) - 5
    half = mates + 1
    passed, (table, ratio, rel, own_sum, part) = refs[:mates], refs[mates:]
    cols = own.shape[1]
    table[...] = early[...]
    arrived = []
    for k in range(1, half):
        if k in late:
            arrived.append(k)
            table[k * RBLK : (k + 1) * RBLK] = passed[k - 1][RBLK : 2 * RBLK]
        other = k ^ half
        arrived.append(other)
        table[other * RBLK : (other + 1) * RBLK] = passed[k - 1][0:RBLK]
    mine, block = columns(weight, arrived), place(table, arrived)
    second = partial[0] + dot(mine, block, 1, 0)
    third = partial[1] + dot(mine, squared(block), 1, 0)
    first = jnp.concatenate([total[...]] * (cols // LANE), axis=1)
    spread(first, second, third, own[0:rows].astype(F32), ratio, rel, own_sum, part)


def gated(weight, table, gates, positions):
    mine, block = columns(weight, positions), place(table, positions)
    wide = gates.astype(F32)
    covs = (wide * block.astype(F32)).astype(BF16)
    squares = (wide * squared(block).astype(F32)).astype(BF16)
    return [dot(mine, values, 1, 0) for values in (gates, covs, squares)]


def early_two_kernel(early, weight, table, gate, ask, *refs):
    arrived, partial = refs[:-1], refs[-1]
    own = pick(gate, ask[0:1], gate.shape[0] // RBLK)
    gates = jnp.concatenate([own] + [ref[...] for ref in arrived], axis=0)
    for i, moment in enumerate(gated(weight, table, gates, [0] + early)):
        partial[i] = moment


def second_kernel(late, rows, weight, table, own, partial, *refs):
    arrived, (ratio, rel, own_sum, part) = refs[:-4], refs[-4:]
    gates = jnp.concatenate([ref[...] for ref in arrived], axis=0)
    moments = gated(weight, table, gates, late)
    first, second, third = [partial[i] + moment for i, moment in enumerate(moments)]
    spread(first, second, third, own[0:rows].astype(F32), ratio, rel, own_sum, part)


def called(ratio, rel, own_sum, theirs, inverse, finish):
    rows, cols = ratio.shape
    share = 0.5 / (cols * lax.axis_size("tgt"))
    root_half = math.sqrt(0.5 * math.log2(math.e))
    for begin in range(0, rows, LANE):
        row = jnp.broadcast_to(theirs[:, begin : begin + LANE], (LANE, LANE))
        column = jnp.sum(jnp.where(diagonal(), row, 0.0), axis=1, keepdims=True)
        shared = (own_sum[begin : begin + LANE] + column) * share
        for start in range(0, LANE, CHUNK):
            here = slice(begin + start, begin + start + CHUNK)
            spot = shared[start : start + CHUNK]
            by_ploidy = inverse[here]
            centres = [max(state, 0.1) * by_ploidy for state in range(6)]
            widths = [jnp.maximum(centre, 0.25) for centre in centres]
            centres = [centre * root_half for centre in centres]
            for lane in range(0, cols, LANE):
                there = slice(lane, lane + LANE)
                level = 0.5 * rel[here, there] + spot
                copies = ratio[here, there] * root_half
                scores, roots = [], []
                for prior, centre, width in zip(LOG_PRIOR, centres, widths):
                    root = lax.rsqrt(level * width + 0.01)
                    delta = (copies - centre) * root
                    scores.append(prior * math.log2(math.e) - delta * delta)
                    roots.append(root)
                peak = functools.reduce(jnp.maximum, scores)
                expo = [jnp.exp2(s - peak) * root for s, root in zip(scores, roots)]
                tail = top = expo[5]
                for state in range(4, 0, -1):
                    tail = tail + expo[state]
                    top = top + tail
                finish(here, there, top / (tail + expo[0]))


def gate_kernel(asked, ratio, rel, own_sum, theirs, inverse, plf, across, *refs):
    rows = ratio.shape[0]
    mates = (len(refs) - 2) // 4
    half = mates + 1
    noted, passed, gate, out = refs[:mates], refs[mates : 2 * mates], refs[2 * mates], refs[2 * mates + 1 :]

    def finish(here, there, value):
        offset = value - plf[here]
        gate[here, there] = (1.0 / (1.0 + 4.0 * (offset * offset))).astype(BF16)

    called(ratio, rel, own_sum, theirs, inverse, finish)
    for p in range(1, 2 * half):
        if p < half:
            source = noted[p - 1]
        elif p == half:
            source = across
        else:
            source = passed[(p ^ half) - 1]
        place = source.shape[0] - asked + p
        out[p - 1][...] = pick(gate, source[place : place + 1], rows // RBLK)


def final_kernel(ratio, rel, own_sum, theirs, inverse, out):
    def finish(here, there, value):
        out[here, there] = value

    called(ratio, rel, own_sum, theirs, inverse, finish)


def body(coverage, neighbours, nbr_weight, ploidy, gc_bin):
    count = lax.axis_size("samp")
    half = count // 2
    mates = range(1, half)
    rows, cols = coverage.shape
    extra = -(-count // 16) * 16
    late = [3] if half > 3 else []
    bins = lax.broadcasted_iota(jnp.int32, (NGC, cols), 0)
    onehot = (bins == gc_bin[None, :]).astype(F32)
    plf = jnp.broadcast_to(ploidy.astype(F32)[:, None], (rows, LANE))
    inverse = 1.0 / plf

    (mine,) = call(stats_kernel, "bin_sums", [((NGC, rows + LANE), F32)], coverage, onehot)
    theirs = swap_tgt(mine)
    (ask,) = call(
        functools.partial(ask_kernel, rows), "choices", [((extra, cols), BF16)], neighbours
    )
    own, wide = call(
        norm_kernel, "normalise",
        [((rows + extra, cols), BF16), ((rows + 2 * extra, cols), BF16)],
        coverage, mine, theirs, onehot, ask,
    )
    across = send(wide, half, count)
    noted = [send(ask if k in late else own, k, count) for k in mates]
    weight, total = call(
        map_kernel, "weight_map", [((rows, count * RBLK), BF16), ((rows, LANE), F32)],
        neighbours, nbr_weight, plf, own, scratch=[pltpu.VMEM((count, rows, RBLK), F32)],
    )
    passed = call(
        functools.partial(pass_kernel, late, extra), "pass_on",
        [(((2 if k in late else 1) * RBLK + extra, cols), BF16) for k in mates],
        total, own, across, *noted,
    )
    passed = [send(block, k, count) for k, block in zip(mates, passed)]
    spreads = [((rows, cols), F32), ((rows, cols), F32), ((rows, LANE), F32), ((1, rows), F32)]
    early = [0] + [k for k in mates if k not in late] + [half]
    table, partial = call(
        functools.partial(early_one_kernel, early, rows), "early_moments_one",
        [((count * RBLK, cols), BF16), ((2, rows, cols), F32)],
        weight, own, across, ask, *noted,
    )
    table, ratio, rel, own_sum, part = call(
        functools.partial(first_kernel, late, rows), "moments_one",
        [((count * RBLK, cols), BF16)] + spreads,
        weight, total, own, table, partial, *passed,
    )
    gate, *gates = call(
        functools.partial(gate_kernel, extra), "gate",
        [((rows, cols), BF16)] + [((RBLK, cols), BF16)] * (count - 1),
        ratio, rel, own_sum, swap_tgt(part), inverse, plf, across, *noted, *passed,
    )
    order = [half + i for i in (0, 2, 1) if i < half] + list(range(half + 3, count))
    order += list(range(half - 1, 0, -1))
    gates = [send(gates[p - 1], p, count) for p in order]
    last = 1
    (partial,) = call(
        functools.partial(early_two_kernel, order[:-last]), "early_moments_two",
        [((3, rows, cols), F32)], weight, table, gate, ask, *gates[:-last],
    )
    ratio, rel, own_sum, part = call(
        functools.partial(second_kernel, order[-last:], rows), "moments_two", spreads,
        weight, table, own, partial, *gates[-last:],
    )
    (out,) = call(
        final_kernel, "copy_number", [((rows, cols), F32)],
        ratio, rel, own_sum, swap_tgt(part), inverse,
    )
    return out


def solution(mesh):
    in_specs = (
        P("samp", ("slab", "tgt")),
        P("samp", None),
        P("samp", None),
        P("samp"),
        P(("slab", "tgt")),
    )
    out_specs = P("samp", ("slab", "tgt"))
    return jax.shard_map(body, mesh=mesh, in_specs=in_specs, out_specs=out_specs, check_vma=False)
```

time: 47.3 us -> 45.4 us (0.960)
  Pallas kernels: 9.16 us -> 8.4 us
  other arithmetic: 0.01 us -> 0.73 us
  waiting for transfers between devices: 12.6 us -> 11.9 us
  local copies, waits for them, and re-layouts: 2.46 us -> 1.83 us
  starting transfers between devices: 22.9 us -> 22.3 us
    pallas_call x9 -> x11, Pallas kernels: 9.16 us -> 8.4 us  [call(): pl.pallas_call(body, out_shape=[jax.ShapeDtypeStruct(shape, dtype) for sh...]
    ppermute x14, starting transfers between devices: 22.4 us -> 21.6 us  [send(): return lax.ppermute(value, 'samp', [(i, i ^ step) for i in range(count)])]
    convert_element_type x0 -> x1, other arithmetic: none -> 0.72 us  [body(): onehot = (bins == gc_bin[None, :]).astype(F32)]
    unnamed x10 -> x8, local copies, waits for them, and re-layouts: 2.37 us -> 1.66 us
    ppermute x14, waiting for transfers between devices: 9.72 us -> 9.17 us  [send(): return lax.ppermute(value, 'samp', [(i, i ^ step) for i in range(count)])]
  transfers between devices with their start and end apart: 17 -> 17, of which waited for: 9 -> 10; matrix products, arithmetic and copies ran while one was open for 0% -> 0% of each run, Pallas kernels for 7% -> 9%
where the time goes in v4:
time: 45.4 us; the launch traced here: 45.2 us
  starting transfers between devices  22.3 us (49%)
  waiting for transfers between devices  11.9 us (26%)
  Pallas kernels  8.4 us (19%)
  local copies, waits for them, and re-layouts  1.83 us (4%)
  other arithmetic  0.73 us (2%)
    ppermute x14, starting transfers between devices, send(): return lax.ppermute(value, 'samp', [(i, i ^ step) for i in range(count)])  21.6 us
    ppermute x14, waiting for transfers between devices, send(): return lax.ppermute(value, 'samp', [(i, i ^ step) for i in range(count)])  9.17 us
    pallas_call x11, Pallas kernels, call(): pl.pallas_call(body, out_shape=[jax.ShapeDtypeStruct(shape, dtype) for sh...  8.4 us
    ppermute x3, waiting for transfers between devices, swap_tgt(): return lax.ppermute(value, 'tgt', [(0, 1), (1, 0)])  2.69 us
    unnamed x8, local copies, waits for them, and re-layouts  1.66 us
  transfers between devices with their start and end apart: 17, of which 10 were waited for; matrix products, arithmetic and copies ran while one was open for 0% of the time, Pallas kernels for 9%

profile of v4, /device:TPU:0, one launch (start us, length us, event | category | flops | bytes accessed | tf_op | source)
XLA Modules:
  0.0 45.2 jit_solution(17670974044362251367)
XLA Ops:
  0.0 0.7 %fusion.onehot = f32[8,256]{1,0:T(8,128)S(1)} fusion(s32[256]{0:T(256)} %param.9), kind=kLoop, calls=%fused_computation.1 | loop fusion | flops 4096 | bytes 9216 | tf_op jit(solution)/shard_map/convert_element_type | solution.py:310
  0.7 0.9 %copy-done.1 = bf16[256,256]{1,0:T(8,128)(2,1)S(1)} copy-done((bf16[256,256]{1,0:T(8,128)(2,1)S(1)}, bf16[256,256]{1,0:T(8,128)(2,1)}, u32[]{:S(2)}) %copy-start.1) | copy-done | bytes 131096
  3.6 4.0 %collective-permute-start.1 = (bf16[288,256]{1,0:T(8,128)(2,1)S(1)}, bf16[288,256]{1,0:T(8,128)(2,1)S(1)}, u32[]{:S(2)}, u32[]{:S(2)}) collective-permute-start(bf16[288,256]{1,0:T(8,128)(2,1)S(1)} %get-tuple-element.34), channel_id=1, source_target_pairs={{0,8},{2,10},{4,12},{6,14},{8,0},{10,2},{12,4},{14,6},{1,9},{3,11}... | collective-permute-start | bytes 442376 | tf_op jit(solution)/shard_map/ppermute | solution.py:29
  7.6 1.5 %collective-permute-start.2 = (bf16[272,256]{1,0:T(8,128)(2,1)S(1)}, bf16[272,256]{1,0:T(8,128)(2,1)S(1)}, u32[]{:S(2)}, u32[]{:S(2)}) collective-permute-start(bf16[272,256]{1,0:T(8,128)(2,1)S(1)} %get-tuple-element.31.noted.own), channel_id=1, source_target_pairs={{0,2},{2,0},{4,6},{6,4},{8,10},{10,8},{12,14},{14,12},{1,3},{3,1},... | collective-permute-start | bytes 417800 | tf_op jit(solution)/shard_map/ppermute | solution.py:29
  9.1 1.6 %collective-permute-start.3 = (bf16[272,256]{1,0:T(8,128)(2,1)S(1)}, bf16[272,256]{1,0:T(8,128)(2,1)S(1)}, u32[]{:S(2)}, u32[]{:S(2)}) collective-permute-start(bf16[272,256]{1,0:T(8,128)(2,1)S(1)} %get-tuple-element.31.noted.own), channel_id=1, source_target_pairs={{0,4},{2,6},{4,0},{6,2},{8,12},{10,14},{12,8},{14,10},{1,5},{3,7},... | collective-permute-start | bytes 417800 | tf_op jit(solution)/shard_map/ppermute | solution.py:29
  11.2 0.7 %copy-done.2 = bf16[256,128]{1,0:T(8,128)(2,1)S(1)} copy-done((bf16[256,128]{1,0:T(8,128)(2,1)S(1)}, bf16[256,128]{1,0:T(8,128)(2,1)}, u32[]{:S(2)}) %copy-start.2) | copy-done | bytes 65560
  11.9 2.9 %weight_map.1 = (bf16[256,1024]{1,0:T(8,128)(2,1)S(1)}, f32[256,128]{1,0:T(8,128)S(1)}) custom-call(s32[256,128]{1,0:T(8,128)S(1)} %copy-done, bf16[256,128]{1,0:T(8,128)(2,1)S(1)} %copy-done.2, f32[256,128]{1,0:T(8,128)S(1)} %broadcast_in_dim.4.plf, bf16[272,256]{1,0:T(8,128)(2,1)S(1)} %get-tuple-element.31.noted.own), custom_call_target="tpu_custom_call" | custom-call | flops 1 | bytes 1 | tf_op jit(solution)/shard_map/weight_map/pallas_call | solution.py:33
  14.8 1.6 %collective-permute-done.4.refs_2_ = bf16[16,256]{1,0:T(8,128)(2,1)S(1)} collective-permute-done((bf16[16,256]{1,0:T(8,128)(2,1)S(1)}, bf16[16,256]{1,0:T(8,128)(2,1)S(1)}, u32[]{:S(2)}, u32[]{:S(2)}) %collective-permute-start.4) | collective-permute-done | bytes 8224 | tf_op jit(solution)/shard_map/ppermute | solution.py:29
  16.5 1.2 %collective-permute-start.7 = (bf16[272,256]{1,0:T(8,128)(2,1)S(1)}, bf16[272,256]{1,0:T(8,128)(2,1)S(1)}, u32[]{:S(2)}, u32[]{:S(2)}) collective-permute-start(bf16[272,256]{1,0:T(8,128)(2,1)S(1)} %get-tuple-element.39), channel_id=1, source_target_pairs={{0,6},{2,4},{4,2},{6,0},{8,14},{10,12},{12,10},{14,8},{1,7},{3,5},... | collective-permute-start | bytes 417800 | tf_op jit(solution)/shard_map/ppermute | solution.py:29
  17.7 1.5 %collective-permute-start.5 = (bf16[144,256]{1,0:T(8,128)(2,1)S(1)}, bf16[144,256]{1,0:T(8,128)(2,1)S(1)}, u32[]{:S(2)}, u32[]{:S(2)}) collective-permute-start(bf16[144,256]{1,0:T(8,128)(2,1)S(1)} %get-tuple-element.37), channel_id=1, source_target_pairs={{0,2},{2,0},{4,6},{6,4},{8,10},{10,8},{12,14},{14,12},{1,3},{3,1},... | collective-permute-start | bytes 221192 | tf_op jit(solution)/shard_map/ppermute | solution.py:29
  19.3 0.8 %collective-permute-start.6 = (bf16[144,256]{1,0:T(8,128)(2,1)S(1)}, bf16[144,256]{1,0:T(8,128)(2,1)S(1)}, u32[]{:S(2)}, u32[]{:S(2)}) collective-permute-start(bf16[144,256]{1,0:T(8,128)(2,1)S(1)} %get-tuple-element.38), channel_id=1, source_target_pairs={{0,4},{2,6},{4,0},{6,2},{8,12},{10,14},{12,8},{14,10},{1,5},{3,7},... | collective-permute-start | bytes 221192 | tf_op jit(solution)/shard_map/ppermute | solution.py:29
  20.4 3.0 %collective-permute-done.5.refs_0_.refs_3_ = bf16[144,256]{1,0:T(8,128)(2,1)S(1)} collective-permute-done((bf16[144,256]{1,0:T(8,128)(2,1)S(1)}, bf16[144,256]{1,0:T(8,128)(2,1)S(1)}, u32[]{:S(2)}, u32[]{:S(2)}) %collective-permute-start.5) | collective-permute-done | bytes 73760 | tf_op jit(solution)/shard_map/ppermute | solution.py:29
  24.1 1.1 %collective-permute-done.8.theirs = f32[1,256]{1,0:T(1,128)S(1)} collective-permute-done((f32[1,256]{1,0:T(1,128)S(1)}, f32[1,256]{1,0:T(1,128)S(1)}, u32[]{:S(2)}, u32[]{:S(2)}) %collective-permute-start.8) | collective-permute-done | bytes 1056 | tf_op jit(solution)/shard_map/ppermute | solution.py:25
  25.4 1.0 %gate.1 = (bf16[256,256]{1,0:T(8,128)(2,1)S(1)}, bf16[128,256]{1,0:T(8,128)(2,1)S(1)}, bf16[128,256]{1,0:T(8,128)(2,1)S(1)}, bf16[128,256]{1,0:T(8,128)(2,1)S(1)...) custom-call(f32[256,256]{1,0:T(8,128)S(1)} %get-tuple-element.41.rat, ...), custom_call_target="tpu_custom_call" | custom-call | flops 1 | bytes 1 | tf_op jit(solution)/shard_map/gate/pallas_call | solution.py:33
  26.4 3.2 %collective-permute-start.10 = (bf16[128,256]{1,0:T(8,128)(2,1)S(1)}, bf16[128,256]{1,0:T(8,128)(2,1)S(1)}, u32[]{:S(2)}, u32[]{:S(2)}) collective-permute-start(bf16[128,256]{1,0:T(8,128)(2,1)S(1)} %get-tuple-element.47), channel_id=1, source_target_pairs={{0,12},{2,14},{4,8},{6,10},{8,4},{10,6},{12,0},{14,2},{1,13},{3,15... | collective-permute-start | bytes 196616 | tf_op jit(solution)/shard_map/ppermute | solution.py:29
  29.7 2.6 %collective-permute-start.12 = (bf16[128,256]{1,0:T(8,128)(2,1)S(1)}, bf16[128,256]{1,0:T(8,128)(2,1)S(1)}, u32[]{:S(2)}, u32[]{:S(2)}) collective-permute-start(bf16[128,256]{1,0:T(8,128)(2,1)S(1)} %get-tuple-element.49), channel_id=1, source_target_pairs={{0,14},{2,12},{4,10},{6,8},{8,6},{10,4},{12,2},{14,0},{1,15},{3,13... | collective-permute-start | bytes 196616 | tf_op jit(solution)/shard_map/ppermute | solution.py:29
  32.2 1.8 %collective-permute-start.13 = (bf16[128,256]{1,0:T(8,128)(2,1)S(1)}, bf16[128,256]{1,0:T(8,128)(2,1)S(1)}, u32[]{:S(2)}, u32[]{:S(2)}) collective-permute-start(bf16[128,256]{1,0:T(8,128)(2,1)S(1)} %get-tuple-element.50), channel_id=1, source_target_pairs={{0,6},{2,4},{4,2},{6,0},{8,14},{10,12},{12,10},{14,8},{1,7},{3,5},... | collective-permute-start | bytes 196616 | tf_op jit(solution)/shard_map/ppermute | solution.py:29
  34.1 1.0 %collective-permute-start.14 = (bf16[128,256]{1,0:T(8,128)(2,1)S(1)}, bf16[128,256]{1,0:T(8,128)(2,1)S(1)}, u32[]{:S(2)}, u32[]{:S(2)}) collective-permute-start(bf16[128,256]{1,0:T(8,128)(2,1)S(1)} %get-tuple-element.51), channel_id=1, source_target_pairs={{0,4},{2,6},{4,0},{6,2},{8,12},{10,14},{12,8},{14,10},{1,5},{3,7},... | collective-permute-start | bytes 196616 | tf_op jit(solution)/shard_map/ppermute | solution.py:29
  35.1 0.9 %collective-permute-start.9 = (bf16[128,256]{1,0:T(8,128)(2,1)S(1)}, bf16[128,256]{1,0:T(8,128)(2,1)S(1)}, u32[]{:S(2)}, u32[]{:S(2)}) collective-permute-start(bf16[128,256]{1,0:T(8,128)(2,1)S(1)} %get-tuple-element.46), channel_id=1, source_target_pairs={{0,8},{2,10},{4,12},{6,14},{8,0},{10,2},{12,4},{14,6},{1,9},{3,11}... | collective-permute-start | bytes 196616 | tf_op jit(solution)/shard_map/ppermute | solution.py:29
  35.9 1.7 %collective-permute-done.11.refs_2_ = bf16[128,256]{1,0:T(8,128)(2,1)S(1)} collective-permute-done((bf16[128,256]{1,0:T(8,128)(2,1)S(1)}, bf16[128,256]{1,0:T(8,128)(2,1)S(1)}, u32[]{:S(2)}, u32[]{:S(2)}) %collective-permute-start.11) | collective-permute-done | bytes 65568 | tf_op jit(solution)/shard_map/ppermute | solution.py:29
  37.6 1.1 %collective-permute-start.15 = (bf16[128,256]{1,0:T(8,128)(2,1)S(1)}, bf16[128,256]{1,0:T(8,128)(2,1)S(1)}, u32[]{:S(2)}, u32[]{:S(2)}) collective-permute-start(bf16[128,256]{1,0:T(8,128)(2,1)S(1)} %get-tuple-element.52), channel_id=1, source_target_pairs={{0,2},{2,0},{4,6},{6,4},{8,10},{10,8},{12,14},{14,12},{1,3},{3,1},... | collective-permute-start | bytes 196616 | tf_op jit(solution)/shard_map/ppermute | solution.py:29
  39.0 1.8 %collective-permute-done.14.refs_5_ = bf16[128,256]{1,0:T(8,128)(2,1)S(1)} collective-permute-done((bf16[128,256]{1,0:T(8,128)(2,1)S(1)}, bf16[128,256]{1,0:T(8,128)(2,1)S(1)}, u32[]{:S(2)}, u32[]{:S(2)}) %collective-permute-start.14) | collective-permute-done | bytes 65568 | tf_op jit(solution)/shard_map/ppermute | solution.py:29
  42.4 1.1 %collective-permute-done.16.theirs = f32[1,256]{1,0:T(1,128)S(1)} collective-permute-done((f32[1,256]{1,0:T(1,128)S(1)}, f32[1,256]{1,0:T(1,128)S(1)}, u32[]{:S(2)}, u32[]{:S(2)}) %collective-permute-start.16) | collective-permute-done | bytes 1056 | tf_op jit(solution)/shard_map/ppermute | solution.py:25
  43.5 1.7 %copy_number.1 = f32[256,256]{1,0:T(8,128)} custom-call(f32[256,256]{1,0:T(8,128)S(1)} %get-tuple-element.53.ratio, f32[256,256]{1,0:T(8,128)S(1)} %get-tuple-element.54.rel, f32[256,128]{1,0:T(8,128)S(1)} %get-tuple-element.55.own_sum, f32[1,256]{1,0:T(1,128)S(1)} %collective-permute-done.16.theirs, f32[256,128]{1,0:T(8,128)S(1)} %broadcast_in_dim.10.inverse), custom_call_target="tpu_custom_call" | custom-call | flops 1 | bytes 1 | tf_op jit(solution)/shard_map/copy_number/pallas_call | solution.py:33
  (34 shorter events, 5.6 us)
Async XLA Ops:
  0.0 2.3 %copy-start = (s32[256,128]{1,0:T(8,128)S(1)}, s32[256,128]{1,0:T(8,128)}, u32[]{:S(2)}) copy-start(s32[256,128]{1,0:T(8,128)} %neighbours.3) | copy-start | bytes 393220
  0.7 0.9 %copy-start.1 = (bf16[256,256]{1,0:T(8,128)(2,1)S(1)}, bf16[256,256]{1,0:T(8,128)(2,1)}, u32[]{:S(2)}) copy-start(bf16[256,256]{1,0:T(8,128)(2,1)} %coverage.3) | copy-start | bytes 393220
  1.8 1.3 %collective-permute-start = (f32[8,384]{1,0:T(8,128)S(1)}, f32[8,384]{1,0:T(8,128)S(1)}, u32[]{:S(2)}, u32[]{:S(2)}) collective-permute-start(f32[8,384]{1,0:T(8,128)S(1)} %bin_sums.1.mine), channel_id=1, source_target_pairs={{0,1},{1,0},{2,3},{3,2},{4,5},{5,4},{6,7},{7,6},{8,9},{9,8},{10,11... | collective-permute-start | bytes 36872 | tf_op jit(solution)/shard_map/ppermute | solution.py:25
  3.6 7.5 %copy-start.3 = (s32[256]{0:T(256)S(1)}, s32[256]{0:T(256)}, u32[]{:S(2)}) copy-start(s32[256]{0:T(256)} %param.8) | copy-start | bytes 3076
  3.6 12.9 %collective-permute-start.1 = (bf16[288,256]{1,0:T(8,128)(2,1)S(1)}, bf16[288,256]{1,0:T(8,128)(2,1)S(1)}, u32[]{:S(2)}, u32[]{:S(2)}) collective-permute-start(bf16[288,256]{1,0:T(8,128)(2,1)S(1)} %get-tuple-element.34), channel_id=1, source_target_pairs={{0,8},{2,10},{4,12},{6,14},{8,0},{10,2},{12,4},{14,6},{1,9},{3,11}... | collective-permute-start | bytes 442376 | tf_op jit(solution)/shard_map/ppermute | solution.py:29
  7.6 8.9 %collective-permute-start.2 = (bf16[272,256]{1,0:T(8,128)(2,1)S(1)}, bf16[272,256]{1,0:T(8,128)(2,1)S(1)}, u32[]{:S(2)}, u32[]{:S(2)}) collective-permute-start(bf16[272,256]{1,0:T(8,128)(2,1)S(1)} %get-tuple-element.31.noted.own), channel_id=1, source_target_pairs={{0,2},{2,0},{4,6},{6,4},{8,10},{10,8},{12,14},{14,12},{1,3},{3,1},... | collective-permute-start | bytes 417800 | tf_op jit(solution)/shard_map/ppermute | solution.py:29
  9.1 7.4 %collective-permute-start.3 = (bf16[272,256]{1,0:T(8,128)(2,1)S(1)}, bf16[272,256]{1,0:T(8,128)(2,1)S(1)}, u32[]{:S(2)}, u32[]{:S(2)}) collective-permute-start(bf16[272,256]{1,0:T(8,128)(2,1)S(1)} %get-tuple-element.31.noted.own), channel_id=1, source_target_pairs={{0,4},{2,6},{4,0},{6,2},{8,12},{10,14},{12,8},{14,10},{1,5},{3,7},... | collective-permute-start | bytes 417800 | tf_op jit(solution)/shard_map/ppermute | solution.py:29
  10.7 5.8 %collective-permute-start.4 = (bf16[16,256]{1,0:T(8,128)(2,1)S(1)}, bf16[16,256]{1,0:T(8,128)(2,1)S(1)}, u32[]{:S(2)}, u32[]{:S(2)}) collective-permute-start(bf16[16,256]{1,0:T(8,128)(2,1)S(1)} %choices.1.ask), channel_id=1, source_target_pairs={{0,6},{2,4},{4,2},{6,0},{8,14},{10,12},{12,10},{14,8},{1,7},{3,5},... | collective-permute-start | bytes 24584 | tf_op jit(solution)/shard_map/ppermute | solution.py:29
  11.1 0.8 %copy-start.2 = (bf16[256,128]{1,0:T(8,128)(2,1)S(1)}, bf16[256,128]{1,0:T(8,128)(2,1)}, u32[]{:S(2)}) copy-start(bf16[256,128]{1,0:T(8,128)(2,1)} %weight.1) | copy-start | bytes 196612
  16.5 7.1 %collective-permute-start.7 = (bf16[272,256]{1,0:T(8,128)(2,1)S(1)}, bf16[272,256]{1,0:T(8,128)(2,1)S(1)}, u32[]{:S(2)}, u32[]{:S(2)}) collective-permute-start(bf16[272,256]{1,0:T(8,128)(2,1)S(1)} %get-tuple-element.39), channel_id=1, source_target_pairs={{0,6},{2,4},{4,2},{6,0},{8,14},{10,12},{12,10},{14,8},{1,7},{3,5},... | collective-permute-start | bytes 417800 | tf_op jit(solution)/shard_map/ppermute | solution.py:29
  17.7 5.7 %collective-permute-start.5 = (bf16[144,256]{1,0:T(8,128)(2,1)S(1)}, bf16[144,256]{1,0:T(8,128)(2,1)S(1)}, u32[]{:S(2)}, u32[]{:S(2)}) collective-permute-start(bf16[144,256]{1,0:T(8,128)(2,1)S(1)} %get-tuple-element.37), channel_id=1, source_target_pairs={{0,2},{2,0},{4,6},{6,4},{8,10},{10,8},{12,14},{14,12},{1,3},{3,1},... | collective-permute-start | bytes 221192 | tf_op jit(solution)/shard_map/ppermute | solution.py:29
  19.3 4.4 %collective-permute-start.6 = (bf16[144,256]{1,0:T(8,128)(2,1)S(1)}, bf16[144,256]{1,0:T(8,128)(2,1)S(1)}, u32[]{:S(2)}, u32[]{:S(2)}) collective-permute-start(bf16[144,256]{1,0:T(8,128)(2,1)S(1)} %get-tuple-element.38), channel_id=1, source_target_pairs={{0,4},{2,6},{4,0},{6,2},{8,12},{10,14},{12,8},{14,10},{1,5},{3,7},... | collective-permute-start | bytes 221192 | tf_op jit(solution)/shard_map/ppermute | solution.py:29
  24.1 1.2 %collective-permute-start.8 = (f32[1,256]{1,0:T(1,128)S(1)}, f32[1,256]{1,0:T(1,128)S(1)}, u32[]{:S(2)}, u32[]{:S(2)}) collective-permute-start(f32[1,256]{1,0:T(1,128)S(1)} %get-tuple-element.44), channel_id=1, source_target_pairs={{0,1},{1,0},{2,3},{3,2},{4,5},{5,4},{6,7},{7,6},{8,9},{9,8},{10,11... | collective-permute-start | bytes 3080 | tf_op jit(solution)/shard_map/ppermute | solution.py:25
  26.4 8.7 %collective-permute-start.10 = (bf16[128,256]{1,0:T(8,128)(2,1)S(1)}, bf16[128,256]{1,0:T(8,128)(2,1)S(1)}, u32[]{:S(2)}, u32[]{:S(2)}) collective-permute-start(bf16[128,256]{1,0:T(8,128)(2,1)S(1)} %get-tuple-element.47), channel_id=1, source_target_pairs={{0,12},{2,14},{4,8},{6,10},{8,4},{10,6},{12,0},{14,2},{1,13},{3,15... | collective-permute-start | bytes 196616 | tf_op jit(solution)/shard_map/ppermute | solution.py:29
  29.6 8.1 %collective-permute-start.11 = (bf16[128,256]{1,0:T(8,128)(2,1)S(1)}, bf16[128,256]{1,0:T(8,128)(2,1)S(1)}, u32[]{:S(2)}, u32[]{:S(2)}) collective-permute-start(bf16[128,256]{1,0:T(8,128)(2,1)S(1)} %get-tuple-element.48), channel_id=1, source_target_pairs={{0,10},{2,8},{4,14},{6,12},{8,2},{10,0},{12,6},{14,4},{1,11},{3,9}... | collective-permute-start | bytes 196616 | tf_op jit(solution)/shard_map/ppermute | solution.py:29
  29.7 9.1 %collective-permute-start.12 = (bf16[128,256]{1,0:T(8,128)(2,1)S(1)}, bf16[128,256]{1,0:T(8,128)(2,1)S(1)}, u32[]{:S(2)}, u32[]{:S(2)}) collective-permute-start(bf16[128,256]{1,0:T(8,128)(2,1)S(1)} %get-tuple-element.49), channel_id=1, source_target_pairs={{0,14},{2,12},{4,10},{6,8},{8,6},{10,4},{12,2},{14,0},{1,15},{3,13... | collective-permute-start | bytes 196616 | tf_op jit(solution)/shard_map/ppermute | solution.py:29
  32.2 6.8 %collective-permute-start.13 = (bf16[128,256]{1,0:T(8,128)(2,1)S(1)}, bf16[128,256]{1,0:T(8,128)(2,1)S(1)}, u32[]{:S(2)}, u32[]{:S(2)}) collective-permute-start(bf16[128,256]{1,0:T(8,128)(2,1)S(1)} %get-tuple-element.50), channel_id=1, source_target_pairs={{0,6},{2,4},{4,2},{6,0},{8,14},{10,12},{12,10},{14,8},{1,7},{3,5},... | collective-permute-start | bytes 196616 | tf_op jit(solution)/shard_map/ppermute | solution.py:29
  34.1 6.7 %collective-permute-start.14 = (bf16[128,256]{1,0:T(8,128)(2,1)S(1)}, bf16[128,256]{1,0:T(8,128)(2,1)S(1)}, u32[]{:S(2)}, u32[]{:S(2)}) collective-permute-start(bf16[128,256]{1,0:T(8,128)(2,1)S(1)} %get-tuple-element.51), channel_id=1, source_target_pairs={{0,4},{2,6},{4,0},{6,2},{8,12},{10,14},{12,8},{14,10},{1,5},{3,7},... | collective-permute-start | bytes 196616 | tf_op jit(solution)/shard_map/ppermute | solution.py:29
  35.1 6.2 %collective-permute-start.9 = (bf16[128,256]{1,0:T(8,128)(2,1)S(1)}, bf16[128,256]{1,0:T(8,128)(2,1)S(1)}, u32[]{:S(2)}, u32[]{:S(2)}) collective-permute-start(bf16[128,256]{1,0:T(8,128)(2,1)S(1)} %get-tuple-element.46), channel_id=1, source_target_pairs={{0,8},{2,10},{4,12},{6,14},{8,0},{10,2},{12,4},{14,6},{1,9},{3,11}... | collective-permute-start | bytes 196616 | tf_op jit(solution)/shard_map/ppermute | solution.py:29
  37.6 4.3 %collective-permute-start.15 = (bf16[128,256]{1,0:T(8,128)(2,1)S(1)}, bf16[128,256]{1,0:T(8,128)(2,1)S(1)}, u32[]{:S(2)}, u32[]{:S(2)}) collective-permute-start(bf16[128,256]{1,0:T(8,128)(2,1)S(1)} %get-tuple-element.52), channel_id=1, source_target_pairs={{0,2},{2,0},{4,6},{6,4},{8,10},{10,8},{12,14},{14,12},{1,3},{3,1},... | collective-permute-start | bytes 196616 | tf_op jit(solution)/shard_map/ppermute | solution.py:29
  42.3 1.2 %collective-permute-start.16 = (f32[1,256]{1,0:T(1,128)S(1)}, f32[1,256]{1,0:T(1,128)S(1)}, u32[]{:S(2)}, u32[]{:S(2)}) collective-permute-start(f32[1,256]{1,0:T(1,128)S(1)} %get-tuple-element.56), channel_id=1, source_target_pairs={{0,1},{1,0},{2,3},{3,2},{4,5},{5,4},{6,7},{7,6},{8,9},{9,8},{10,11... | collective-permute-start | bytes 3080 | tf_op jit(solution)/shard_map/ppermute | solution.py:25

commit v5 on v4

--- a/solution.py
+++ b/solution.py
@@ -11,7 +11,7 @@
 NGC = 8
 RBLK = 128
 LANE = 128
-CHUNK = 32
+CHUNK = 16
 GROUP = 8
 
 LOG_PRIOR = (-4.6051702, -3.2188758, -0.1625189, -2.8134107, -3.5065579, -4.6051702)
@@ -27,6 +27,10 @@
 
 def send(value, step, count):
     return lax.ppermute(value, "samp", [(i, i ^ step) for i in range(count)])
+
+
+def across_of(half):
+    return half + half // 2
 
 
 def call(body, name, outs, *args, scratch=(), cost=1):
@@ -72,7 +76,7 @@
     ask[...] = jnp.broadcast_to(best.astype(F32), ask.shape).astype(BF16)
 
 
-def map_kernel(neighbours, weight, plf, noted, out, total, wide):
+def map_kernel(neighbours, weight, plf, noted, out, total, inverse, wide):
     rows = neighbours.shape[0]
     listed = neighbours.shape[1]
     count = lax.axis_size("samp")
@@ -109,24 +113,26 @@
         out[:, p * RBLK : (p + 1) * RBLK] = wide[p].astype(BF16)
     summed = jnp.sum(weight[...].astype(F32), axis=1, keepdims=True)
     total[...] = jnp.broadcast_to(summed, total.shape)
-
-
-def stats_kernel(coverage, onehot, stats):
-    rows = coverage.shape[0]
-    stats[:, 0:rows] = dot(onehot[...].astype(BF16), coverage[...], 1, 1)
-    number = jnp.sum(onehot[...], axis=1, keepdims=True)
-    stats[:, rows:] = jnp.broadcast_to(number, (NGC, LANE))
-
-
-def norm_kernel(coverage, mine, theirs, onehot, ask, noted, wide):
-    rows, cols = coverage.shape
+    inverse[...] = 1.0 / plf[...]
+
+
+def bin_rows(bins):
+    return lax.broadcasted_iota(jnp.int32, (NGC, bins.shape[1]), 0) == bins[...]
+
+
+def stats_kernel(coverage, bins, stats):
+    stats[...] = dot(bin_rows(bins).astype(F32).astype(BF16), coverage[...], 1, 1)
+
+
+def norm_kernel(coverage, mine, theirs, bins, ask, noted, wide):
+    rows, cols = coverage.shape[0] - LANE, coverage.shape[1]
     extra = ask.shape[0]
     sums = mine[:, 0:rows] + theirs[:, 0:rows]
     number = mine[:, rows : rows + 1] + theirs[:, rows : rows + 1]
     mean = jnp.sum(sums, axis=0, keepdims=True) / (cols * lax.axis_size("tgt"))
     scale = mean / (sums / jnp.maximum(number, 1.0))
-    scale = dot(jnp.where(sums > 0, scale, 0.0), onehot[...], 0, 0, EXACT)
-    block = (coverage[...].astype(F32) * scale).astype(BF16)
+    scale = dot(jnp.where(sums > 0, scale, 0.0), bin_rows(bins).astype(F32), 0, 0, EXACT)
+    block = (coverage[0:rows].astype(F32) * scale).astype(BF16)
     for out in (noted, wide):
         out[0:rows] = block
         out[rows : rows + extra] = ask[...]
@@ -146,7 +152,6 @@
         out[k - 1][0:RBLK] = pick(across, note[other : other + 1], parts)
         if k in late:
             out[k - 1][RBLK : 2 * RBLK] = pick(own, note[base + k : base + k + 1], parts)
-        out[k - 1][out[k - 1].shape[0] - asked :] = across[rows : rows + asked]
 
 
 def spread(first, second, third, normf, ratio, rel, own_sum, part):
@@ -220,11 +225,13 @@
     return [dot(mine, values, 1, 0) for values in (gates, covs, squares)]
 
 
-def early_two_kernel(early, weight, table, gate, ask, *refs):
+def early_two_kernel(early, weight, table, gate, across, ask, *refs):
     arrived, partial = refs[:-1], refs[-1]
-    own = pick(gate, ask[0:1], gate.shape[0] // RBLK)
-    gates = jnp.concatenate([own] + [ref[...] for ref in arrived], axis=0)
-    for i, moment in enumerate(gated(weight, table, gates, [0] + early)):
+    parts = gate.shape[0] // RBLK
+    far = early[-1]
+    gates = [pick(gate, ask[0:1], parts)] + [ref[...] for ref in arrived]
+    gates = jnp.concatenate(gates + [pick(across, ask[far : far + 1], parts)], axis=0)
+    for i, moment in enumerate(gated(weight, table, gates, early)):
         partial[i] = moment
 
 
@@ -270,26 +277,26 @@
                 finish(here, there, top / (tail + expo[0]))
 
 
-def gate_kernel(asked, ratio, rel, own_sum, theirs, inverse, plf, across, *refs):
+def gate_kernel(order, asked, ratio, rel, own_sum, theirs, inverse, plf, *refs):
     rows = ratio.shape[0]
-    mates = (len(refs) - 2) // 4
-    half = mates + 1
-    noted, passed, gate, out = refs[:mates], refs[mates : 2 * mates], refs[2 * mates], refs[2 * mates + 1 :]
+    noted, gate, out = refs[: len(order)], refs[len(order)], refs[len(order) + 1 :]
 
     def finish(here, there, value):
         offset = value - plf[here]
         gate[here, there] = (1.0 / (1.0 + 4.0 * (offset * offset))).astype(BF16)
 
     called(ratio, rel, own_sum, theirs, inverse, finish)
-    for p in range(1, 2 * half):
-        if p < half:
-            source = noted[p - 1]
-        elif p == half:
-            source = across
-        else:
-            source = passed[(p ^ half) - 1]
-        place = source.shape[0] - asked + p
-        out[p - 1][...] = pick(gate, source[place : place + 1], rows // RBLK)
+    for k, ref in zip(order, out):
+        spot = noted[k - 1].shape[0] - asked + k
+        ref[...] = pick(gate, noted[k - 1][spot : spot + 1], rows // RBLK)
+
+
+def pass_gate_kernel(order, asked, across, *refs):
+    noted, out = refs[: len(order)], refs[len(order) :]
+    far = across_of(len(order) + 1)
+    for k, ref in zip(order, out):
+        spot = noted[k - 1].shape[0] - asked + (k ^ far)
+        ref[...] = pick(across, noted[k - 1][spot : spot + 1], across.shape[0] // RBLK)
 
 
 def final_kernel(ratio, rel, own_sum, theirs, inverse, out):
@@ -306,12 +313,11 @@
     rows, cols = coverage.shape
     extra = -(-count // 16) * 16
     late = [3] if half > 3 else []
-    bins = lax.broadcasted_iota(jnp.int32, (NGC, cols), 0)
-    onehot = (bins == gc_bin[None, :]).astype(F32)
+    bins = gc_bin.reshape(1, cols)
+    counted = jnp.pad(coverage, ((0, LANE), (0, 0)), constant_values=1)
     plf = jnp.broadcast_to(ploidy.astype(F32)[:, None], (rows, LANE))
-    inverse = 1.0 / plf
-
-    (mine,) = call(stats_kernel, "bin_sums", [((NGC, rows + LANE), F32)], coverage, onehot)
+
+    (mine,) = call(stats_kernel, "bin_sums", [((NGC, rows + LANE), F32)], counted, bins)
     theirs = swap_tgt(mine)
     (ask,) = call(
         functools.partial(ask_kernel, rows), "choices", [((extra, cols), BF16)], neighbours
@@ -319,17 +325,18 @@
     own, wide = call(
         norm_kernel, "normalise",
         [((rows + extra, cols), BF16), ((rows + 2 * extra, cols), BF16)],
-        coverage, mine, theirs, onehot, ask,
+        counted, mine, theirs, bins, ask,
     )
     across = send(wide, half, count)
     noted = [send(ask if k in late else own, k, count) for k in mates]
-    weight, total = call(
-        map_kernel, "weight_map", [((rows, count * RBLK), BF16), ((rows, LANE), F32)],
+    weight, total, inverse = call(
+        map_kernel, "weight_map",
+        [((rows, count * RBLK), BF16), ((rows, LANE), F32), ((rows, LANE), F32)],
         neighbours, nbr_weight, plf, own, scratch=[pltpu.VMEM((count, rows, RBLK), F32)],
     )
     passed = call(
         functools.partial(pass_kernel, late, extra), "pass_on",
-        [(((2 if k in late else 1) * RBLK + extra, cols), BF16) for k in mates],
+        [(((2 if k in late else 1) * RBLK, cols), BF16) for k in mates],
         total, own, across, *noted,
     )
     passed = [send(block, k, count) for k, block in zip(mates, passed)]
@@ -345,22 +352,28 @@
         [((count * RBLK, cols), BF16)] + spreads,
         weight, total, own, table, partial, *passed,
     )
+    order = list(range(half - 1, 0, -1))
     gate, *gates = call(
-        functools.partial(gate_kernel, extra), "gate",
-        [((rows, cols), BF16)] + [((RBLK, cols), BF16)] * (count - 1),
-        ratio, rel, own_sum, swap_tgt(part), inverse, plf, across, *noted, *passed,
-    )
-    order = [half + i for i in (0, 2, 1) if i < half] + list(range(half + 3, count))
-    order += list(range(half - 1, 0, -1))
-    gates = [send(gates[p - 1], p, count) for p in order]
-    last = 1
+        functools.partial(gate_kernel, order, extra), "gate",
+        [((rows, cols), BF16)] + [((RBLK, cols), BF16)] * len(order),
+        ratio, rel, own_sum, swap_tgt(part), inverse, plf, *noted,
+    )
+    far = across_of(half)
+    far_gate = send(gate, far, count)
+    gates = [send(block, k, count) for k, block in zip(order, gates)]
     (partial,) = call(
-        functools.partial(early_two_kernel, order[:-last]), "early_moments_two",
-        [((3, rows, cols), F32)], weight, table, gate, ask, *gates[:-last],
-    )
+        functools.partial(early_two_kernel, [0] + order + [far]), "early_moments_two",
+        [((3, rows, cols), F32)], weight, table, gate, far_gate, ask, *gates,
+    )
+    order = [3, 1, 2] if half == 4 else order
+    gates = call(
+        functools.partial(pass_gate_kernel, order, extra), "pass_on_gate",
+        [((RBLK, cols), BF16)] * len(order), far_gate, *noted,
+    )
+    gates = [send(block, k, count) for k, block in zip(order, gates)]
     ratio, rel, own_sum, part = call(
-        functools.partial(second_kernel, order[-last:], rows), "moments_two", spreads,
-        weight, table, own, partial, *gates[-last:],
+        functools.partial(second_kernel, [k ^ far for k in order], rows), "moments_two", spreads,
+        weight, table, own, partial, *gates,
     )
     (out,) = call(
         final_kernel, "copy_number", [((rows, cols), F32)],

time: 45.4 us -> 43.9 us (0.967)
  other arithmetic: 0.73 us -> 0.01 us
  starting transfers between devices: 22.3 us -> 21.6 us
    pad x0 -> x1, local copies, waits for them, and re-layouts: none -> 0.93 us  [body(): counted = jnp.pad(coverage, ((0, LANE), (0, 0)), constant_values=1)]
    convert_element_type x1 -> x0, other arithmetic: 0.72 us -> none  [body(): onehot = (bins == gc_bin[None, :]).astype(F32)]
    unnamed x8, local copies, waits for them, and re-layouts: 1.66 us -> 1 us
    ppermute x14, starting transfers between devices: 21.6 us -> 21 us  [send(): return lax.ppermute(value, 'samp', [(i, i ^ step) for i in range(count)])]
    pallas_call x11 -> x12, Pallas kernels: 8.4 us -> 8.34 us  [call(): pl.pallas_call(body, out_shape=[jax.ShapeDtypeStruct(shape, dtype) for sh...]
where the time goes in v5:
time: 43.9 us; the launch traced here: 43.7 us
  starting transfers between devices  21.6 us (49%)
  waiting for transfers between devices  11.6 us (26%)
  Pallas kernels  8.34 us (19%)
  local copies, waits for them, and re-layouts  2.02 us (5%)
    ppermute x14, starting transfers between devices, send(): return lax.ppermute(value, 'samp', [(i, i ^ step) for i in range(count)])  21 us
    ppermute x14, waiting for transfers between devices, send(): return lax.ppermute(value, 'samp', [(i, i ^ step) for i in range(count)])  9.12 us
    pallas_call x12, Pallas kernels, call(): pl.pallas_call(body, out_shape=[jax.ShapeDtypeStruct(shape, dtype) for sh...  8.34 us
    ppermute x3, waiting for transfers between devices, swap_tgt(): return lax.ppermute(value, 'tgt', [(0, 1), (1, 0)])  2.45 us
    unnamed x8, local copies, waits for them, and re-layouts  1 us
    pad x1, local copies, waits for them, and re-layouts, body(): counted = jnp.pad(coverage, ((0, LANE), (0, 0)), constant_values=1)  0.93 us
  transfers between devices with their start and end apart: 17, of which 10 were waited for; matrix products, arithmetic and copies ran while one was open for 0% of the time, Pallas kernels for 9%

profile of v5, /device:TPU:0, one launch (start us, length us, event | category | flops | bytes accessed | tf_op | source)
XLA Modules:
  0.0 43.7 jit_solution(1263841546218376490)
XLA Ops:
  0.0 0.9 %pad.4.coverage = bf16[384,256]{1,0:T(8,128)(2,1)S(1)} pad(bf16[256,256]{1,0:T(8,128)(2,1)} %param.5, bf16[]{:T(256)} %constant.2.clone.1), padding=0_128x0_0 | pad | bytes 327682 | tf_op jit(solution)/shard_map/jit(_pad)/pad | solution.py:317
  2.9 4.0 %collective-permute-start.1 = (bf16[288,256]{1,0:T(8,128)(2,1)S(1)}, bf16[288,256]{1,0:T(8,128)(2,1)S(1)}, u32[]{:S(2)}, u32[]{:S(2)}) collective-permute-start(bf16[288,256]{1,0:T(8,128)(2,1)S(1)} %get-tuple-element.34), channel_id=1, source_target_pairs={{0,8},{2,10},{4,12},{6,14},{8,0},{10,2},{12,4},{14,6},{1,9},{3,11}... | collective-permute-start | bytes 442376 | tf_op jit(solution)/shard_map/ppermute | solution.py:29
  6.9 1.6 %collective-permute-start.3 = (bf16[272,256]{1,0:T(8,128)(2,1)S(1)}, bf16[272,256]{1,0:T(8,128)(2,1)S(1)}, u32[]{:S(2)}, u32[]{:S(2)}) collective-permute-start(bf16[272,256]{1,0:T(8,128)(2,1)S(1)} %get-tuple-element.31.noted.own), channel_id=1, source_target_pairs={{0,4},{2,6},{4,0},{6,2},{8,12},{10,14},{12,8},{14,10},{1,5},{3,7},... | collective-permute-start | bytes 417800 | tf_op jit(solution)/shard_map/ppermute | solution.py:29
  8.5 1.5 %collective-permute-start.2 = (bf16[272,256]{1,0:T(8,128)(2,1)S(1)}, bf16[272,256]{1,0:T(8,128)(2,1)S(1)}, u32[]{:S(2)}, u32[]{:S(2)}) collective-permute-start(bf16[272,256]{1,0:T(8,128)(2,1)S(1)} %get-tuple-element.31.noted.own), channel_id=1, source_target_pairs={{0,2},{2,0},{4,6},{6,4},{8,10},{10,8},{12,14},{14,12},{1,3},{3,1},... | collective-permute-start | bytes 417800 | tf_op jit(solution)/shard_map/ppermute | solution.py:29
  10.5 0.7 %copy-done.1 = bf16[256,128]{1,0:T(8,128)(2,1)S(1)} copy-done((bf16[256,128]{1,0:T(8,128)(2,1)S(1)}, bf16[256,128]{1,0:T(8,128)(2,1)}, u32[]{:S(2)}) %copy-start.1) | copy-done | bytes 65560
  11.3 2.9 %weight_map.1 = (bf16[256,1024]{1,0:T(8,128)(2,1)S(1)}, f32[256,128]{1,0:T(8,128)S(1)}, f32[256,128]{1,0:T(8,128)S(1)}) custom-call(s32[256,128]{1,0:T(8,128)S(1)} %copy-done, bf16[256,128]{1,0:T(8,128)(2,1)S(1)} %copy-done.1, f32[256,128]{1,0:T(8,128)S(1)} %broadcast_in_dim.2.plf, bf16[272,256]{1,0:T(8,128)(2,1)S(1)} %get-tuple-element.31.noted.own), custom_call_target="tpu_custom_call" | custom-call | flops 1 | bytes 1 | tf_op jit(solution)/shard_map/weight_map/pallas_call | solution.py:37
  14.2 1.4 %collective-permute-done.4.refs_2_ = bf16[16,256]{1,0:T(8,128)(2,1)S(1)} collective-permute-done((bf16[16,256]{1,0:T(8,128)(2,1)S(1)}, bf16[16,256]{1,0:T(8,128)(2,1)S(1)}, u32[]{:S(2)}, u32[]{:S(2)}) %collective-permute-start.4) | collective-permute-done | bytes 8224 | tf_op jit(solution)/shard_map/ppermute | solution.py:29
  15.6 1.4 %collective-permute-start.7 = (bf16[256,256]{1,0:T(8,128)(2,1)S(1)}, bf16[256,256]{1,0:T(8,128)(2,1)S(1)}, u32[]{:S(2)}, u32[]{:S(2)}) collective-permute-start(bf16[256,256]{1,0:T(8,128)(2,1)S(1)} %get-tuple-element.39), channel_id=1, source_target_pairs={{0,6},{2,4},{4,2},{6,0},{8,14},{10,12},{12,10},{14,8},{1,7},{3,5},... | collective-permute-start | bytes 393224 | tf_op jit(solution)/shard_map/ppermute | solution.py:29
  17.1 1.5 %collective-permute-start.5 = (bf16[128,256]{1,0:T(8,128)(2,1)S(1)}, bf16[128,256]{1,0:T(8,128)(2,1)S(1)}, u32[]{:S(2)}, u32[]{:S(2)}) collective-permute-start(bf16[128,256]{1,0:T(8,128)(2,1)S(1)} %get-tuple-element.37), channel_id=1, source_target_pairs={{0,2},{2,0},{4,6},{6,4},{8,10},{10,8},{12,14},{14,12},{1,3},{3,1},... | collective-permute-start | bytes 196616 | tf_op jit(solution)/shard_map/ppermute | solution.py:29
  18.6 0.6 %collective-permute-start.6 = (bf16[128,256]{1,0:T(8,128)(2,1)S(1)}, bf16[128,256]{1,0:T(8,128)(2,1)S(1)}, u32[]{:S(2)}, u32[]{:S(2)}) collective-permute-start(bf16[128,256]{1,0:T(8,128)(2,1)S(1)} %get-tuple-element.38), channel_id=1, source_target_pairs={{0,4},{2,6},{4,0},{6,2},{8,12},{10,14},{12,8},{14,10},{1,5},{3,7},... | collective-permute-start | bytes 196616 | tf_op jit(solution)/shard_map/ppermute | solution.py:29
  19.5 3.0 %collective-permute-done.5.refs_0_ = bf16[128,256]{1,0:T(8,128)(2,1)S(1)} collective-permute-done((bf16[128,256]{1,0:T(8,128)(2,1)S(1)}, bf16[128,256]{1,0:T(8,128)(2,1)S(1)}, u32[]{:S(2)}, u32[]{:S(2)}) %collective-permute-start.5) | collective-permute-done | bytes 65568 | tf_op jit(solution)/shard_map/ppermute | solution.py:29
  23.4 1.1 %collective-permute-done.8.theirs = f32[1,256]{1,0:T(1,128)S(1)} collective-permute-done((f32[1,256]{1,0:T(1,128)S(1)}, f32[1,256]{1,0:T(1,128)S(1)}, u32[]{:S(2)}, u32[]{:S(2)}) %collective-permute-start.8) | collective-permute-done | bytes 1056 | tf_op jit(solution)/shard_map/ppermute | solution.py:25
  24.5 1.0 %gate.1 = (bf16[256,256]{1,0:T(8,128)(2,1)S(1)}, bf16[128,256]{1,0:T(8,128)(2,1)S(1)}, bf16[128,256]{1,0:T(8,128)(2,1)S(1)}, bf16[128,256]{1,0:T(8,128)(2,1)S(1)}) custom-call(f32[256,256]{1,0:T(8,128)S(1)} %get-tuple-element.41.ratio, f32[256,256]{1,0:T(8,128)S(1)} %get-tuple-element.42.rel, f32[256,128]{1,0:T(8,128)S(1)} %get-tuple-element.43.own_sum, ...), custom_call_target="tpu_custom_call" | custom-call | flops 1 | bytes 1 | tf_op jit(solution)/shard_map/gate/pallas_call | solution.py:37
  25.5 2.9 %collective-permute-start.9 = (bf16[256,256]{1,0:T(8,128)(2,1)S(1)}, bf16[256,256]{1,0:T(8,128)(2,1)S(1)}, u32[]{:S(2)}, u32[]{:S(2)}) collective-permute-start(bf16[256,256]{1,0:T(8,128)(2,1)S(1)} %get-tuple-element.46.gate), channel_id=1, source_target_pairs={{0,12},{2,14},{4,8},{6,10},{8,4},{10,6},{12,0},{14,2},{1,13},{3,15... | collective-permute-start | bytes 393224 | tf_op jit(solution)/shard_map/ppermute | solution.py:29
  28.4 2.2 %collective-permute-start.11 = (bf16[128,256]{1,0:T(8,128)(2,1)S(1)}, bf16[128,256]{1,0:T(8,128)(2,1)S(1)}, u32[]{:S(2)}, u32[]{:S(2)}) collective-permute-start(bf16[128,256]{1,0:T(8,128)(2,1)S(1)} %get-tuple-element.48), channel_id=1, source_target_pairs={{0,4},{2,6},{4,0},{6,2},{8,12},{10,14},{12,8},{14,10},{1,5},{3,7},... | collective-permute-start | bytes 196616 | tf_op jit(solution)/shard_map/ppermute | solution.py:29
  30.6 1.3 %collective-permute-start.12 = (bf16[128,256]{1,0:T(8,128)(2,1)S(1)}, bf16[128,256]{1,0:T(8,128)(2,1)S(1)}, u32[]{:S(2)}, u32[]{:S(2)}) collective-permute-start(bf16[128,256]{1,0:T(8,128)(2,1)S(1)} %get-tuple-element.49), channel_id=1, source_target_pairs={{0,2},{2,0},{4,6},{6,4},{8,10},{10,8},{12,14},{14,12},{1,3},{3,1},... | collective-permute-start | bytes 196616 | tf_op jit(solution)/shard_map/ppermute | solution.py:29
  31.9 1.8 %collective-permute-done.9.across = bf16[256,256]{1,0:T(8,128)(2,1)S(1)} collective-permute-done((bf16[256,256]{1,0:T(8,128)(2,1)S(1)}, bf16[256,256]{1,0:T(8,128)(2,1)S(1)}, u32[]{:S(2)}, u32[]{:S(2)}) %collective-permute-start.9) | collective-permute-done | bytes 131104 | tf_op jit(solution)/shard_map/ppermute | solution.py:29
  33.8 1.4 %collective-permute-start.13 = (bf16[128,256]{1,0:T(8,128)(2,1)S(1)}, bf16[128,256]{1,0:T(8,128)(2,1)S(1)}, u32[]{:S(2)}, u32[]{:S(2)}) collective-permute-start(bf16[128,256]{1,0:T(8,128)(2,1)S(1)} %get-tuple-element.50), channel_id=1, source_target_pairs={{0,6},{2,4},{4,2},{6,0},{8,14},{10,12},{12,10},{14,8},{1,7},{3,5},... | collective-permute-start | bytes 196616 | tf_op jit(solution)/shard_map/ppermute | solution.py:29
  35.2 0.9 %collective-permute-start.14 = (bf16[128,256]{1,0:T(8,128)(2,1)S(1)}, bf16[128,256]{1,0:T(8,128)(2,1)S(1)}, u32[]{:S(2)}, u32[]{:S(2)}) collective-permute-start(bf16[128,256]{1,0:T(8,128)(2,1)S(1)} %get-tuple-element.51), channel_id=1, source_target_pairs={{0,2},{2,0},{4,6},{6,4},{8,10},{10,8},{12,14},{14,12},{1,3},{3,1},... | collective-permute-start | bytes 196616 | tf_op jit(solution)/shard_map/ppermute | solution.py:29
  36.1 1.2 %collective-permute-start.15 = (bf16[128,256]{1,0:T(8,128)(2,1)S(1)}, bf16[128,256]{1,0:T(8,128)(2,1)S(1)}, u32[]{:S(2)}, u32[]{:S(2)}) collective-permute-start(bf16[128,256]{1,0:T(8,128)(2,1)S(1)} %get-tuple-element.52), channel_id=1, source_target_pairs={{0,4},{2,6},{4,0},{6,2},{8,12},{10,14},{12,8},{14,10},{1,5},{3,7},... | collective-permute-start | bytes 196616 | tf_op jit(solution)/shard_map/ppermute | solution.py:29
  37.3 0.5 %early_moments_two.1.partial = f32[3,256,256]{2,1,0:T(8,128)S(1)} custom-call(bf16[256,1024]{1,0:T(8,128)(2,1)S(1)} %get-tuple-element.32.weight, bf16[1024,256]{1,0:T(8,128)(2,1)S(1)} %get-tuple-element.40.table, bf16[256,256]{1,0:T(8,128)(2,1)S(1)} %get-tuple-element.46.gate, bf16[256,256]{1,0:T(8,128)(2,1)S(1)} %collective-permute-done.9.across, ...), custom_call_target="tpu_custom_call" | custom-call | flops 1 | bytes 1 | tf_op jit(solution)/shard_map/early_moments_two/pallas_call | solution.py:37
  37.9 1.7 %collective-permute-done.13.refs_0_ = bf16[128,256]{1,0:T(8,128)(2,1)S(1)} collective-permute-done((bf16[128,256]{1,0:T(8,128)(2,1)S(1)}, bf16[128,256]{1,0:T(8,128)(2,1)S(1)}, u32[]{:S(2)}, u32[]{:S(2)}) %collective-permute-start.13) | collective-permute-done | bytes 65568 | tf_op jit(solution)/shard_map/ppermute | solution.py:29
  41.0 1.1 %collective-permute-done.16.theirs = f32[1,256]{1,0:T(1,128)S(1)} collective-permute-done((f32[1,256]{1,0:T(1,128)S(1)}, f32[1,256]{1,0:T(1,128)S(1)}, u32[]{:S(2)}, u32[]{:S(2)}) %collective-permute-start.16) | collective-permute-done | bytes 1056 | tf_op jit(solution)/shard_map/ppermute | solution.py:25
  42.1 1.6 %copy_number.1 = f32[256,256]{1,0:T(8,128)} custom-call(f32[256,256]{1,0:T(8,128)S(1)} %get-tuple-element.53.ratio, f32[256,256]{1,0:T(8,128)S(1)} %get-tuple-element.54.rel, f32[256,128]{1,0:T(8,128)S(1)} %get-tuple-element.55.own_sum, f32[1,256]{1,0:T(1,128)S(1)} %collective-permute-done.16.theirs, f32[256,128]{1,0:T(8,128)S(1)} %get-tuple-element.45.inverse), custom_call_target="tpu_custom_call" | custom-call | flops 1 | bytes 1 | tf_op jit(solution)/shard_map/copy_number/pallas_call | solution.py:37
  (33 shorter events, 5.1 us)
Async XLA Ops:
  0.0 0.9 %copy-start.2 = (s32[256]{0:T(256)S(1)}, s32[256]{0:T(256)}, u32[]{:S(2)}) copy-start(s32[256]{0:T(256)} %param.9) | copy-start | bytes 3076
  0.9 0.9 %copy-start = (s32[256,128]{1,0:T(8,128)S(1)}, s32[256,128]{1,0:T(8,128)}, u32[]{:S(2)}) copy-start(s32[256,128]{1,0:T(8,128)} %neighbours.3) | copy-start | bytes 393220
  1.1 1.3 %collective-permute-start = (f32[8,384]{1,0:T(8,128)S(1)}, f32[8,384]{1,0:T(8,128)S(1)}, u32[]{:S(2)}, u32[]{:S(2)}) collective-permute-start(f32[8,384]{1,0:T(8,128)S(1)} %bin_sums.1.mine), channel_id=1, source_target_pairs={{0,1},{1,0},{2,3},{3,2},{4,5},{5,4},{6,7},{7,6},{8,9},{9,8},{10,11... | collective-permute-start | bytes 36872 | tf_op jit(solution)/shard_map/ppermute | solution.py:25
  2.9 7.5 %copy-start.3 = (s32[256]{0:T(256)S(1)}, s32[256]{0:T(256)}, u32[]{:S(2)}) copy-start(s32[256]{0:T(256)} %param.8) | copy-start | bytes 3076
  2.9 12.6 %collective-permute-start.1 = (bf16[288,256]{1,0:T(8,128)(2,1)S(1)}, bf16[288,256]{1,0:T(8,128)(2,1)S(1)}, u32[]{:S(2)}, u32[]{:S(2)}) collective-permute-start(bf16[288,256]{1,0:T(8,128)(2,1)S(1)} %get-tuple-element.34), channel_id=1, source_target_pairs={{0,8},{2,10},{4,12},{6,14},{8,0},{10,2},{12,4},{14,6},{1,9},{3,11}... | collective-permute-start | bytes 442376 | tf_op jit(solution)/shard_map/ppermute | solution.py:29
  6.9 8.6 %collective-permute-start.3 = (bf16[272,256]{1,0:T(8,128)(2,1)S(1)}, bf16[272,256]{1,0:T(8,128)(2,1)S(1)}, u32[]{:S(2)}, u32[]{:S(2)}) collective-permute-start(bf16[272,256]{1,0:T(8,128)(2,1)S(1)} %get-tuple-element.31.noted.own), channel_id=1, source_target_pairs={{0,4},{2,6},{4,0},{6,2},{8,12},{10,14},{12,8},{14,10},{1,5},{3,7},... | collective-permute-start | bytes 417800 | tf_op jit(solution)/shard_map/ppermute | solution.py:29
  8.5 7.1 %collective-permute-start.2 = (bf16[272,256]{1,0:T(8,128)(2,1)S(1)}, bf16[272,256]{1,0:T(8,128)(2,1)S(1)}, u32[]{:S(2)}, u32[]{:S(2)}) collective-permute-start(bf16[272,256]{1,0:T(8,128)(2,1)S(1)} %get-tuple-element.31.noted.own), channel_id=1, source_target_pairs={{0,2},{2,0},{4,6},{6,4},{8,10},{10,8},{12,14},{14,12},{1,3},{3,1},... | collective-permute-start | bytes 417800 | tf_op jit(solution)/shard_map/ppermute | solution.py:29
  10.0 5.5 %collective-permute-start.4 = (bf16[16,256]{1,0:T(8,128)(2,1)S(1)}, bf16[16,256]{1,0:T(8,128)(2,1)S(1)}, u32[]{:S(2)}, u32[]{:S(2)}) collective-permute-start(bf16[16,256]{1,0:T(8,128)(2,1)S(1)} %choices.1.ask), channel_id=1, source_target_pairs={{0,6},{2,4},{4,2},{6,0},{8,14},{10,12},{12,10},{14,8},{1,7},{3,5},... | collective-permute-start | bytes 24584 | tf_op jit(solution)/shard_map/ppermute | solution.py:29
  10.4 0.8 %copy-start.1 = (bf16[256,128]{1,0:T(8,128)(2,1)S(1)}, bf16[256,128]{1,0:T(8,128)(2,1)}, u32[]{:S(2)}) copy-start(bf16[256,128]{1,0:T(8,128)(2,1)} %weight.1) | copy-start | bytes 196612
  15.6 7.2 %collective-permute-start.7 = (bf16[256,256]{1,0:T(8,128)(2,1)S(1)}, bf16[256,256]{1,0:T(8,128)(2,1)S(1)}, u32[]{:S(2)}, u32[]{:S(2)}) collective-permute-start(bf16[256,256]{1,0:T(8,128)(2,1)S(1)} %get-tuple-element.39), channel_id=1, source_target_pairs={{0,6},{2,4},{4,2},{6,0},{8,14},{10,12},{12,10},{14,8},{1,7},{3,5},... | collective-permute-start | bytes 393224 | tf_op jit(solution)/shard_map/ppermute | solution.py:29
  17.1 5.4 %collective-permute-start.5 = (bf16[128,256]{1,0:T(8,128)(2,1)S(1)}, bf16[128,256]{1,0:T(8,128)(2,1)S(1)}, u32[]{:S(2)}, u32[]{:S(2)}) collective-permute-start(bf16[128,256]{1,0:T(8,128)(2,1)S(1)} %get-tuple-element.37), channel_id=1, source_target_pairs={{0,2},{2,0},{4,6},{6,4},{8,10},{10,8},{12,14},{14,12},{1,3},{3,1},... | collective-permute-start | bytes 196616 | tf_op jit(solution)/shard_map/ppermute | solution.py:29
  18.6 4.3 %collective-permute-start.6 = (bf16[128,256]{1,0:T(8,128)(2,1)S(1)}, bf16[128,256]{1,0:T(8,128)(2,1)S(1)}, u32[]{:S(2)}, u32[]{:S(2)}) collective-permute-start(bf16[128,256]{1,0:T(8,128)(2,1)S(1)} %get-tuple-element.38), channel_id=1, source_target_pairs={{0,4},{2,6},{4,0},{6,2},{8,12},{10,14},{12,8},{14,10},{1,5},{3,7},... | collective-permute-start | bytes 196616 | tf_op jit(solution)/shard_map/ppermute | solution.py:29
  23.3 1.2 %collective-permute-start.8 = (f32[1,256]{1,0:T(1,128)S(1)}, f32[1,256]{1,0:T(1,128)S(1)}, u32[]{:S(2)}, u32[]{:S(2)}) collective-permute-start(f32[1,256]{1,0:T(1,128)S(1)} %get-tuple-element.44), channel_id=1, source_target_pairs={{0,1},{1,0},{2,3},{3,2},{4,5},{5,4},{6,7},{7,6},{8,9},{9,8},{10,11... | collective-permute-start | bytes 3080 | tf_op jit(solution)/shard_map/ppermute | solution.py:25
  25.5 8.2 %collective-permute-start.9 = (bf16[256,256]{1,0:T(8,128)(2,1)S(1)}, bf16[256,256]{1,0:T(8,128)(2,1)S(1)}, u32[]{:S(2)}, u32[]{:S(2)}) collective-permute-start(bf16[256,256]{1,0:T(8,128)(2,1)S(1)} %get-tuple-element.46.gate), channel_id=1, source_target_pairs={{0,12},{2,14},{4,8},{6,10},{8,4},{10,6},{12,0},{14,2},{1,13},{3,15... | collective-permute-start | bytes 393224 | tf_op jit(solution)/shard_map/ppermute | solution.py:29
  28.4 7.7 %collective-permute-start.10 = (bf16[128,256]{1,0:T(8,128)(2,1)S(1)}, bf16[128,256]{1,0:T(8,128)(2,1)S(1)}, u32[]{:S(2)}, u32[]{:S(2)}) collective-permute-start(bf16[128,256]{1,0:T(8,128)(2,1)S(1)} %get-tuple-element.47), channel_id=1, source_target_pairs={{0,6},{2,4},{4,2},{6,0},{8,14},{10,12},{12,10},{14,8},{1,7},{3,5},... | collective-permute-start | bytes 196616 | tf_op jit(solution)/shard_map/ppermute | solution.py:29
  28.4 8.9 %collective-permute-start.11 = (bf16[128,256]{1,0:T(8,128)(2,1)S(1)}, bf16[128,256]{1,0:T(8,128)(2,1)S(1)}, u32[]{:S(2)}, u32[]{:S(2)}) collective-permute-start(bf16[128,256]{1,0:T(8,128)(2,1)S(1)} %get-tuple-element.48), channel_id=1, source_target_pairs={{0,4},{2,6},{4,0},{6,2},{8,12},{10,14},{12,8},{14,10},{1,5},{3,7},... | collective-permute-start | bytes 196616 | tf_op jit(solution)/shard_map/ppermute | solution.py:29
  30.6 6.7 %collective-permute-start.12 = (bf16[128,256]{1,0:T(8,128)(2,1)S(1)}, bf16[128,256]{1,0:T(8,128)(2,1)S(1)}, u32[]{:S(2)}, u32[]{:S(2)}) collective-permute-start(bf16[128,256]{1,0:T(8,128)(2,1)S(1)} %get-tuple-element.49), channel_id=1, source_target_pairs={{0,2},{2,0},{4,6},{6,4},{8,10},{10,8},{12,14},{14,12},{1,3},{3,1},... | collective-permute-start | bytes 196616 | tf_op jit(solution)/shard_map/ppermute | solution.py:29
  33.8 5.8 %collective-permute-start.13 = (bf16[128,256]{1,0:T(8,128)(2,1)S(1)}, bf16[128,256]{1,0:T(8,128)(2,1)S(1)}, u32[]{:S(2)}, u32[]{:S(2)}) collective-permute-start(bf16[128,256]{1,0:T(8,128)(2,1)S(1)} %get-tuple-element.50), channel_id=1, source_target_pairs={{0,6},{2,4},{4,2},{6,0},{8,14},{10,12},{12,10},{14,8},{1,7},{3,5},... | collective-permute-start | bytes 196616 | tf_op jit(solution)/shard_map/ppermute | solution.py:29
  35.2 4.7 %collective-permute-start.14 = (bf16[128,256]{1,0:T(8,128)(2,1)S(1)}, bf16[128,256]{1,0:T(8,128)(2,1)S(1)}, u32[]{:S(2)}, u32[]{:S(2)}) collective-permute-start(bf16[128,256]{1,0:T(8,128)(2,1)S(1)} %get-tuple-element.51), channel_id=1, source_target_pairs={{0,2},{2,0},{4,6},{6,4},{8,10},{10,8},{12,14},{14,12},{1,3},{3,1},... | collective-permute-start | bytes 196616 | tf_op jit(solution)/shard_map/ppermute | solution.py:29
  36.1 4.3 %collective-permute-start.15 = (bf16[128,256]{1,0:T(8,128)(2,1)S(1)}, bf16[128,256]{1,0:T(8,128)(2,1)S(1)}, u32[]{:S(2)}, u32[]{:S(2)}) collective-permute-start(bf16[128,256]{1,0:T(8,128)(2,1)S(1)} %get-tuple-element.52), channel_id=1, source_target_pairs={{0,4},{2,6},{4,0},{6,2},{8,12},{10,14},{12,8},{14,10},{1,5},{3,7},... | collective-permute-start | bytes 196616 | tf_op jit(solution)/shard_map/ppermute | solution.py:29
  40.9 1.2 %collective-permute-start.16 = (f32[1,256]{1,0:T(1,128)S(1)}, f32[1,256]{1,0:T(1,128)S(1)}, u32[]{:S(2)}, u32[]{:S(2)}) collective-permute-start(f32[1,256]{1,0:T(1,128)S(1)} %get-tuple-element.56), channel_id=1, source_target_pairs={{0,1},{1,0},{2,3},{3,2},{4,5},{5,4},{6,7},{7,6},{8,9},{9,8},{10,11... | collective-permute-start | bytes 3080 | tf_op jit(solution)/shard_map/ppermute | solution.py:25

commit v6 on v5

--- a/solution.py
+++ b/solution.py
@@ -18,7 +18,6 @@
 
 F32 = jnp.float32
 BF16 = jnp.bfloat16
-EXACT = lax.Precision.HIGHEST
 
 
 def swap_tgt(value):
@@ -46,14 +45,9 @@
     )(*args)
 
 
-def dot(left, right, left_dim, right_dim, precision=None):
-    return lax.dot_general(
-        left,
-        right,
-        (((left_dim,), (right_dim,)), ((), ())),
-        precision=precision,
-        preferred_element_type=F32,
-    )
+def dot(left, right, left_dim, right_dim):
+    dims = (((left_dim,), (right_dim,)), ((), ()))
+    return lax.dot_general(left, right, dims, preferred_element_type=F32)
 
 
 def pick(ref, ask, parts):
@@ -124,19 +118,28 @@
     stats[...] = dot(bin_rows(bins).astype(F32).astype(BF16), coverage[...], 1, 1)
 
 
-def norm_kernel(coverage, mine, theirs, bins, ask, noted, wide):
+def spread_bins(scale, bins):
+    terms = []
+    for _ in range(3):
+        terms.append(scale.astype(BF16).astype(F32))
+        scale = scale - terms[-1]
+    picked = bin_rows(bins).astype(F32)
+    left = jnp.concatenate(terms, axis=0).astype(BF16)
+    return dot(left, jnp.concatenate([picked] * 3, axis=0).astype(BF16), 0, 0)
+
+
+def norm_kernel(coverage, mine, theirs, bins, ask, noted, plain):
     rows, cols = coverage.shape[0] - LANE, coverage.shape[1]
     extra = ask.shape[0]
     sums = mine[:, 0:rows] + theirs[:, 0:rows]
     number = mine[:, rows : rows + 1] + theirs[:, rows : rows + 1]
     mean = jnp.sum(sums, axis=0, keepdims=True) / (cols * lax.axis_size("tgt"))
     scale = mean / (sums / jnp.maximum(number, 1.0))
-    scale = dot(jnp.where(sums > 0, scale, 0.0), bin_rows(bins).astype(F32), 0, 0, EXACT)
+    scale = spread_bins(jnp.where(sums > 0, scale, 0.0), bins)
     block = (coverage[0:rows].astype(F32) * scale).astype(BF16)
-    for out in (noted, wide):
-        out[0:rows] = block
-        out[rows : rows + extra] = ask[...]
-    wide[rows + extra :] = ask[...]
+    plain[...] = block
+    noted[0:rows] = block
+    noted[rows : rows + extra] = ask[...]
 
 
 def pass_kernel(late, asked, total, own, across, *refs):
@@ -199,7 +202,7 @@
 def first_kernel(late, rows, weight, total, own, early, partial, *refs):
     mates = len(refs) - 5
     half = mates + 1
-    passed, (table, ratio, rel, own_sum, part) = refs[:mates], refs[mates:]
+    passed, (table, ratio, rel, own_sum, part) = refs[:mates][::-1], refs[mates:]
     cols = own.shape[1]
     table[...] = early[...]
     arrived = []
@@ -322,12 +325,12 @@
     (ask,) = call(
         functools.partial(ask_kernel, rows), "choices", [((extra, cols), BF16)], neighbours
     )
-    own, wide = call(
+    own, plain = call(
         norm_kernel, "normalise",
-        [((rows + extra, cols), BF16), ((rows + 2 * extra, cols), BF16)],
+        [((rows + extra, cols), BF16), ((rows, cols), BF16)],
         counted, mine, theirs, bins, ask,
     )
-    across = send(wide, half, count)
+    across = send(plain, half, count)
     noted = [send(ask if k in late else own, k, count) for k in mates]
     weight, total, inverse = call(
         map_kernel, "weight_map",
@@ -350,7 +353,7 @@
     table, ratio, rel, own_sum, part = call(
         functools.partial(first_kernel, late, rows), "moments_one",
         [((count * RBLK, cols), BF16)] + spreads,
-        weight, total, own, table, partial, *passed,
+        weight, total, own, table, partial, *passed[::-1],
     )
     order = list(range(half - 1, 0, -1))
     gate, *gates = call(

time: 43.9 us -> 43.3 us (0.986)
  transfers between devices with their start and end apart: 17 -> 17, of which waited for: 10 -> 11; matrix products, arithmetic and copies ran while one was open for 0% -> 0% of each run, Pallas kernels for 9% -> 10%
where the time goes in v6:
time: 43.3 us; the launch traced here: 43.2 us
  starting transfers between devices  21.4 us (49%)
  waiting for transfers between devices  11.4 us (26%)
  Pallas kernels  8.14 us (19%)
  local copies, waits for them, and re-layouts  2.02 us (5%)
    ppermute x14, starting transfers between devices, send(): return lax.ppermute(value, 'samp', [(i, i ^ step) for i in range(count)])  20.8 us
    ppermute x14, waiting for transfers between devices, send(): return lax.ppermute(value, 'samp', [(i, i ^ step) for i in range(count)])  8.99 us
    pallas_call x12, Pallas kernels, call(): pl.pallas_call(body, out_shape=[jax.ShapeDtypeStruct(shape, dtype) for sh...  8.14 us
    ppermute x3, waiting for transfers between devices, swap_tgt(): return lax.ppermute(value, 'tgt', [(0, 1), (1, 0)])  2.46 us
    unnamed x8, local copies, waits for them, and re-layouts  1 us
    pad x1, local copies, waits for them, and re-layouts, body(): counted = jnp.pad(coverage, ((0, LANE), (0, 0)), constant_values=1)  0.93 us
  transfers between devices with their start and end apart: 17, of which 11 were waited for; matrix products, arithmetic and copies ran while one was open for 0% of the time, Pallas kernels for 10%

profile of v6, /device:TPU:0, one launch (start us, length us, event | category | flops | bytes accessed | tf_op | source)
XLA Modules:
  0.0 43.2 jit_solution(4972353945862770880)
XLA Ops:
  0.0 0.9 %pad.4.coverage = bf16[384,256]{1,0:T(8,128)(2,1)S(1)} pad(bf16[256,256]{1,0:T(8,128)(2,1)} %param.5, bf16[]{:T(256)} %constant.2.clone.1), padding=0_128x0_0 | pad | bytes 327682 | tf_op jit(solution)/shard_map/jit(_pad)/pad | solution.py:320
  2.8 3.0 %collective-permute-start.3 = (bf16[272,256]{1,0:T(8,128)(2,1)S(1)}, bf16[272,256]{1,0:T(8,128)(2,1)S(1)}, u32[]{:S(2)}, u32[]{:S(2)}) collective-permute-start(bf16[272,256]{1,0:T(8,128)(2,1)S(1)} %get-tuple-element.31.noted.own), channel_id=1, source_target_pairs={{0,4},{2,6},{4,0},{6,2},{8,12},{10,14},{12,8},{14,10},{1,5},{3,7},... | collective-permute-start | bytes 417800 | tf_op jit(solution)/shard_map/ppermute | solution.py:28
  5.7 1.5 %collective-permute-start.2 = (bf16[272,256]{1,0:T(8,128)(2,1)S(1)}, bf16[272,256]{1,0:T(8,128)(2,1)S(1)}, u32[]{:S(2)}, u32[]{:S(2)}) collective-permute-start(bf16[272,256]{1,0:T(8,128)(2,1)S(1)} %get-tuple-element.31.noted.own), channel_id=1, source_target_pairs={{0,2},{2,0},{4,6},{6,4},{8,10},{10,8},{12,14},{14,12},{1,3},{3,1},... | collective-permute-start | bytes 417800 | tf_op jit(solution)/shard_map/ppermute | solution.py:28
  7.3 2.6 %collective-permute-start.1 = (bf16[256,256]{1,0:T(8,128)(2,1)S(1)}, bf16[256,256]{1,0:T(8,128)(2,1)S(1)}, u32[]{:S(2)}, u32[]{:S(2)}) collective-permute-start(bf16[256,256]{1,0:T(8,128)(2,1)S(1)} %get-tuple-element.34), channel_id=1, source_target_pairs={{0,8},{2,10},{4,12},{6,14},{8,0},{10,2},{12,4},{14,6},{1,9},{3,11}... | collective-permute-start | bytes 393224 | tf_op jit(solution)/shard_map/ppermute | solution.py:28
  10.3 0.7 %copy-done.1 = bf16[256,128]{1,0:T(8,128)(2,1)S(1)} copy-done((bf16[256,128]{1,0:T(8,128)(2,1)S(1)}, bf16[256,128]{1,0:T(8,128)(2,1)}, u32[]{:S(2)}) %copy-start.1) | copy-done | bytes 65560
  11.1 2.9 %weight_map.1 = (bf16[256,1024]{1,0:T(8,128)(2,1)S(1)}, f32[256,128]{1,0:T(8,128)S(1)}, f32[256,128]{1,0:T(8,128)S(1)}) custom-call(s32[256,128]{1,0:T(8,128)S(1)} %copy-done, bf16[256,128]{1,0:T(8,128)(2,1)S(1)} %copy-done.1, f32[256,128]{1,0:T(8,128)S(1)} %broadcast_in_dim.2.plf, bf16[272,256]{1,0:T(8,128)(2,1)S(1)} %get-tuple-element.31.noted.own), custom_call_target="tpu_custom_call" | custom-call | flops 1 | bytes 1 | tf_op jit(solution)/shard_map/weight_map/pallas_call | solution.py:36
  14.4 1.6 %collective-permute-done.1.across = bf16[256,256]{1,0:T(8,128)(2,1)S(1)} collective-permute-done((bf16[256,256]{1,0:T(8,128)(2,1)S(1)}, bf16[256,256]{1,0:T(8,128)(2,1)S(1)}, u32[]{:S(2)}, u32[]{:S(2)}) %collective-permute-start.1) | collective-permute-done | bytes 131104 | tf_op jit(solution)/shard_map/ppermute | solution.py:28
  16.0 0.7 %collective-permute-start.5 = (bf16[256,256]{1,0:T(8,128)(2,1)S(1)}, bf16[256,256]{1,0:T(8,128)(2,1)S(1)}, u32[]{:S(2)}, u32[]{:S(2)}) collective-permute-start(bf16[256,256]{1,0:T(8,128)(2,1)S(1)} %get-tuple-element.37), channel_id=1, source_target_pairs={{0,6},{2,4},{4,2},{6,0},{8,14},{10,12},{12,10},{14,8},{1,7},{3,5},... | collective-permute-start | bytes 393224 | tf_op jit(solution)/shard_map/ppermute | solution.py:28
  16.7 1.4 %collective-permute-start.6 = (bf16[128,256]{1,0:T(8,128)(2,1)S(1)}, bf16[128,256]{1,0:T(8,128)(2,1)S(1)}, u32[]{:S(2)}, u32[]{:S(2)}) collective-permute-start(bf16[128,256]{1,0:T(8,128)(2,1)S(1)} %get-tuple-element.38), channel_id=1, source_target_pairs={{0,4},{2,6},{4,0},{6,2},{8,12},{10,14},{12,8},{14,10},{1,5},{3,7},... | collective-permute-start | bytes 196616 | tf_op jit(solution)/shard_map/ppermute | solution.py:28
  18.1 1.5 %collective-permute-start.7 = (bf16[128,256]{1,0:T(8,128)(2,1)S(1)}, bf16[128,256]{1,0:T(8,128)(2,1)S(1)}, u32[]{:S(2)}, u32[]{:S(2)}) collective-permute-start(bf16[128,256]{1,0:T(8,128)(2,1)S(1)} %get-tuple-element.39), channel_id=1, source_target_pairs={{0,2},{2,0},{4,6},{6,4},{8,10},{10,8},{12,14},{14,12},{1,3},{3,1},... | collective-permute-start | bytes 196616 | tf_op jit(solution)/shard_map/ppermute | solution.py:28
  19.9 1.8 %collective-permute-done.6.refs_1_ = bf16[128,256]{1,0:T(8,128)(2,1)S(1)} collective-permute-done((bf16[128,256]{1,0:T(8,128)(2,1)S(1)}, bf16[128,256]{1,0:T(8,128)(2,1)S(1)}, u32[]{:S(2)}, u32[]{:S(2)}) %collective-permute-start.6) | collective-permute-done | bytes 65568 | tf_op jit(solution)/shard_map/ppermute | solution.py:28
  21.7 0.9 %collective-permute-done.7.refs_2_ = bf16[128,256]{1,0:T(8,128)(2,1)S(1)} collective-permute-done((bf16[128,256]{1,0:T(8,128)(2,1)S(1)}, bf16[128,256]{1,0:T(8,128)(2,1)S(1)}, u32[]{:S(2)}, u32[]{:S(2)}) %collective-permute-start.7) | collective-permute-done | bytes 65568 | tf_op jit(solution)/shard_map/ppermute | solution.py:28
  23.2 1.1 %collective-permute-done.8.theirs = f32[1,256]{1,0:T(1,128)S(1)} collective-permute-done((f32[1,256]{1,0:T(1,128)S(1)}, f32[1,256]{1,0:T(1,128)S(1)}, u32[]{:S(2)}, u32[]{:S(2)}) %collective-permute-start.8) | collective-permute-done | bytes 1056 | tf_op jit(solution)/shard_map/ppermute | solution.py:24
  24.3 1.0 %gate.1 = (bf16[256,256]{1,0:T(8,128)(2,1)S(1)}, bf16[128,256]{1,0:T(8,128)(2,1)S(1)}, bf16[128,256]{1,0:T(8,128)(2,1)S(1)}, bf16[128,256]{1,0:T(8,128)(2,1)S(1)}) custom-call(f32[256,256]{1,0:T(8,128)S(1)} %get-tuple-element.41.ratio, f32[256,256]{1,0:T(8,128)S(1)} %get-tuple-element.42.rel, f32[256,128]{1,0:T(8,128)S(1)} %get-tuple-element.43.own_sum, ...), custom_call_target="tpu_custom_call" | custom-call | flops 1 | bytes 1 | tf_op jit(solution)/shard_map/gate/pallas_call | solution.py:36
  25.3 2.7 %collective-permute-start.9 = (bf16[256,256]{1,0:T(8,128)(2,1)S(1)}, bf16[256,256]{1,0:T(8,128)(2,1)S(1)}, u32[]{:S(2)}, u32[]{:S(2)}) collective-permute-start(bf16[256,256]{1,0:T(8,128)(2,1)S(1)} %get-tuple-element.46.gate), channel_id=1, source_target_pairs={{0,12},{2,14},{4,8},{6,10},{8,4},{10,6},{12,0},{14,2},{1,13},{3,15... | collective-permute-start | bytes 393224 | tf_op jit(solution)/shard_map/ppermute | solution.py:28
  28.0 2.5 %collective-permute-start.11 = (bf16[128,256]{1,0:T(8,128)(2,1)S(1)}, bf16[128,256]{1,0:T(8,128)(2,1)S(1)}, u32[]{:S(2)}, u32[]{:S(2)}) collective-permute-start(bf16[128,256]{1,0:T(8,128)(2,1)S(1)} %get-tuple-element.48), channel_id=1, source_target_pairs={{0,4},{2,6},{4,0},{6,2},{8,12},{10,14},{12,8},{14,10},{1,5},{3,7},... | collective-permute-start | bytes 196616 | tf_op jit(solution)/shard_map/ppermute | solution.py:28
  30.5 1.0 %collective-permute-start.12 = (bf16[128,256]{1,0:T(8,128)(2,1)S(1)}, bf16[128,256]{1,0:T(8,128)(2,1)S(1)}, u32[]{:S(2)}, u32[]{:S(2)}) collective-permute-start(bf16[128,256]{1,0:T(8,128)(2,1)S(1)} %get-tuple-element.49), channel_id=1, source_target_pairs={{0,2},{2,0},{4,6},{6,4},{8,10},{10,8},{12,14},{14,12},{1,3},{3,1},... | collective-permute-start | bytes 196616 | tf_op jit(solution)/shard_map/ppermute | solution.py:28
  31.5 2.0 %collective-permute-done.9.across = bf16[256,256]{1,0:T(8,128)(2,1)S(1)} collective-permute-done((bf16[256,256]{1,0:T(8,128)(2,1)S(1)}, bf16[256,256]{1,0:T(8,128)(2,1)S(1)}, u32[]{:S(2)}, u32[]{:S(2)}) %collective-permute-start.9) | collective-permute-done | bytes 131104 | tf_op jit(solution)/shard_map/ppermute | solution.py:28
  33.5 0.9 %collective-permute-start.13 = (bf16[128,256]{1,0:T(8,128)(2,1)S(1)}, bf16[128,256]{1,0:T(8,128)(2,1)S(1)}, u32[]{:S(2)}, u32[]{:S(2)}) collective-permute-start(bf16[128,256]{1,0:T(8,128)(2,1)S(1)} %get-tuple-element.50), channel_id=1, source_target_pairs={{0,6},{2,4},{4,2},{6,0},{8,14},{10,12},{12,10},{14,8},{1,7},{3,5},... | collective-permute-start | bytes 196616 | tf_op jit(solution)/shard_map/ppermute | solution.py:28
  34.5 1.1 %collective-permute-start.14 = (bf16[128,256]{1,0:T(8,128)(2,1)S(1)}, bf16[128,256]{1,0:T(8,128)(2,1)S(1)}, u32[]{:S(2)}, u32[]{:S(2)}) collective-permute-start(bf16[128,256]{1,0:T(8,128)(2,1)S(1)} %get-tuple-element.51), channel_id=1, source_target_pairs={{0,2},{2,0},{4,6},{6,4},{8,10},{10,8},{12,14},{14,12},{1,3},{3,1},... | collective-permute-start | bytes 196616 | tf_op jit(solution)/shard_map/ppermute | solution.py:28
  35.6 1.5 %collective-permute-start.15 = (bf16[128,256]{1,0:T(8,128)(2,1)S(1)}, bf16[128,256]{1,0:T(8,128)(2,1)S(1)}, u32[]{:S(2)}, u32[]{:S(2)}) collective-permute-start(bf16[128,256]{1,0:T(8,128)(2,1)S(1)} %get-tuple-element.52), channel_id=1, source_target_pairs={{0,4},{2,6},{4,0},{6,2},{8,12},{10,14},{12,8},{14,10},{1,5},{3,7},... | collective-permute-start | bytes 196616 | tf_op jit(solution)/shard_map/ppermute | solution.py:28
  37.6 1.6 %collective-permute-done.13.refs_0_ = bf16[128,256]{1,0:T(8,128)(2,1)S(1)} collective-permute-done((bf16[128,256]{1,0:T(8,128)(2,1)S(1)}, bf16[128,256]{1,0:T(8,128)(2,1)S(1)}, u32[]{:S(2)}, u32[]{:S(2)}) %collective-permute-start.13) | collective-permute-done | bytes 65568 | tf_op jit(solution)/shard_map/ppermute | solution.py:28
  40.4 1.1 %collective-permute-done.16.theirs = f32[1,256]{1,0:T(1,128)S(1)} collective-permute-done((f32[1,256]{1,0:T(1,128)S(1)}, f32[1,256]{1,0:T(1,128)S(1)}, u32[]{:S(2)}, u32[]{:S(2)}) %collective-permute-start.16) | collective-permute-done | bytes 1056 | tf_op jit(solution)/shard_map/ppermute | solution.py:24
  41.5 1.6 %copy_number.1 = f32[256,256]{1,0:T(8,128)} custom-call(f32[256,256]{1,0:T(8,128)S(1)} %get-tuple-element.53.ratio, f32[256,256]{1,0:T(8,128)S(1)} %get-tuple-element.54.rel, f32[256,128]{1,0:T(8,128)S(1)} %get-tuple-element.55.own_sum, f32[1,256]{1,0:T(1,128)S(1)} %collective-permute-done.16.theirs, f32[256,128]{1,0:T(8,128)S(1)} %get-tuple-element.45.inverse), custom_call_target="tpu_custom_call" | custom-call | flops 1 | bytes 1 | tf_op jit(solution)/shard_map/copy_number/pallas_call | solution.py:36
  (33 shorter events, 5.3 us)
Async XLA Ops:
  0.0 0.9 %copy-start.2 = (s32[256]{0:T(256)S(1)}, s32[256]{0:T(256)}, u32[]{:S(2)}) copy-start(s32[256]{0:T(256)} %param.9) | copy-start | bytes 3076
  0.9 0.9 %copy-start = (s32[256,128]{1,0:T(8,128)S(1)}, s32[256,128]{1,0:T(8,128)}, u32[]{:S(2)}) copy-start(s32[256,128]{1,0:T(8,128)} %neighbours.3) | copy-start | bytes 393220
  1.1 1.3 %collective-permute-start = (f32[8,384]{1,0:T(8,128)S(1)}, f32[8,384]{1,0:T(8,128)S(1)}, u32[]{:S(2)}, u32[]{:S(2)}) collective-permute-start(f32[8,384]{1,0:T(8,128)S(1)} %bin_sums.1.mine), channel_id=1, source_target_pairs={{0,1},{1,0},{2,3},{3,2},{4,5},{5,4},{6,7},{7,6},{8,9},{9,8},{10,11... | collective-permute-start | bytes 36872 | tf_op jit(solution)/shard_map/ppermute | solution.py:24
  2.7 7.5 %copy-start.3 = (s32[256]{0:T(256)S(1)}, s32[256]{0:T(256)}, u32[]{:S(2)}) copy-start(s32[256]{0:T(256)} %param.8) | copy-start | bytes 3076
  2.8 13.2 %collective-permute-start.3 = (bf16[272,256]{1,0:T(8,128)(2,1)S(1)}, bf16[272,256]{1,0:T(8,128)(2,1)S(1)}, u32[]{:S(2)}, u32[]{:S(2)}) collective-permute-start(bf16[272,256]{1,0:T(8,128)(2,1)S(1)} %get-tuple-element.31.noted.own), channel_id=1, source_target_pairs={{0,4},{2,6},{4,0},{6,2},{8,12},{10,14},{12,8},{14,10},{1,5},{3,7},... | collective-permute-start | bytes 417800 | tf_op jit(solution)/shard_map/ppermute | solution.py:28
  5.7 10.2 %collective-permute-start.2 = (bf16[272,256]{1,0:T(8,128)(2,1)S(1)}, bf16[272,256]{1,0:T(8,128)(2,1)S(1)}, u32[]{:S(2)}, u32[]{:S(2)}) collective-permute-start(bf16[272,256]{1,0:T(8,128)(2,1)S(1)} %get-tuple-element.31.noted.own), channel_id=1, source_target_pairs={{0,2},{2,0},{4,6},{6,4},{8,10},{10,8},{12,14},{14,12},{1,3},{3,1},... | collective-permute-start | bytes 417800 | tf_op jit(solution)/shard_map/ppermute | solution.py:28
  7.3 8.7 %collective-permute-start.1 = (bf16[256,256]{1,0:T(8,128)(2,1)S(1)}, bf16[256,256]{1,0:T(8,128)(2,1)S(1)}, u32[]{:S(2)}, u32[]{:S(2)}) collective-permute-start(bf16[256,256]{1,0:T(8,128)(2,1)S(1)} %get-tuple-element.34), channel_id=1, source_target_pairs={{0,8},{2,10},{4,12},{6,14},{8,0},{10,2},{12,4},{14,6},{1,9},{3,11}... | collective-permute-start | bytes 393224 | tf_op jit(solution)/shard_map/ppermute | solution.py:28
  9.8 4.5 %collective-permute-start.4 = (bf16[16,256]{1,0:T(8,128)(2,1)S(1)}, bf16[16,256]{1,0:T(8,128)(2,1)S(1)}, u32[]{:S(2)}, u32[]{:S(2)}) collective-permute-start(bf16[16,256]{1,0:T(8,128)(2,1)S(1)} %choices.1.ask), channel_id=1, source_target_pairs={{0,6},{2,4},{4,2},{6,0},{8,14},{10,12},{12,10},{14,8},{1,7},{3,5},... | collective-permute-start | bytes 24584 | tf_op jit(solution)/shard_map/ppermute | solution.py:28
  10.2 0.8 %copy-start.1 = (bf16[256,128]{1,0:T(8,128)(2,1)S(1)}, bf16[256,128]{1,0:T(8,128)(2,1)}, u32[]{:S(2)}) copy-start(bf16[256,128]{1,0:T(8,128)(2,1)} %weight.1) | copy-start | bytes 196612
  16.0 6.6 %collective-permute-start.5 = (bf16[256,256]{1,0:T(8,128)(2,1)S(1)}, bf16[256,256]{1,0:T(8,128)(2,1)S(1)}, u32[]{:S(2)}, u32[]{:S(2)}) collective-permute-start(bf16[256,256]{1,0:T(8,128)(2,1)S(1)} %get-tuple-element.37), channel_id=1, source_target_pairs={{0,6},{2,4},{4,2},{6,0},{8,14},{10,12},{12,10},{14,8},{1,7},{3,5},... | collective-permute-start | bytes 393224 | tf_op jit(solution)/shard_map/ppermute | solution.py:28
  16.7 5.1 %collective-permute-start.6 = (bf16[128,256]{1,0:T(8,128)(2,1)S(1)}, bf16[128,256]{1,0:T(8,128)(2,1)S(1)}, u32[]{:S(2)}, u32[]{:S(2)}) collective-permute-start(bf16[128,256]{1,0:T(8,128)(2,1)S(1)} %get-tuple-element.38), channel_id=1, source_target_pairs={{0,4},{2,6},{4,0},{6,2},{8,12},{10,14},{12,8},{14,10},{1,5},{3,7},... | collective-permute-start | bytes 196616 | tf_op jit(solution)/shard_map/ppermute | solution.py:28
  18.1 4.6 %collective-permute-start.7 = (bf16[128,256]{1,0:T(8,128)(2,1)S(1)}, bf16[128,256]{1,0:T(8,128)(2,1)S(1)}, u32[]{:S(2)}, u32[]{:S(2)}) collective-permute-start(bf16[128,256]{1,0:T(8,128)(2,1)S(1)} %get-tuple-element.39), channel_id=1, source_target_pairs={{0,2},{2,0},{4,6},{6,4},{8,10},{10,8},{12,14},{14,12},{1,3},{3,1},... | collective-permute-start | bytes 196616 | tf_op jit(solution)/shard_map/ppermute | solution.py:28
  23.1 1.2 %collective-permute-start.8 = (f32[1,256]{1,0:T(1,128)S(1)}, f32[1,256]{1,0:T(1,128)S(1)}, u32[]{:S(2)}, u32[]{:S(2)}) collective-permute-start(f32[1,256]{1,0:T(1,128)S(1)} %get-tuple-element.44), channel_id=1, source_target_pairs={{0,1},{1,0},{2,3},{3,2},{4,5},{5,4},{6,7},{7,6},{8,9},{9,8},{10,11... | collective-permute-start | bytes 3080 | tf_op jit(solution)/shard_map/ppermute | solution.py:24
  25.3 8.2 %collective-permute-start.9 = (bf16[256,256]{1,0:T(8,128)(2,1)S(1)}, bf16[256,256]{1,0:T(8,128)(2,1)S(1)}, u32[]{:S(2)}, u32[]{:S(2)}) collective-permute-start(bf16[256,256]{1,0:T(8,128)(2,1)S(1)} %get-tuple-element.46.gate), channel_id=1, source_target_pairs={{0,12},{2,14},{4,8},{6,10},{8,4},{10,6},{12,0},{14,2},{1,13},{3,15... | collective-permute-start | bytes 393224 | tf_op jit(solution)/shard_map/ppermute | solution.py:28
  28.0 7.6 %collective-permute-start.10 = (bf16[128,256]{1,0:T(8,128)(2,1)S(1)}, bf16[128,256]{1,0:T(8,128)(2,1)S(1)}, u32[]{:S(2)}, u32[]{:S(2)}) collective-permute-start(bf16[128,256]{1,0:T(8,128)(2,1)S(1)} %get-tuple-element.47), channel_id=1, source_target_pairs={{0,6},{2,4},{4,2},{6,0},{8,14},{10,12},{12,10},{14,8},{1,7},{3,5},... | collective-permute-start | bytes 196616 | tf_op jit(solution)/shard_map/ppermute | solution.py:28
  28.0 9.1 %collective-permute-start.11 = (bf16[128,256]{1,0:T(8,128)(2,1)S(1)}, bf16[128,256]{1,0:T(8,128)(2,1)S(1)}, u32[]{:S(2)}, u32[]{:S(2)}) collective-permute-start(bf16[128,256]{1,0:T(8,128)(2,1)S(1)} %get-tuple-element.48), channel_id=1, source_target_pairs={{0,4},{2,6},{4,0},{6,2},{8,12},{10,14},{12,8},{14,10},{1,5},{3,7},... | collective-permute-start | bytes 196616 | tf_op jit(solution)/shard_map/ppermute | solution.py:28
  30.5 6.6 %collective-permute-start.12 = (bf16[128,256]{1,0:T(8,128)(2,1)S(1)}, bf16[128,256]{1,0:T(8,128)(2,1)S(1)}, u32[]{:S(2)}, u32[]{:S(2)}) collective-permute-start(bf16[128,256]{1,0:T(8,128)(2,1)S(1)} %get-tuple-element.49), channel_id=1, source_target_pairs={{0,2},{2,0},{4,6},{6,4},{8,10},{10,8},{12,14},{14,12},{1,3},{3,1},... | collective-permute-start | bytes 196616 | tf_op jit(solution)/shard_map/ppermute | solution.py:28
  33.5 5.7 %collective-permute-start.13 = (bf16[128,256]{1,0:T(8,128)(2,1)S(1)}, bf16[128,256]{1,0:T(8,128)(2,1)S(1)}, u32[]{:S(2)}, u32[]{:S(2)}) collective-permute-start(bf16[128,256]{1,0:T(8,128)(2,1)S(1)} %get-tuple-element.50), channel_id=1, source_target_pairs={{0,6},{2,4},{4,2},{6,0},{8,14},{10,12},{12,10},{14,8},{1,7},{3,5},... | collective-permute-start | bytes 196616 | tf_op jit(solution)/shard_map/ppermute | solution.py:28
  34.5 5.0 %collective-permute-start.14 = (bf16[128,256]{1,0:T(8,128)(2,1)S(1)}, bf16[128,256]{1,0:T(8,128)(2,1)S(1)}, u32[]{:S(2)}, u32[]{:S(2)}) collective-permute-start(bf16[128,256]{1,0:T(8,128)(2,1)S(1)} %get-tuple-element.51), channel_id=1, source_target_pairs={{0,2},{2,0},{4,6},{6,4},{8,10},{10,8},{12,14},{14,12},{1,3},{3,1},... | collective-permute-start | bytes 196616 | tf_op jit(solution)/shard_map/ppermute | solution.py:28
  35.6 4.3 %collective-permute-start.15 = (bf16[128,256]{1,0:T(8,128)(2,1)S(1)}, bf16[128,256]{1,0:T(8,128)(2,1)S(1)}, u32[]{:S(2)}, u32[]{:S(2)}) collective-permute-start(bf16[128,256]{1,0:T(8,128)(2,1)S(1)} %get-tuple-element.52), channel_id=1, source_target_pairs={{0,4},{2,6},{4,0},{6,2},{8,12},{10,14},{12,8},{14,10},{1,5},{3,7},... | collective-permute-start | bytes 196616 | tf_op jit(solution)/shard_map/ppermute | solution.py:28
  40.3 1.2 %collective-permute-start.16 = (f32[1,256]{1,0:T(1,128)S(1)}, f32[1,256]{1,0:T(1,128)S(1)}, u32[]{:S(2)}, u32[]{:S(2)}) collective-permute-start(f32[1,256]{1,0:T(1,128)S(1)} %get-tuple-element.56), channel_id=1, source_target_pairs={{0,1},{1,0},{2,3},{3,2},{4,5},{5,4},{6,7},{7,6},{8,9},{9,8},{10,11... | collective-permute-start | bytes 3080 | tf_op jit(solution)/shard_map/ppermute | solution.py:24

commit v7 on v6

--- a/solution.py
+++ b/solution.py
@@ -12,7 +12,7 @@
 RBLK = 128
 LANE = 128
 CHUNK = 16
-GROUP = 8
+GROUP = 16
 
 LOG_PRIOR = (-4.6051702, -3.2188758, -0.1625189, -2.8134107, -3.5065579, -4.6051702)
 
@@ -28,8 +28,21 @@
     return lax.ppermute(value, "samp", [(i, i ^ step) for i in range(count)])
 
 
-def across_of(half):
-    return half + half // 2
+BLOCK_ACROSS, GATE_ACROSS = 4, 6
+NOTED, PASSED, OWN_GATES, PASSED_GATES = (1, 2, 3), (3, 2, 1), (3, 2, 1), (3, 1, 2)
+SPARE = 0
+
+
+def order_of(given, half):
+    return list(given) if half == 4 else list(range(1, half))
+
+
+def block_across(half):
+    return BLOCK_ACROSS if half == 4 else half
+
+
+def gate_across(half):
+    return GATE_ACROSS if half == 4 else half
 
 
 def call(body, name, outs, *args, scratch=(), cost=1):
@@ -48,6 +61,11 @@
 def dot(left, right, left_dim, right_dim):
     dims = (((left_dim,), (right_dim,)), ((), ()))
     return lax.dot_general(left, right, dims, preferred_element_type=F32)
+
+
+def line(ref, at):
+    start = at // 16 * 16
+    return ref[start : start + 16][at - start : at - start + 1]
 
 
 def pick(ref, ask, parts):
@@ -137,7 +155,7 @@
     scale = mean / (sums / jnp.maximum(number, 1.0))
     scale = spread_bins(jnp.where(sums > 0, scale, 0.0), bins)
     block = (coverage[0:rows].astype(F32) * scale).astype(BF16)
-    plain[...] = block
+    plain[0:rows] = block
     noted[0:rows] = block
     noted[rows : rows + extra] = ask[...]
 
@@ -145,16 +163,16 @@
 def pass_kernel(late, asked, total, own, across, *refs):
     mates = len(refs) // 2
     half = mates + 1
-    noted, out = refs[:mates], refs[mates:]
+    order, out = order_of(NOTED, half), refs[mates:]
     rows = own.shape[0] - asked
     parts = rows // RBLK
     for k in range(1, half):
-        note = noted[k - 1]
+        note = refs[order.index(k)]
         base = note.shape[0] - asked
-        other = base + (k ^ half)
-        out[k - 1][0:RBLK] = pick(across, note[other : other + 1], parts)
+        other = base + (k ^ block_across(half))
+        out[k - 1][0:RBLK] = pick(across, line(note, other), parts)
         if k in late:
-            out[k - 1][RBLK : 2 * RBLK] = pick(own, note[base + k : base + k + 1], parts)
+            out[k - 1][RBLK : 2 * RBLK] = pick(own, line(note, base + k), parts)
 
 
 def spread(first, second, third, normf, ratio, rel, own_sum, part):
@@ -192,8 +210,8 @@
     parts = rows // RBLK
     half = len(noted) + 1
     for p in early:
-        source = own if p == 0 else across if p == half else noted[p - 1]
-        table[p * RBLK : (p + 1) * RBLK] = pick(source, ask[p : p + 1], parts)
+        source = own if p == 0 else across if p == early[-1] else noted[p - 1]
+        table[p * RBLK : (p + 1) * RBLK] = pick(source, line(ask, p), parts)
     mine, block = columns(weight, early), place(table, early)
     partial[0] = dot(mine, block, 1, 0)
     partial[1] = dot(mine, squared(block), 1, 0)
@@ -202,17 +220,17 @@
 def first_kernel(late, rows, weight, total, own, early, partial, *refs):
     mates = len(refs) - 5
     half = mates + 1
-    passed, (table, ratio, rel, own_sum, part) = refs[:mates][::-1], refs[mates:]
+    order, (table, ratio, rel, own_sum, part) = order_of(PASSED, half), refs[mates:]
     cols = own.shape[1]
     table[...] = early[...]
     arrived = []
-    for k in range(1, half):
+    for k, ref in zip(order, refs):
         if k in late:
             arrived.append(k)
-            table[k * RBLK : (k + 1) * RBLK] = passed[k - 1][RBLK : 2 * RBLK]
-        other = k ^ half
+            table[k * RBLK : (k + 1) * RBLK] = ref[RBLK : 2 * RBLK]
+        other = k ^ block_across(half)
         arrived.append(other)
-        table[other * RBLK : (other + 1) * RBLK] = passed[k - 1][0:RBLK]
+        table[other * RBLK : (other + 1) * RBLK] = ref[0:RBLK]
     mine, block = columns(weight, arrived), place(table, arrived)
     second = partial[0] + dot(mine, block, 1, 0)
     third = partial[1] + dot(mine, squared(block), 1, 0)
@@ -232,8 +250,8 @@
     arrived, partial = refs[:-1], refs[-1]
     parts = gate.shape[0] // RBLK
     far = early[-1]
-    gates = [pick(gate, ask[0:1], parts)] + [ref[...] for ref in arrived]
-    gates = jnp.concatenate(gates + [pick(across, ask[far : far + 1], parts)], axis=0)
+    gates = [pick(gate, line(ask, 0), parts)] + [ref[...] for ref in arrived]
+    gates = jnp.concatenate(gates + [pick(across, line(ask, far), parts)], axis=0)
     for i, moment in enumerate(gated(weight, table, gates, early)):
         partial[i] = moment
 
@@ -258,19 +276,23 @@
             here = slice(begin + start, begin + start + CHUNK)
             spot = shared[start : start + CHUNK]
             by_ploidy = inverse[here]
-            centres = [max(state, 0.1) * by_ploidy for state in range(6)]
-            widths = [jnp.maximum(centre, 0.25) for centre in centres]
-            centres = [centre * root_half for centre in centres]
+            step = by_ploidy * root_half
             for lane in range(0, cols, LANE):
                 there = slice(lane, lane + LANE)
                 level = 0.5 * rel[here, there] + spot
                 copies = ratio[here, there] * root_half
+                grow = level * by_ploidy
                 scores, roots = [], []
-                for prior, centre, width in zip(LOG_PRIOR, centres, widths):
-                    root = lax.rsqrt(level * width + 0.01)
-                    delta = (copies - centre) * root
-                    scores.append(prior * math.log2(math.e) - delta * delta)
-                    roots.append(root)
+                for state, prior in enumerate(LOG_PRIOR):
+                    if state == 0:
+                        var, delta = 0.25 * level + 0.01, copies - 0.1 * step
+                    elif state == 1:
+                        var, delta = grow + 0.01, copies - step
+                    else:
+                        var, delta = var + grow, delta - step
+                    roots.append(lax.rsqrt(var))
+                    score = delta * roots[state]
+                    scores.append(prior * math.log2(math.e) - score * score)
                 peak = functools.reduce(jnp.maximum, scores)
                 expo = [jnp.exp2(s - peak) * root for s, root in zip(scores, roots)]
                 tail = top = expo[5]
@@ -291,15 +313,15 @@
     called(ratio, rel, own_sum, theirs, inverse, finish)
     for k, ref in zip(order, out):
         spot = noted[k - 1].shape[0] - asked + k
-        ref[...] = pick(gate, noted[k - 1][spot : spot + 1], rows // RBLK)
+        ref[...] = pick(gate, line(noted[k - 1], spot), rows // RBLK)
 
 
 def pass_gate_kernel(order, asked, across, *refs):
     noted, out = refs[: len(order)], refs[len(order) :]
-    far = across_of(len(order) + 1)
+    far = gate_across(len(order) + 1)
     for k, ref in zip(order, out):
         spot = noted[k - 1].shape[0] - asked + (k ^ far)
-        ref[...] = pick(across, noted[k - 1][spot : spot + 1], across.shape[0] // RBLK)
+        ref[...] = pick(across, line(noted[k - 1], spot), across.shape[0] // RBLK)
 
 
 def final_kernel(ratio, rel, own_sum, theirs, inverse, out):
@@ -327,10 +349,10 @@
     )
     own, plain = call(
         norm_kernel, "normalise",
-        [((rows + extra, cols), BF16), ((rows, cols), BF16)],
+        [((rows + extra, cols), BF16), ((rows + SPARE, cols), BF16)],
         counted, mine, theirs, bins, ask,
     )
-    across = send(plain, half, count)
+    across = send(plain, block_across(half), count)
     noted = [send(ask if k in late else own, k, count) for k in mates]
     weight, total, inverse = call(
         map_kernel, "weight_map",
@@ -340,11 +362,11 @@
     passed = call(
         functools.partial(pass_kernel, late, extra), "pass_on",
         [(((2 if k in late else 1) * RBLK, cols), BF16) for k in mates],
-        total, own, across, *noted,
+        total, own, across, *[noted[k - 1] for k in order_of(NOTED, half)],
     )
     passed = [send(block, k, count) for k, block in zip(mates, passed)]
     spreads = [((rows, cols), F32), ((rows, cols), F32), ((rows, LANE), F32), ((1, rows), F32)]
-    early = [0] + [k for k in mates if k not in late] + [half]
+    early = [0] + [k for k in mates if k not in late] + [block_across(half)]
     table, partial = call(
         functools.partial(early_one_kernel, early, rows), "early_moments_one",
         [((count * RBLK, cols), BF16), ((2, rows, cols), F32)],
@@ -353,22 +375,22 @@
     table, ratio, rel, own_sum, part = call(
         functools.partial(first_kernel, late, rows), "moments_one",
         [((count * RBLK, cols), BF16)] + spreads,
-        weight, total, own, table, partial, *passed[::-1],
-    )
-    order = list(range(half - 1, 0, -1))
+        weight, total, own, table, partial, *[passed[k - 1] for k in order_of(PASSED, half)],
+    )
+    order = order_of(OWN_GATES, half)
     gate, *gates = call(
         functools.partial(gate_kernel, order, extra), "gate",
         [((rows, cols), BF16)] + [((RBLK, cols), BF16)] * len(order),
         ratio, rel, own_sum, swap_tgt(part), inverse, plf, *noted,
     )
-    far = across_of(half)
+    far = gate_across(half)
     far_gate = send(gate, far, count)
     gates = [send(block, k, count) for k, block in zip(order, gates)]
     (partial,) = call(
         functools.partial(early_two_kernel, [0] + order + [far]), "early_moments_two",
         [((3, rows, cols), F32)], weight, table, gate, far_gate, ask, *gates,
     )
-    order = [3, 1, 2] if half == 4 else order
+    order = order_of(PASSED_GATES, half)
     gates = call(
         functools.partial(pass_gate_kernel, order, extra), "pass_on_gate",
         [((RBLK, cols), BF16)] * len(order), far_gate, *noted,

time: 43.3 us -> 42.9 us (level)
  Pallas kernels: 8.14 us -> 7.67 us
    pallas_call x12, Pallas kernels: 8.14 us -> 7.67 us  [call(): pl.pallas_call(body, out_shape=[jax.ShapeDtypeStruct(shape, dtype) for sh...]
  transfers between devices with their start and end apart: 17 -> 17, of which waited for: 11 -> 11; matrix products, arithmetic and copies ran while one was open for 0% -> 0% of each run, Pallas kernels for 10% -> 9%
where the time goes in v7:
time: 42.9 us; the launch traced here: 42.7 us
  starting transfers between devices  21.4 us (50%)
  waiting for transfers between devices  11.4 us (27%)
  Pallas kernels  7.67 us (18%)
  local copies, waits for them, and re-layouts  2.02 us (5%)
    ppermute x14, starting transfers between devices, send(): return lax.ppermute(value, 'samp', [(i, i ^ step) for i in range(count)])  20.8 us
    ppermute x14, waiting for transfers between devices, send(): return lax.ppermute(value, 'samp', [(i, i ^ step) for i in range(count)])  8.99 us
    pallas_call x12, Pallas kernels, call(): pl.pallas_call(body, out_shape=[jax.ShapeDtypeStruct(shape, dtype) for sh...  7.67 us
    ppermute x3, waiting for transfers between devices, swap_tgt(): return lax.ppermute(value, 'tgt', [(0, 1), (1, 0)])  2.46 us
    unnamed x8, local copies, waits for them, and re-layouts  1 us
    pad x1, local copies, waits for them, and re-layouts, body(): counted = jnp.pad(coverage, ((0, LANE), (0, 0)), constant_values=1)  0.93 us
  transfers between devices with their start and end apart: 17, of which 11 were waited for; matrix products, arithmetic and copies ran while one was open for 0% of the time, Pallas kernels for 9%

profile of v7, /device:TPU:0, one launch (start us, length us, event | category | flops | bytes accessed | tf_op | source)
XLA Modules:
  0.0 42.7 jit_solution(11275616191980060025)
XLA Ops:
  0.0 0.9 %pad.4.coverage = bf16[384,256]{1,0:T(8,128)(2,1)S(1)} pad(bf16[256,256]{1,0:T(8,128)(2,1)} %param.5, bf16[]{:T(256)} %constant.2.clone.1), padding=0_128x0_0 | pad | bytes 327682 | tf_op jit(solution)/shard_map/jit(_pad)/pad | solution.py:342
  2.8 3.0 %collective-permute-start.3 = (bf16[272,256]{1,0:T(8,128)(2,1)S(1)}, bf16[272,256]{1,0:T(8,128)(2,1)S(1)}, u32[]{:S(2)}, u32[]{:S(2)}) collective-permute-start(bf16[272,256]{1,0:T(8,128)(2,1)S(1)} %get-tuple-element.31.noted.own), channel_id=1, source_target_pairs={{0,4},{2,6},{4,0},{6,2},{8,12},{10,14},{12,8},{14,10},{1,5},{3,7},... | collective-permute-start | bytes 417800 | tf_op jit(solution)/shard_map/ppermute | solution.py:28
  5.7 1.5 %collective-permute-start.2 = (bf16[272,256]{1,0:T(8,128)(2,1)S(1)}, bf16[272,256]{1,0:T(8,128)(2,1)S(1)}, u32[]{:S(2)}, u32[]{:S(2)}) collective-permute-start(bf16[272,256]{1,0:T(8,128)(2,1)S(1)} %get-tuple-element.31.noted.own), channel_id=1, source_target_pairs={{0,2},{2,0},{4,6},{6,4},{8,10},{10,8},{12,14},{14,12},{1,3},{3,1},... | collective-permute-start | bytes 417800 | tf_op jit(solution)/shard_map/ppermute | solution.py:28
  7.3 2.6 %collective-permute-start.1 = (bf16[256,256]{1,0:T(8,128)(2,1)S(1)}, bf16[256,256]{1,0:T(8,128)(2,1)S(1)}, u32[]{:S(2)}, u32[]{:S(2)}) collective-permute-start(bf16[256,256]{1,0:T(8,128)(2,1)S(1)} %get-tuple-element.34), channel_id=1, source_target_pairs={{0,8},{2,10},{4,12},{6,14},{8,0},{10,2},{12,4},{14,6},{1,9},{3,11}... | collective-permute-start | bytes 393224 | tf_op jit(solution)/shard_map/ppermute | solution.py:28
  10.3 0.7 %copy-done.1 = bf16[256,128]{1,0:T(8,128)(2,1)S(1)} copy-done((bf16[256,128]{1,0:T(8,128)(2,1)S(1)}, bf16[256,128]{1,0:T(8,128)(2,1)}, u32[]{:S(2)}) %copy-start.1) | copy-done | bytes 65560
  11.1 2.6 %weight_map.1 = (bf16[256,1024]{1,0:T(8,128)(2,1)S(1)}, f32[256,128]{1,0:T(8,128)S(1)}, f32[256,128]{1,0:T(8,128)S(1)}) custom-call(s32[256,128]{1,0:T(8,128)S(1)} %copy-done, bf16[256,128]{1,0:T(8,128)(2,1)S(1)} %copy-done.1, f32[256,128]{1,0:T(8,128)S(1)} %broadcast_in_dim.2.plf, bf16[272,256]{1,0:T(8,128)(2,1)S(1)} %get-tuple-element.31.noted.own), custom_call_target="tpu_custom_call" | custom-call | flops 1 | bytes 1 | tf_op jit(solution)/shard_map/weight_map/pallas_call | solution.py:49
  13.7 0.7 %collective-permute-done.4.refs_2_ = bf16[16,256]{1,0:T(8,128)(2,1)S(1)} collective-permute-done((bf16[16,256]{1,0:T(8,128)(2,1)S(1)}, bf16[16,256]{1,0:T(8,128)(2,1)S(1)}, u32[]{:S(2)}, u32[]{:S(2)}) %collective-permute-start.4) | collective-permute-done | bytes 8224 | tf_op jit(solution)/shard_map/ppermute | solution.py:28
  14.4 1.6 %collective-permute-done.1.across = bf16[256,256]{1,0:T(8,128)(2,1)S(1)} collective-permute-done((bf16[256,256]{1,0:T(8,128)(2,1)S(1)}, bf16[256,256]{1,0:T(8,128)(2,1)S(1)}, u32[]{:S(2)}, u32[]{:S(2)}) %collective-permute-start.1) | collective-permute-done | bytes 131104 | tf_op jit(solution)/shard_map/ppermute | solution.py:28
  16.5 1.6 %collective-permute-start.6 = (bf16[128,256]{1,0:T(8,128)(2,1)S(1)}, bf16[128,256]{1,0:T(8,128)(2,1)S(1)}, u32[]{:S(2)}, u32[]{:S(2)}) collective-permute-start(bf16[128,256]{1,0:T(8,128)(2,1)S(1)} %get-tuple-element.38), channel_id=1, source_target_pairs={{0,4},{2,6},{4,0},{6,2},{8,12},{10,14},{12,8},{14,10},{1,5},{3,7},... | collective-permute-start | bytes 196616 | tf_op jit(solution)/shard_map/ppermute | solution.py:28
  18.1 1.5 %collective-permute-start.7 = (bf16[128,256]{1,0:T(8,128)(2,1)S(1)}, bf16[128,256]{1,0:T(8,128)(2,1)S(1)}, u32[]{:S(2)}, u32[]{:S(2)}) collective-permute-start(bf16[128,256]{1,0:T(8,128)(2,1)S(1)} %get-tuple-element.39), channel_id=1, source_target_pairs={{0,2},{2,0},{4,6},{6,4},{8,10},{10,8},{12,14},{14,12},{1,3},{3,1},... | collective-permute-start | bytes 196616 | tf_op jit(solution)/shard_map/ppermute | solution.py:28
  19.9 1.8 %collective-permute-done.6.refs_1_ = bf16[128,256]{1,0:T(8,128)(2,1)S(1)} collective-permute-done((bf16[128,256]{1,0:T(8,128)(2,1)S(1)}, bf16[128,256]{1,0:T(8,128)(2,1)S(1)}, u32[]{:S(2)}, u32[]{:S(2)}) %collective-permute-start.6) | collective-permute-done | bytes 65568 | tf_op jit(solution)/shard_map/ppermute | solution.py:28
  21.7 0.9 %collective-permute-done.7.refs_2_ = bf16[128,256]{1,0:T(8,128)(2,1)S(1)} collective-permute-done((bf16[128,256]{1,0:T(8,128)(2,1)S(1)}, bf16[128,256]{1,0:T(8,128)(2,1)S(1)}, u32[]{:S(2)}, u32[]{:S(2)}) %collective-permute-start.7) | collective-permute-done | bytes 65568 | tf_op jit(solution)/shard_map/ppermute | solution.py:28
  23.2 1.1 %collective-permute-done.8.theirs = f32[1,256]{1,0:T(1,128)S(1)} collective-permute-done((f32[1,256]{1,0:T(1,128)S(1)}, f32[1,256]{1,0:T(1,128)S(1)}, u32[]{:S(2)}, u32[]{:S(2)}) %collective-permute-start.8) | collective-permute-done | bytes 1056 | tf_op jit(solution)/shard_map/ppermute | solution.py:24
  24.3 0.9 %gate.1 = (bf16[256,256]{1,0:T(8,128)(2,1)S(1)}, bf16[128,256]{1,0:T(8,128)(2,1)S(1)}, bf16[128,256]{1,0:T(8,128)(2,1)S(1)}, bf16[128,256]{1,0:T(8,128)(2,1)S(1)}) custom-call(f32[256,256]{1,0:T(8,128)S(1)} %get-tuple-element.41.ratio, f32[256,256]{1,0:T(8,128)S(1)} %get-tuple-element.42.rel, f32[256,128]{1,0:T(8,128)S(1)} %get-tuple-element.43.own_sum, ...), custom_call_target="tpu_custom_call" | custom-call | flops 1 | bytes 1 | tf_op jit(solution)/shard_map/gate/pallas_call | solution.py:49
  25.2 2.7 %collective-permute-start.9 = (bf16[256,256]{1,0:T(8,128)(2,1)S(1)}, bf16[256,256]{1,0:T(8,128)(2,1)S(1)}, u32[]{:S(2)}, u32[]{:S(2)}) collective-permute-start(bf16[256,256]{1,0:T(8,128)(2,1)S(1)} %get-tuple-element.46.gate), channel_id=1, source_target_pairs={{0,12},{2,14},{4,8},{6,10},{8,4},{10,6},{12,0},{14,2},{1,13},{3,15... | collective-permute-start | bytes 393224 | tf_op jit(solution)/shard_map/ppermute | solution.py:28
  27.9 2.5 %collective-permute-start.11 = (bf16[128,256]{1,0:T(8,128)(2,1)S(1)}, bf16[128,256]{1,0:T(8,128)(2,1)S(1)}, u32[]{:S(2)}, u32[]{:S(2)}) collective-permute-start(bf16[128,256]{1,0:T(8,128)(2,1)S(1)} %get-tuple-element.48), channel_id=1, source_target_pairs={{0,4},{2,6},{4,0},{6,2},{8,12},{10,14},{12,8},{14,10},{1,5},{3,7},... | collective-permute-start | bytes 196616 | tf_op jit(solution)/shard_map/ppermute | solution.py:28
  30.4 1.0 %collective-permute-start.12 = (bf16[128,256]{1,0:T(8,128)(2,1)S(1)}, bf16[128,256]{1,0:T(8,128)(2,1)S(1)}, u32[]{:S(2)}, u32[]{:S(2)}) collective-permute-start(bf16[128,256]{1,0:T(8,128)(2,1)S(1)} %get-tuple-element.49), channel_id=1, source_target_pairs={{0,2},{2,0},{4,6},{6,4},{8,10},{10,8},{12,14},{14,12},{1,3},{3,1},... | collective-permute-start | bytes 196616 | tf_op jit(solution)/shard_map/ppermute | solution.py:28
  31.4 2.0 %collective-permute-done.9.across = bf16[256,256]{1,0:T(8,128)(2,1)S(1)} collective-permute-done((bf16[256,256]{1,0:T(8,128)(2,1)S(1)}, bf16[256,256]{1,0:T(8,128)(2,1)S(1)}, u32[]{:S(2)}, u32[]{:S(2)}) %collective-permute-start.9) | collective-permute-done | bytes 131104 | tf_op jit(solution)/shard_map/ppermute | solution.py:28
  33.4 0.9 %collective-permute-start.13 = (bf16[128,256]{1,0:T(8,128)(2,1)S(1)}, bf16[128,256]{1,0:T(8,128)(2,1)S(1)}, u32[]{:S(2)}, u32[]{:S(2)}) collective-permute-start(bf16[128,256]{1,0:T(8,128)(2,1)S(1)} %get-tuple-element.50), channel_id=1, source_target_pairs={{0,6},{2,4},{4,2},{6,0},{8,14},{10,12},{12,10},{14,8},{1,7},{3,5},... | collective-permute-start | bytes 196616 | tf_op jit(solution)/shard_map/ppermute | solution.py:28
  34.4 0.8 %collective-permute-start.14 = (bf16[128,256]{1,0:T(8,128)(2,1)S(1)}, bf16[128,256]{1,0:T(8,128)(2,1)S(1)}, u32[]{:S(2)}, u32[]{:S(2)}) collective-permute-start(bf16[128,256]{1,0:T(8,128)(2,1)S(1)} %get-tuple-element.51), channel_id=1, source_target_pairs={{0,2},{2,0},{4,6},{6,4},{8,10},{10,8},{12,14},{14,12},{1,3},{3,1},... | collective-permute-start | bytes 196616 | tf_op jit(solution)/shard_map/ppermute | solution.py:28
  35.1 1.9 %collective-permute-start.15 = (bf16[128,256]{1,0:T(8,128)(2,1)S(1)}, bf16[128,256]{1,0:T(8,128)(2,1)S(1)}, u32[]{:S(2)}, u32[]{:S(2)}) collective-permute-start(bf16[128,256]{1,0:T(8,128)(2,1)S(1)} %get-tuple-element.52), channel_id=1, source_target_pairs={{0,4},{2,6},{4,0},{6,2},{8,12},{10,14},{12,8},{14,10},{1,5},{3,7},... | collective-permute-start | bytes 196616 | tf_op jit(solution)/shard_map/ppermute | solution.py:28
  37.5 1.6 %collective-permute-done.13.refs_0_ = bf16[128,256]{1,0:T(8,128)(2,1)S(1)} collective-permute-done((bf16[128,256]{1,0:T(8,128)(2,1)S(1)}, bf16[128,256]{1,0:T(8,128)(2,1)S(1)}, u32[]{:S(2)}, u32[]{:S(2)}) %collective-permute-start.13) | collective-permute-done | bytes 65568 | tf_op jit(solution)/shard_map/ppermute | solution.py:28
  40.0 1.1 %collective-permute-done.16.theirs = f32[1,256]{1,0:T(1,128)S(1)} collective-permute-done((f32[1,256]{1,0:T(1,128)S(1)}, f32[1,256]{1,0:T(1,128)S(1)}, u32[]{:S(2)}, u32[]{:S(2)}) %collective-permute-start.16) | collective-permute-done | bytes 1056 | tf_op jit(solution)/shard_map/ppermute | solution.py:24
  41.2 1.5 %copy_number.1 = f32[256,256]{1,0:T(8,128)} custom-call(f32[256,256]{1,0:T(8,128)S(1)} %get-tuple-element.53.ratio, f32[256,256]{1,0:T(8,128)S(1)} %get-tuple-element.54.rel, f32[256,128]{1,0:T(8,128)S(1)} %get-tuple-element.55.own_sum, f32[1,256]{1,0:T(1,128)S(1)} %collective-permute-done.16.theirs, f32[256,128]{1,0:T(8,128)S(1)} %get-tuple-element.45.inverse), custom_call_target="tpu_custom_call" | custom-call | flops 1 | bytes 1 | tf_op jit(solution)/shard_map/copy_number/pallas_call | solution.py:49
  (33 shorter events, 5.1 us)
Async XLA Ops:
  0.0 0.9 %copy-start.2 = (s32[256]{0:T(256)S(1)}, s32[256]{0:T(256)}, u32[]{:S(2)}) copy-start(s32[256]{0:T(256)} %param.9) | copy-start | bytes 3076
  0.9 0.9 %copy-start = (s32[256,128]{1,0:T(8,128)S(1)}, s32[256,128]{1,0:T(8,128)}, u32[]{:S(2)}) copy-start(s32[256,128]{1,0:T(8,128)} %neighbours.3) | copy-start | bytes 393220
  1.1 1.3 %collective-permute-start = (f32[8,384]{1,0:T(8,128)S(1)}, f32[8,384]{1,0:T(8,128)S(1)}, u32[]{:S(2)}, u32[]{:S(2)}) collective-permute-start(f32[8,384]{1,0:T(8,128)S(1)} %bin_sums.1.mine), channel_id=1, source_target_pairs={{0,1},{1,0},{2,3},{3,2},{4,5},{5,4},{6,7},{7,6},{8,9},{9,8},{10,11... | collective-permute-start | bytes 36872 | tf_op jit(solution)/shard_map/ppermute | solution.py:24
  2.7 7.5 %copy-start.3 = (s32[256]{0:T(256)S(1)}, s32[256]{0:T(256)}, u32[]{:S(2)}) copy-start(s32[256]{0:T(256)} %param.8) | copy-start | bytes 3076
  2.8 13.2 %collective-permute-start.3 = (bf16[272,256]{1,0:T(8,128)(2,1)S(1)}, bf16[272,256]{1,0:T(8,128)(2,1)S(1)}, u32[]{:S(2)}, u32[]{:S(2)}) collective-permute-start(bf16[272,256]{1,0:T(8,128)(2,1)S(1)} %get-tuple-element.31.noted.own), channel_id=1, source_target_pairs={{0,4},{2,6},{4,0},{6,2},{8,12},{10,14},{12,8},{14,10},{1,5},{3,7},... | collective-permute-start | bytes 417800 | tf_op jit(solution)/shard_map/ppermute | solution.py:28
  5.7 10.2 %collective-permute-start.2 = (bf16[272,256]{1,0:T(8,128)(2,1)S(1)}, bf16[272,256]{1,0:T(8,128)(2,1)S(1)}, u32[]{:S(2)}, u32[]{:S(2)}) collective-permute-start(bf16[272,256]{1,0:T(8,128)(2,1)S(1)} %get-tuple-element.31.noted.own), channel_id=1, source_target_pairs={{0,2},{2,0},{4,6},{6,4},{8,10},{10,8},{12,14},{14,12},{1,3},{3,1},... | collective-permute-start | bytes 417800 | tf_op jit(solution)/shard_map/ppermute | solution.py:28
  7.3 8.7 %collective-permute-start.1 = (bf16[256,256]{1,0:T(8,128)(2,1)S(1)}, bf16[256,256]{1,0:T(8,128)(2,1)S(1)}, u32[]{:S(2)}, u32[]{:S(2)}) collective-permute-start(bf16[256,256]{1,0:T(8,128)(2,1)S(1)} %get-tuple-element.34), channel_id=1, source_target_pairs={{0,8},{2,10},{4,12},{6,14},{8,0},{10,2},{12,4},{14,6},{1,9},{3,11}... | collective-permute-start | bytes 393224 | tf_op jit(solution)/shard_map/ppermute | solution.py:28
  9.8 4.5 %collective-permute-start.4 = (bf16[16,256]{1,0:T(8,128)(2,1)S(1)}, bf16[16,256]{1,0:T(8,128)(2,1)S(1)}, u32[]{:S(2)}, u32[]{:S(2)}) collective-permute-start(bf16[16,256]{1,0:T(8,128)(2,1)S(1)} %choices.1.ask), channel_id=1, source_target_pairs={{0,6},{2,4},{4,2},{6,0},{8,14},{10,12},{12,10},{14,8},{1,7},{3,5},... | collective-permute-start | bytes 24584 | tf_op jit(solution)/shard_map/ppermute | solution.py:28
  10.2 0.8 %copy-start.1 = (bf16[256,128]{1,0:T(8,128)(2,1)S(1)}, bf16[256,128]{1,0:T(8,128)(2,1)}, u32[]{:S(2)}) copy-start(bf16[256,128]{1,0:T(8,128)(2,1)} %weight.1) | copy-start | bytes 196612
  16.0 6.6 %collective-permute-start.5 = (bf16[256,256]{1,0:T(8,128)(2,1)S(1)}, bf16[256,256]{1,0:T(8,128)(2,1)S(1)}, u32[]{:S(2)}, u32[]{:S(2)}) collective-permute-start(bf16[256,256]{1,0:T(8,128)(2,1)S(1)} %get-tuple-element.37), channel_id=1, source_target_pairs={{0,6},{2,4},{4,2},{6,0},{8,14},{10,12},{12,10},{14,8},{1,7},{3,5},... | collective-permute-start | bytes 393224 | tf_op jit(solution)/shard_map/ppermute | solution.py:28
  16.5 5.2 %collective-permute-start.6 = (bf16[128,256]{1,0:T(8,128)(2,1)S(1)}, bf16[128,256]{1,0:T(8,128)(2,1)S(1)}, u32[]{:S(2)}, u32[]{:S(2)}) collective-permute-start(bf16[128,256]{1,0:T(8,128)(2,1)S(1)} %get-tuple-element.38), channel_id=1, source_target_pairs={{0,4},{2,6},{4,0},{6,2},{8,12},{10,14},{12,8},{14,10},{1,5},{3,7},... | collective-permute-start | bytes 196616 | tf_op jit(solution)/shard_map/ppermute | solution.py:28
  18.1 4.6 %collective-permute-start.7 = (bf16[128,256]{1,0:T(8,128)(2,1)S(1)}, bf16[128,256]{1,0:T(8,128)(2,1)S(1)}, u32[]{:S(2)}, u32[]{:S(2)}) collective-permute-start(bf16[128,256]{1,0:T(8,128)(2,1)S(1)} %get-tuple-element.39), channel_id=1, source_target_pairs={{0,2},{2,0},{4,6},{6,4},{8,10},{10,8},{12,14},{14,12},{1,3},{3,1},... | collective-permute-start | bytes 196616 | tf_op jit(solution)/shard_map/ppermute | solution.py:28
  23.1 1.2 %collective-permute-start.8 = (f32[1,256]{1,0:T(1,128)S(1)}, f32[1,256]{1,0:T(1,128)S(1)}, u32[]{:S(2)}, u32[]{:S(2)}) collective-permute-start(f32[1,256]{1,0:T(1,128)S(1)} %get-tuple-element.44), channel_id=1, source_target_pairs={{0,1},{1,0},{2,3},{3,2},{4,5},{5,4},{6,7},{7,6},{8,9},{9,8},{10,11... | collective-permute-start | bytes 3080 | tf_op jit(solution)/shard_map/ppermute | solution.py:24
  25.2 8.2 %collective-permute-start.9 = (bf16[256,256]{1,0:T(8,128)(2,1)S(1)}, bf16[256,256]{1,0:T(8,128)(2,1)S(1)}, u32[]{:S(2)}, u32[]{:S(2)}) collective-permute-start(bf16[256,256]{1,0:T(8,128)(2,1)S(1)} %get-tuple-element.46.gate), channel_id=1, source_target_pairs={{0,12},{2,14},{4,8},{6,10},{8,4},{10,6},{12,0},{14,2},{1,13},{3,15... | collective-permute-start | bytes 393224 | tf_op jit(solution)/shard_map/ppermute | solution.py:28
  27.9 7.2 %collective-permute-start.10 = (bf16[128,256]{1,0:T(8,128)(2,1)S(1)}, bf16[128,256]{1,0:T(8,128)(2,1)S(1)}, u32[]{:S(2)}, u32[]{:S(2)}) collective-permute-start(bf16[128,256]{1,0:T(8,128)(2,1)S(1)} %get-tuple-element.47), channel_id=1, source_target_pairs={{0,6},{2,4},{4,2},{6,0},{8,14},{10,12},{12,10},{14,8},{1,7},{3,5},... | collective-permute-start | bytes 196616 | tf_op jit(solution)/shard_map/ppermute | solution.py:28
  27.9 9.1 %collective-permute-start.11 = (bf16[128,256]{1,0:T(8,128)(2,1)S(1)}, bf16[128,256]{1,0:T(8,128)(2,1)S(1)}, u32[]{:S(2)}, u32[]{:S(2)}) collective-permute-start(bf16[128,256]{1,0:T(8,128)(2,1)S(1)} %get-tuple-element.48), channel_id=1, source_target_pairs={{0,4},{2,6},{4,0},{6,2},{8,12},{10,14},{12,8},{14,10},{1,5},{3,7},... | collective-permute-start | bytes 196616 | tf_op jit(solution)/shard_map/ppermute | solution.py:28
  30.4 6.6 %collective-permute-start.12 = (bf16[128,256]{1,0:T(8,128)(2,1)S(1)}, bf16[128,256]{1,0:T(8,128)(2,1)S(1)}, u32[]{:S(2)}, u32[]{:S(2)}) collective-permute-start(bf16[128,256]{1,0:T(8,128)(2,1)S(1)} %get-tuple-element.49), channel_id=1, source_target_pairs={{0,2},{2,0},{4,6},{6,4},{8,10},{10,8},{12,14},{14,12},{1,3},{3,1},... | collective-permute-start | bytes 196616 | tf_op jit(solution)/shard_map/ppermute | solution.py:28
  33.4 5.7 %collective-permute-start.13 = (bf16[128,256]{1,0:T(8,128)(2,1)S(1)}, bf16[128,256]{1,0:T(8,128)(2,1)S(1)}, u32[]{:S(2)}, u32[]{:S(2)}) collective-permute-start(bf16[128,256]{1,0:T(8,128)(2,1)S(1)} %get-tuple-element.50), channel_id=1, source_target_pairs={{0,6},{2,4},{4,2},{6,0},{8,14},{10,12},{12,10},{14,8},{1,7},{3,5},... | collective-permute-start | bytes 196616 | tf_op jit(solution)/shard_map/ppermute | solution.py:28
  34.4 5.0 %collective-permute-start.14 = (bf16[128,256]{1,0:T(8,128)(2,1)S(1)}, bf16[128,256]{1,0:T(8,128)(2,1)S(1)}, u32[]{:S(2)}, u32[]{:S(2)}) collective-permute-start(bf16[128,256]{1,0:T(8,128)(2,1)S(1)} %get-tuple-element.51), channel_id=1, source_target_pairs={{0,2},{2,0},{4,6},{6,4},{8,10},{10,8},{12,14},{14,12},{1,3},{3,1},... | collective-permute-start | bytes 196616 | tf_op jit(solution)/shard_map/ppermute | solution.py:28
  35.1 4.3 %collective-permute-start.15 = (bf16[128,256]{1,0:T(8,128)(2,1)S(1)}, bf16[128,256]{1,0:T(8,128)(2,1)S(1)}, u32[]{:S(2)}, u32[]{:S(2)}) collective-permute-start(bf16[128,256]{1,0:T(8,128)(2,1)S(1)} %get-tuple-element.52), channel_id=1, source_target_pairs={{0,4},{2,6},{4,0},{6,2},{8,12},{10,14},{12,8},{14,10},{1,5},{3,7},... | collective-permute-start | bytes 196616 | tf_op jit(solution)/shard_map/ppermute | solution.py:28
  40.0 1.2 %collective-permute-start.16 = (f32[1,256]{1,0:T(1,128)S(1)}, f32[1,256]{1,0:T(1,128)S(1)}, u32[]{:S(2)}, u32[]{:S(2)}) collective-permute-start(f32[1,256]{1,0:T(1,128)S(1)} %get-tuple-element.56), channel_id=1, source_target_pairs={{0,1},{1,0},{2,3},{3,2},{4,5},{5,4},{6,7},{7,6},{8,9},{9,8},{10,11... | collective-permute-start | bytes 3080 | tf_op jit(solution)/shard_map/ppermute | solution.py:24

commit v8 on v7

--- a/solution.py
+++ b/solution.py
@@ -254,6 +254,13 @@
     gates = jnp.concatenate(gates + [pick(across, line(ask, far), parts)], axis=0)
     for i, moment in enumerate(gated(weight, table, gates, early)):
         partial[i] = moment
+
+
+def more_two_kernel(positions, weight, table, before, *refs):
+    arrived, partial = refs[:-1], refs[-1]
+    gates = jnp.concatenate([ref[...] for ref in arrived], axis=0)
+    for i, moment in enumerate(gated(weight, table, gates, positions)):
+        partial[i] = before[i] + moment
 
 
 def second_kernel(late, rows, weight, table, own, partial, *refs):
@@ -396,9 +403,15 @@
         [((RBLK, cols), BF16)] * len(order), far_gate, *noted,
     )
     gates = [send(block, k, count) for k, block in zip(order, gates)]
+    late = [k ^ far for k in order]
+    if len(late) > 1:
+        (partial,) = call(
+            functools.partial(more_two_kernel, late[:-1]), "more_moments_two",
+            [((3, rows, cols), F32)], weight, table, partial, *gates[:-1],
+        )
     ratio, rel, own_sum, part = call(
-        functools.partial(second_kernel, [k ^ far for k in order], rows), "moments_two", spreads,
-        weight, table, own, partial, *gates,
+        functools.partial(second_kernel, late[-1:], rows), "moments_two", spreads,
+        weight, table, own, partial, gates[-1],
     )
     (out,) = call(
         final_kernel, "copy_number", [((rows, cols), F32)],

time: 42.9 us -> 42.9 us (level)
    pallas_call x12 -> x13, Pallas kernels: 7.67 us -> 7.82 us  [call(): pl.pallas_call(body, out_shape=[jax.ShapeDtypeStruct(shape, dtype) for sh...]
  transfers between devices with their start and end apart: 17 -> 17, of which waited for: 11 -> 10; matrix products, arithmetic and copies ran while one was open for 0% -> 0% of each run, Pallas kernels for 9% -> 10%
where the time goes in v8:
time: 42.9 us; the launch traced here: 42.7 us
  starting transfers between devices  21.4 us (50%)
  waiting for transfers between devices  11.3 us (26%)
  Pallas kernels  7.82 us (18%)
  local copies, waits for them, and re-layouts  2.02 us (5%)
    ppermute x14, starting transfers between devices, send(): return lax.ppermute(value, 'samp', [(i, i ^ step) for i in range(count)])  20.8 us
    ppermute x14, waiting for transfers between devices, send(): return lax.ppermute(value, 'samp', [(i, i ^ step) for i in range(count)])  8.85 us
    pallas_call x13, Pallas kernels, call(): pl.pallas_call(body, out_shape=[jax.ShapeDtypeStruct(shape, dtype) for sh...  7.82 us
    ppermute x3, waiting for transfers between devices, swap_tgt(): return lax.ppermute(value, 'tgt', [(0, 1), (1, 0)])  2.45 us
    unnamed x8, local copies, waits for them, and re-layouts  1 us
    pad x1, local copies, waits for them, and re-layouts, body(): counted = jnp.pad(coverage, ((0, LANE), (0, 0)), constant_values=1)  0.93 us
  transfers between devices with their start and end apart: 17, of which 10 were waited for; matrix products, arithmetic and copies ran while one was open for 0% of the time, Pallas kernels for 10%

profile of v8, /device:TPU:0, one launch (start us, length us, event | category | flops | bytes accessed | tf_op | source)
XLA Modules:
  0.0 42.7 jit_solution(11085365276733853223)
XLA Ops:
  0.0 0.9 %pad.4.coverage = bf16[384,256]{1,0:T(8,128)(2,1)S(1)} pad(bf16[256,256]{1,0:T(8,128)(2,1)} %param.5, bf16[]{:T(256)} %constant.2.clone.1), padding=0_128x0_0 | pad | bytes 327682 | tf_op jit(solution)/shard_map/jit(_pad)/pad | solution.py:349
  2.8 3.0 %collective-permute-start.3 = (bf16[272,256]{1,0:T(8,128)(2,1)S(1)}, bf16[272,256]{1,0:T(8,128)(2,1)S(1)}, u32[]{:S(2)}, u32[]{:S(2)}) collective-permute-start(bf16[272,256]{1,0:T(8,128)(2,1)S(1)} %get-tuple-element.31.noted.own), channel_id=1, source_target_pairs={{0,4},{2,6},{4,0},{6,2},{8,12},{10,14},{12,8},{14,10},{1,5},{3,7},... | collective-permute-start | bytes 417800 | tf_op jit(solution)/shard_map/ppermute | solution.py:28
  5.7 1.5 %collective-permute-start.2 = (bf16[272,256]{1,0:T(8,128)(2,1)S(1)}, bf16[272,256]{1,0:T(8,128)(2,1)S(1)}, u32[]{:S(2)}, u32[]{:S(2)}) collective-permute-start(bf16[272,256]{1,0:T(8,128)(2,1)S(1)} %get-tuple-element.31.noted.own), channel_id=1, source_target_pairs={{0,2},{2,0},{4,6},{6,4},{8,10},{10,8},{12,14},{14,12},{1,3},{3,1},... | collective-permute-start | bytes 417800 | tf_op jit(solution)/shard_map/ppermute | solution.py:28
  7.3 2.6 %collective-permute-start.1 = (bf16[256,256]{1,0:T(8,128)(2,1)S(1)}, bf16[256,256]{1,0:T(8,128)(2,1)S(1)}, u32[]{:S(2)}, u32[]{:S(2)}) collective-permute-start(bf16[256,256]{1,0:T(8,128)(2,1)S(1)} %get-tuple-element.34), channel_id=1, source_target_pairs={{0,8},{2,10},{4,12},{6,14},{8,0},{10,2},{12,4},{14,6},{1,9},{3,11}... | collective-permute-start | bytes 393224 | tf_op jit(solution)/shard_map/ppermute | solution.py:28
  10.3 0.7 %copy-done.1 = bf16[256,128]{1,0:T(8,128)(2,1)S(1)} copy-done((bf16[256,128]{1,0:T(8,128)(2,1)S(1)}, bf16[256,128]{1,0:T(8,128)(2,1)}, u32[]{:S(2)}) %copy-start.1) | copy-done | bytes 65560
  11.1 2.6 %weight_map.1 = (bf16[256,1024]{1,0:T(8,128)(2,1)S(1)}, f32[256,128]{1,0:T(8,128)S(1)}, f32[256,128]{1,0:T(8,128)S(1)}) custom-call(s32[256,128]{1,0:T(8,128)S(1)} %copy-done, bf16[256,128]{1,0:T(8,128)(2,1)S(1)} %copy-done.1, f32[256,128]{1,0:T(8,128)S(1)} %broadcast_in_dim.2.plf, bf16[272,256]{1,0:T(8,128)(2,1)S(1)} %get-tuple-element.31.noted.own), custom_call_target="tpu_custom_call" | custom-call | flops 1 | bytes 1 | tf_op jit(solution)/shard_map/weight_map/pallas_call | solution.py:49
  13.7 0.7 %collective-permute-done.4.refs_2_ = bf16[16,256]{1,0:T(8,128)(2,1)S(1)} collective-permute-done((bf16[16,256]{1,0:T(8,128)(2,1)S(1)}, bf16[16,256]{1,0:T(8,128)(2,1)S(1)}, u32[]{:S(2)}, u32[]{:S(2)}) %collective-permute-start.4) | collective-permute-done | bytes 8224 | tf_op jit(solution)/shard_map/ppermute | solution.py:28
  14.4 1.6 %collective-permute-done.1.across = bf16[256,256]{1,0:T(8,128)(2,1)S(1)} collective-permute-done((bf16[256,256]{1,0:T(8,128)(2,1)S(1)}, bf16[256,256]{1,0:T(8,128)(2,1)S(1)}, u32[]{:S(2)}, u32[]{:S(2)}) %collective-permute-start.1) | collective-permute-done | bytes 131104 | tf_op jit(solution)/shard_map/ppermute | solution.py:28
  16.5 1.6 %collective-permute-start.6 = (bf16[128,256]{1,0:T(8,128)(2,1)S(1)}, bf16[128,256]{1,0:T(8,128)(2,1)S(1)}, u32[]{:S(2)}, u32[]{:S(2)}) collective-permute-start(bf16[128,256]{1,0:T(8,128)(2,1)S(1)} %get-tuple-element.38), channel_id=1, source_target_pairs={{0,4},{2,6},{4,0},{6,2},{8,12},{10,14},{12,8},{14,10},{1,5},{3,7},... | collective-permute-start | bytes 196616 | tf_op jit(solution)/shard_map/ppermute | solution.py:28
  18.1 1.5 %collective-permute-start.7 = (bf16[128,256]{1,0:T(8,128)(2,1)S(1)}, bf16[128,256]{1,0:T(8,128)(2,1)S(1)}, u32[]{:S(2)}, u32[]{:S(2)}) collective-permute-start(bf16[128,256]{1,0:T(8,128)(2,1)S(1)} %get-tuple-element.39), channel_id=1, source_target_pairs={{0,2},{2,0},{4,6},{6,4},{8,10},{10,8},{12,14},{14,12},{1,3},{3,1},... | collective-permute-start | bytes 196616 | tf_op jit(solution)/shard_map/ppermute | solution.py:28
  19.9 1.8 %collective-permute-done.6.refs_1_ = bf16[128,256]{1,0:T(8,128)(2,1)S(1)} collective-permute-done((bf16[128,256]{1,0:T(8,128)(2,1)S(1)}, bf16[128,256]{1,0:T(8,128)(2,1)S(1)}, u32[]{:S(2)}, u32[]{:S(2)}) %collective-permute-start.6) | collective-permute-done | bytes 65568 | tf_op jit(solution)/shard_map/ppermute | solution.py:28
  21.7 0.9 %collective-permute-done.7.refs_2_ = bf16[128,256]{1,0:T(8,128)(2,1)S(1)} collective-permute-done((bf16[128,256]{1,0:T(8,128)(2,1)S(1)}, bf16[128,256]{1,0:T(8,128)(2,1)S(1)}, u32[]{:S(2)}, u32[]{:S(2)}) %collective-permute-start.7) | collective-permute-done | bytes 65568 | tf_op jit(solution)/shard_map/ppermute | solution.py:28
  23.2 1.1 %collective-permute-done.8.theirs = f32[1,256]{1,0:T(1,128)S(1)} collective-permute-done((f32[1,256]{1,0:T(1,128)S(1)}, f32[1,256]{1,0:T(1,128)S(1)}, u32[]{:S(2)}, u32[]{:S(2)}) %collective-permute-start.8) | collective-permute-done | bytes 1056 | tf_op jit(solution)/shard_map/ppermute | solution.py:24
  24.3 0.9 %gate.1 = (bf16[256,256]{1,0:T(8,128)(2,1)S(1)}, bf16[128,256]{1,0:T(8,128)(2,1)S(1)}, bf16[128,256]{1,0:T(8,128)(2,1)S(1)}, bf16[128,256]{1,0:T(8,128)(2,1)S(1)}) custom-call(f32[256,256]{1,0:T(8,128)S(1)} %get-tuple-element.41.ratio, f32[256,256]{1,0:T(8,128)S(1)} %get-tuple-element.42.rel, f32[256,128]{1,0:T(8,128)S(1)} %get-tuple-element.43.own_sum, ...), custom_call_target="tpu_custom_call" | custom-call | flops 1 | bytes 1 | tf_op jit(solution)/shard_map/gate/pallas_call | solution.py:49
  25.2 2.7 %collective-permute-start.9 = (bf16[256,256]{1,0:T(8,128)(2,1)S(1)}, bf16[256,256]{1,0:T(8,128)(2,1)S(1)}, u32[]{:S(2)}, u32[]{:S(2)}) collective-permute-start(bf16[256,256]{1,0:T(8,128)(2,1)S(1)} %get-tuple-element.46.gate), channel_id=1, source_target_pairs={{0,12},{2,14},{4,8},{6,10},{8,4},{10,6},{12,0},{14,2},{1,13},{3,15... | collective-permute-start | bytes 393224 | tf_op jit(solution)/shard_map/ppermute | solution.py:28
  27.9 2.5 %collective-permute-start.11 = (bf16[128,256]{1,0:T(8,128)(2,1)S(1)}, bf16[128,256]{1,0:T(8,128)(2,1)S(1)}, u32[]{:S(2)}, u32[]{:S(2)}) collective-permute-start(bf16[128,256]{1,0:T(8,128)(2,1)S(1)} %get-tuple-element.48), channel_id=1, source_target_pairs={{0,4},{2,6},{4,0},{6,2},{8,12},{10,14},{12,8},{14,10},{1,5},{3,7},... | collective-permute-start | bytes 196616 | tf_op jit(solution)/shard_map/ppermute | solution.py:28
  30.4 1.0 %collective-permute-start.12 = (bf16[128,256]{1,0:T(8,128)(2,1)S(1)}, bf16[128,256]{1,0:T(8,128)(2,1)S(1)}, u32[]{:S(2)}, u32[]{:S(2)}) collective-permute-start(bf16[128,256]{1,0:T(8,128)(2,1)S(1)} %get-tuple-element.49), channel_id=1, source_target_pairs={{0,2},{2,0},{4,6},{6,4},{8,10},{10,8},{12,14},{14,12},{1,3},{3,1},... | collective-permute-start | bytes 196616 | tf_op jit(solution)/shard_map/ppermute | solution.py:28
  31.4 2.0 %collective-permute-done.9.across = bf16[256,256]{1,0:T(8,128)(2,1)S(1)} collective-permute-done((bf16[256,256]{1,0:T(8,128)(2,1)S(1)}, bf16[256,256]{1,0:T(8,128)(2,1)S(1)}, u32[]{:S(2)}, u32[]{:S(2)}) %collective-permute-start.9) | collective-permute-done | bytes 131104 | tf_op jit(solution)/shard_map/ppermute | solution.py:28
  33.4 0.9 %collective-permute-start.13 = (bf16[128,256]{1,0:T(8,128)(2,1)S(1)}, bf16[128,256]{1,0:T(8,128)(2,1)S(1)}, u32[]{:S(2)}, u32[]{:S(2)}) collective-permute-start(bf16[128,256]{1,0:T(8,128)(2,1)S(1)} %get-tuple-element.50), channel_id=1, source_target_pairs={{0,6},{2,4},{4,2},{6,0},{8,14},{10,12},{12,10},{14,8},{1,7},{3,5},... | collective-permute-start | bytes 196616 | tf_op jit(solution)/shard_map/ppermute | solution.py:28
  34.4 0.8 %collective-permute-start.14 = (bf16[128,256]{1,0:T(8,128)(2,1)S(1)}, bf16[128,256]{1,0:T(8,128)(2,1)S(1)}, u32[]{:S(2)}, u32[]{:S(2)}) collective-permute-start(bf16[128,256]{1,0:T(8,128)(2,1)S(1)} %get-tuple-element.51), channel_id=1, source_target_pairs={{0,2},{2,0},{4,6},{6,4},{8,10},{10,8},{12,14},{14,12},{1,3},{3,1},... | collective-permute-start | bytes 196616 | tf_op jit(solution)/shard_map/ppermute | solution.py:28
  35.1 1.9 %collective-permute-start.15 = (bf16[128,256]{1,0:T(8,128)(2,1)S(1)}, bf16[128,256]{1,0:T(8,128)(2,1)S(1)}, u32[]{:S(2)}, u32[]{:S(2)}) collective-permute-start(bf16[128,256]{1,0:T(8,128)(2,1)S(1)} %get-tuple-element.52), channel_id=1, source_target_pairs={{0,4},{2,6},{4,0},{6,2},{8,12},{10,14},{12,8},{14,10},{1,5},{3,7},... | collective-permute-start | bytes 196616 | tf_op jit(solution)/shard_map/ppermute | solution.py:28
  37.5 1.6 %collective-permute-done.13.refs_0_ = bf16[128,256]{1,0:T(8,128)(2,1)S(1)} collective-permute-done((bf16[128,256]{1,0:T(8,128)(2,1)S(1)}, bf16[128,256]{1,0:T(8,128)(2,1)S(1)}, u32[]{:S(2)}, u32[]{:S(2)}) %collective-permute-start.13) | collective-permute-done | bytes 65568 | tf_op jit(solution)/shard_map/ppermute | solution.py:28
  40.1 1.1 %collective-permute-done.16.theirs = f32[1,256]{1,0:T(1,128)S(1)} collective-permute-done((f32[1,256]{1,0:T(1,128)S(1)}, f32[1,256]{1,0:T(1,128)S(1)}, u32[]{:S(2)}, u32[]{:S(2)}) %collective-permute-start.16) | collective-permute-done | bytes 1056 | tf_op jit(solution)/shard_map/ppermute | solution.py:24
  41.2 1.5 %copy_number.1 = f32[256,256]{1,0:T(8,128)} custom-call(f32[256,256]{1,0:T(8,128)S(1)} %get-tuple-element.53.ratio, f32[256,256]{1,0:T(8,128)S(1)} %get-tuple-element.54.rel, f32[256,128]{1,0:T(8,128)S(1)} %get-tuple-element.55.own_sum, f32[1,256]{1,0:T(1,128)S(1)} %collective-permute-done.16.theirs, f32[256,128]{1,0:T(8,128)S(1)} %get-tuple-element.45.inverse), custom_call_target="tpu_custom_call" | custom-call | flops 1 | bytes 1 | tf_op jit(solution)/shard_map/copy_number/pallas_call | solution.py:49
  (34 shorter events, 5.1 us)
Async XLA Ops:
  0.0 0.9 %copy-start.2 = (s32[256]{0:T(256)S(1)}, s32[256]{0:T(256)}, u32[]{:S(2)}) copy-start(s32[256]{0:T(256)} %param.9) | copy-start | bytes 3076
  0.9 0.9 %copy-start = (s32[256,128]{1,0:T(8,128)S(1)}, s32[256,128]{1,0:T(8,128)}, u32[]{:S(2)}) copy-start(s32[256,128]{1,0:T(8,128)} %neighbours.3) | copy-start | bytes 393220
  1.1 1.3 %collective-permute-start = (f32[8,384]{1,0:T(8,128)S(1)}, f32[8,384]{1,0:T(8,128)S(1)}, u32[]{:S(2)}, u32[]{:S(2)}) collective-permute-start(f32[8,384]{1,0:T(8,128)S(1)} %bin_sums.1.mine), channel_id=1, source_target_pairs={{0,1},{1,0},{2,3},{3,2},{4,5},{5,4},{6,7},{7,6},{8,9},{9,8},{10,11... | collective-permute-start | bytes 36872 | tf_op jit(solution)/shard_map/ppermute | solution.py:24
  2.7 7.5 %copy-start.3 = (s32[256]{0:T(256)S(1)}, s32[256]{0:T(256)}, u32[]{:S(2)}) copy-start(s32[256]{0:T(256)} %param.8) | copy-start | bytes 3076
  2.8 13.2 %collective-permute-start.3 = (bf16[272,256]{1,0:T(8,128)(2,1)S(1)}, bf16[272,256]{1,0:T(8,128)(2,1)S(1)}, u32[]{:S(2)}, u32[]{:S(2)}) collective-permute-start(bf16[272,256]{1,0:T(8,128)(2,1)S(1)} %get-tuple-element.31.noted.own), channel_id=1, source_target_pairs={{0,4},{2,6},{4,0},{6,2},{8,12},{10,14},{12,8},{14,10},{1,5},{3,7},... | collective-permute-start | bytes 417800 | tf_op jit(solution)/shard_map/ppermute | solution.py:28
  5.7 10.2 %collective-permute-start.2 = (bf16[272,256]{1,0:T(8,128)(2,1)S(1)}, bf16[272,256]{1,0:T(8,128)(2,1)S(1)}, u32[]{:S(2)}, u32[]{:S(2)}) collective-permute-start(bf16[272,256]{1,0:T(8,128)(2,1)S(1)} %get-tuple-element.31.noted.own), channel_id=1, source_target_pairs={{0,2},{2,0},{4,6},{6,4},{8,10},{10,8},{12,14},{14,12},{1,3},{3,1},... | collective-permute-start | bytes 417800 | tf_op jit(solution)/shard_map/ppermute | solution.py:28
  7.3 8.7 %collective-permute-start.1 = (bf16[256,256]{1,0:T(8,128)(2,1)S(1)}, bf16[256,256]{1,0:T(8,128)(2,1)S(1)}, u32[]{:S(2)}, u32[]{:S(2)}) collective-permute-start(bf16[256,256]{1,0:T(8,128)(2,1)S(1)} %get-tuple-element.34), channel_id=1, source_target_pairs={{0,8},{2,10},{4,12},{6,14},{8,0},{10,2},{12,4},{14,6},{1,9},{3,11}... | collective-permute-start | bytes 393224 | tf_op jit(solution)/shard_map/ppermute | solution.py:28
  9.8 4.5 %collective-permute-start.4 = (bf16[16,256]{1,0:T(8,128)(2,1)S(1)}, bf16[16,256]{1,0:T(8,128)(2,1)S(1)}, u32[]{:S(2)}, u32[]{:S(2)}) collective-permute-start(bf16[16,256]{1,0:T(8,128)(2,1)S(1)} %choices.1.ask), channel_id=1, source_target_pairs={{0,6},{2,4},{4,2},{6,0},{8,14},{10,12},{12,10},{14,8},{1,7},{3,5},... | collective-permute-start | bytes 24584 | tf_op jit(solution)/shard_map/ppermute | solution.py:28
  10.2 0.8 %copy-start.1 = (bf16[256,128]{1,0:T(8,128)(2,1)S(1)}, bf16[256,128]{1,0:T(8,128)(2,1)}, u32[]{:S(2)}) copy-start(bf16[256,128]{1,0:T(8,128)(2,1)} %weight.1) | copy-start | bytes 196612
  16.0 6.6 %collective-permute-start.5 = (bf16[256,256]{1,0:T(8,128)(2,1)S(1)}, bf16[256,256]{1,0:T(8,128)(2,1)S(1)}, u32[]{:S(2)}, u32[]{:S(2)}) collective-permute-start(bf16[256,256]{1,0:T(8,128)(2,1)S(1)} %get-tuple-element.37), channel_id=1, source_target_pairs={{0,6},{2,4},{4,2},{6,0},{8,14},{10,12},{12,10},{14,8},{1,7},{3,5},... | collective-permute-start | bytes 393224 | tf_op jit(solution)/shard_map/ppermute | solution.py:28
  16.5 5.2 %collective-permute-start.6 = (bf16[128,256]{1,0:T(8,128)(2,1)S(1)}, bf16[128,256]{1,0:T(8,128)(2,1)S(1)}, u32[]{:S(2)}, u32[]{:S(2)}) collective-permute-start(bf16[128,256]{1,0:T(8,128)(2,1)S(1)} %get-tuple-element.38), channel_id=1, source_target_pairs={{0,4},{2,6},{4,0},{6,2},{8,12},{10,14},{12,8},{14,10},{1,5},{3,7},... | collective-permute-start | bytes 196616 | tf_op jit(solution)/shard_map/ppermute | solution.py:28
  18.1 4.6 %collective-permute-start.7 = (bf16[128,256]{1,0:T(8,128)(2,1)S(1)}, bf16[128,256]{1,0:T(8,128)(2,1)S(1)}, u32[]{:S(2)}, u32[]{:S(2)}) collective-permute-start(bf16[128,256]{1,0:T(8,128)(2,1)S(1)} %get-tuple-element.39), channel_id=1, source_target_pairs={{0,2},{2,0},{4,6},{6,4},{8,10},{10,8},{12,14},{14,12},{1,3},{3,1},... | collective-permute-start | bytes 196616 | tf_op jit(solution)/shard_map/ppermute | solution.py:28
  23.1 1.2 %collective-permute-start.8 = (f32[1,256]{1,0:T(1,128)S(1)}, f32[1,256]{1,0:T(1,128)S(1)}, u32[]{:S(2)}, u32[]{:S(2)}) collective-permute-start(f32[1,256]{1,0:T(1,128)S(1)} %get-tuple-element.44), channel_id=1, source_target_pairs={{0,1},{1,0},{2,3},{3,2},{4,5},{5,4},{6,7},{7,6},{8,9},{9,8},{10,11... | collective-permute-start | bytes 3080 | tf_op jit(solution)/shard_map/ppermute | solution.py:24
  25.2 8.2 %collective-permute-start.9 = (bf16[256,256]{1,0:T(8,128)(2,1)S(1)}, bf16[256,256]{1,0:T(8,128)(2,1)S(1)}, u32[]{:S(2)}, u32[]{:S(2)}) collective-permute-start(bf16[256,256]{1,0:T(8,128)(2,1)S(1)} %get-tuple-element.46.gate), channel_id=1, source_target_pairs={{0,12},{2,14},{4,8},{6,10},{8,4},{10,6},{12,0},{14,2},{1,13},{3,15... | collective-permute-start | bytes 393224 | tf_op jit(solution)/shard_map/ppermute | solution.py:28
  27.9 7.2 %collective-permute-start.10 = (bf16[128,256]{1,0:T(8,128)(2,1)S(1)}, bf16[128,256]{1,0:T(8,128)(2,1)S(1)}, u32[]{:S(2)}, u32[]{:S(2)}) collective-permute-start(bf16[128,256]{1,0:T(8,128)(2,1)S(1)} %get-tuple-element.47), channel_id=1, source_target_pairs={{0,6},{2,4},{4,2},{6,0},{8,14},{10,12},{12,10},{14,8},{1,7},{3,5},... | collective-permute-start | bytes 196616 | tf_op jit(solution)/shard_map/ppermute | solution.py:28
  27.9 9.1 %collective-permute-start.11 = (bf16[128,256]{1,0:T(8,128)(2,1)S(1)}, bf16[128,256]{1,0:T(8,128)(2,1)S(1)}, u32[]{:S(2)}, u32[]{:S(2)}) collective-permute-start(bf16[128,256]{1,0:T(8,128)(2,1)S(1)} %get-tuple-element.48), channel_id=1, source_target_pairs={{0,4},{2,6},{4,0},{6,2},{8,12},{10,14},{12,8},{14,10},{1,5},{3,7},... | collective-permute-start | bytes 196616 | tf_op jit(solution)/shard_map/ppermute | solution.py:28
  30.4 6.6 %collective-permute-start.12 = (bf16[128,256]{1,0:T(8,128)(2,1)S(1)}, bf16[128,256]{1,0:T(8,128)(2,1)S(1)}, u32[]{:S(2)}, u32[]{:S(2)}) collective-permute-start(bf16[128,256]{1,0:T(8,128)(2,1)S(1)} %get-tuple-element.49), channel_id=1, source_target_pairs={{0,2},{2,0},{4,6},{6,4},{8,10},{10,8},{12,14},{14,12},{1,3},{3,1},... | collective-permute-start | bytes 196616 | tf_op jit(solution)/shard_map/ppermute | solution.py:28
  33.4 5.7 %collective-permute-start.13 = (bf16[128,256]{1,0:T(8,128)(2,1)S(1)}, bf16[128,256]{1,0:T(8,128)(2,1)S(1)}, u32[]{:S(2)}, u32[]{:S(2)}) collective-permute-start(bf16[128,256]{1,0:T(8,128)(2,1)S(1)} %get-tuple-element.50), channel_id=1, source_target_pairs={{0,6},{2,4},{4,2},{6,0},{8,14},{10,12},{12,10},{14,8},{1,7},{3,5},... | collective-permute-start | bytes 196616 | tf_op jit(solution)/shard_map/ppermute | solution.py:28
  34.4 5.0 %collective-permute-start.14 = (bf16[128,256]{1,0:T(8,128)(2,1)S(1)}, bf16[128,256]{1,0:T(8,128)(2,1)S(1)}, u32[]{:S(2)}, u32[]{:S(2)}) collective-permute-start(bf16[128,256]{1,0:T(8,128)(2,1)S(1)} %get-tuple-element.51), channel_id=1, source_target_pairs={{0,2},{2,0},{4,6},{6,4},{8,10},{10,8},{12,14},{14,12},{1,3},{3,1},... | collective-permute-start | bytes 196616 | tf_op jit(solution)/shard_map/ppermute | solution.py:28
  35.1 4.5 %collective-permute-start.15 = (bf16[128,256]{1,0:T(8,128)(2,1)S(1)}, bf16[128,256]{1,0:T(8,128)(2,1)S(1)}, u32[]{:S(2)}, u32[]{:S(2)}) collective-permute-start(bf16[128,256]{1,0:T(8,128)(2,1)S(1)} %get-tuple-element.52), channel_id=1, source_target_pairs={{0,4},{2,6},{4,0},{6,2},{8,12},{10,14},{12,8},{14,10},{1,5},{3,7},... | collective-permute-start | bytes 196616 | tf_op jit(solution)/shard_map/ppermute | solution.py:28
  40.0 1.2 %collective-permute-start.16 = (f32[1,256]{1,0:T(1,128)S(1)}, f32[1,256]{1,0:T(1,128)S(1)}, u32[]{:S(2)}, u32[]{:S(2)}) collective-permute-start(f32[1,256]{1,0:T(1,128)S(1)} %get-tuple-element.56), channel_id=1, source_target_pairs={{0,1},{1,0},{2,3},{3,2},{4,5},{5,4},{6,7},{7,6},{8,9},{9,8},{10,11... | collective-permute-start | bytes 3080 | tf_op jit(solution)/shard_map/ppermute | solution.py:24

commit v9 on v8

--- a/solution.py
+++ b/solution.py
@@ -217,25 +217,40 @@
     partial[1] = dot(mine, squared(block), 1, 0)
 
 
-def first_kernel(late, rows, weight, total, own, early, partial, *refs):
-    mates = len(refs) - 5
-    half = mates + 1
-    order, (table, ratio, rel, own_sum, part) = order_of(PASSED, half), refs[mates:]
-    cols = own.shape[1]
-    table[...] = early[...]
-    arrived = []
+def arrivals(late, order, half, refs):
+    found = []
     for k, ref in zip(order, refs):
         if k in late:
-            arrived.append(k)
-            table[k * RBLK : (k + 1) * RBLK] = ref[RBLK : 2 * RBLK]
-        other = k ^ block_across(half)
-        arrived.append(other)
-        table[other * RBLK : (other + 1) * RBLK] = ref[0:RBLK]
-    mine, block = columns(weight, arrived), place(table, arrived)
-    second = partial[0] + dot(mine, block, 1, 0)
-    third = partial[1] + dot(mine, squared(block), 1, 0)
-    first = jnp.concatenate([total[...]] * (cols // LANE), axis=1)
-    spread(first, second, third, own[0:rows].astype(F32), ratio, rel, own_sum, part)
+            found.append((k, ref[RBLK : 2 * RBLK]))
+        found.append((k ^ block_across(half), ref[0:RBLK]))
+    return zip(*found)
+
+
+def add_kernel(late, order, half, weight, early, before, *refs):
+    passed, (table, partial) = refs[:-2], refs[-2:]
+    positions, blocks = arrivals(late, order, half, passed)
+    table[...] = early[...]
+    for p, block in zip(positions, blocks):
+        table[p * RBLK : (p + 1) * RBLK] = block
+    mine, block = columns(weight, positions), jnp.concatenate(blocks, axis=0)
+    partial[0] = before[0] + dot(mine, block, 1, 0)
+    partial[1] = before[1] + dot(mine, squared(block), 1, 0)
+
+
+def first_kernel(late, order, half, rows, weight, total, own, before, passed, *refs):
+    positions, blocks = arrivals(late, order, half, [passed])
+    mine, block = columns(weight, positions), jnp.concatenate(blocks, axis=0)
+    second = before[0] + dot(mine, block, 1, 0)
+    third = before[1] + dot(mine, squared(block), 1, 0)
+    first = jnp.concatenate([total[...]] * (own.shape[1] // LANE), axis=1)
+    spread(first, second, third, own[0:rows].astype(F32), *refs)
+
+
+def fill_kernel(late, order, half, early, passed, ratio, table):
+    positions, blocks = arrivals(late, order, half, [passed])
+    table[...] = early[...]
+    for p, block in zip(positions, blocks):
+        table[p * RBLK : (p + 1) * RBLK] = block
 
 
 def gated(weight, table, gates, positions):
@@ -379,10 +394,21 @@
         [((count * RBLK, cols), BF16), ((2, rows, cols), F32)],
         weight, own, across, ask, *noted,
     )
-    table, ratio, rel, own_sum, part = call(
-        functools.partial(first_kernel, late, rows), "moments_one",
-        [((count * RBLK, cols), BF16)] + spreads,
-        weight, total, own, table, partial, *[passed[k - 1] for k in order_of(PASSED, half)],
+    order = order_of(PASSED, half)
+    passed = [passed[k - 1] for k in order]
+    if len(order) > 1:
+        table, partial = call(
+            functools.partial(add_kernel, late, order[:-1], half), "more_moments_one",
+            [((count * RBLK, cols), BF16), ((2, rows, cols), F32)],
+            weight, table, partial, *passed[:-1],
+        )
+    ratio, rel, own_sum, part = call(
+        functools.partial(first_kernel, late, order[-1:], half, rows), "moments_one", spreads,
+        weight, total, own, partial, passed[-1],
+    )
+    (table,) = call(
+        functools.partial(fill_kernel, late, order[-1:], half), "fill_table",
+        [((count * RBLK, cols), BF16)], table, passed[-1], own_sum,
     )
     order = order_of(OWN_GATES, half)
     gate, *gates = call(

time: 42.9 us -> 43 us (level)
    pallas_call x13 -> x15, Pallas kernels: 7.82 us -> 8.05 us  [call(): pl.pallas_call(body, out_shape=[jax.ShapeDtypeStruct(shape, dtype) for sh...]
  transfers between devices with their start and end apart: 17 -> 17, of which waited for: 10 -> 11; matrix products, arithmetic and copies ran while one was open for 0% -> 0% of each run, Pallas kernels for 10% -> 11%
where the time goes in v9:
time: 43 us; the launch traced here: 42.8 us
  starting transfers between devices  21.4 us (50%)
  waiting for transfers between devices  11.1 us (26%)
  Pallas kernels  8.05 us (19%)
  local copies, waits for them, and re-layouts  2.02 us (5%)
    ppermute x14, starting transfers between devices, send(): return lax.ppermute(value, 'samp', [(i, i ^ step) for i in range(count)])  20.8 us
    ppermute x14, waiting for transfers between devices, send(): return lax.ppermute(value, 'samp', [(i, i ^ step) for i in range(count)])  8.67 us
    pallas_call x15, Pallas kernels, call(): pl.pallas_call(body, out_shape=[jax.ShapeDtypeStruct(shape, dtype) for sh...  8.05 us
    ppermute x3, waiting for transfers between devices, swap_tgt(): return lax.ppermute(value, 'tgt', [(0, 1), (1, 0)])  2.45 us
    unnamed x8, local copies, waits for them, and re-layouts  1 us
    pad x1, local copies, waits for them, and re-layouts, body(): counted = jnp.pad(coverage, ((0, LANE), (0, 0)), constant_values=1)  0.93 us
  transfers between devices with their start and end apart: 17, of which 11 were waited for; matrix products, arithmetic and copies ran while one was open for 0% of the time, Pallas kernels for 11%

profile of v9, /device:TPU:0, one launch (start us, length us, event | category | flops | bytes accessed | tf_op | source)
XLA Modules:
  0.0 42.8 jit_solution(6420390869496824013)
XLA Ops:
  0.0 0.9 %pad.4.coverage = bf16[384,256]{1,0:T(8,128)(2,1)S(1)} pad(bf16[256,256]{1,0:T(8,128)(2,1)} %param.5, bf16[]{:T(256)} %constant.2.clone.1), padding=0_128x0_0 | pad | bytes 327682 | tf_op jit(solution)/shard_map/jit(_pad)/pad | solution.py:364
  2.7 3.0 %collective-permute-start.3 = (bf16[272,256]{1,0:T(8,128)(2,1)S(1)}, bf16[272,256]{1,0:T(8,128)(2,1)S(1)}, u32[]{:S(2)}, u32[]{:S(2)}) collective-permute-start(bf16[272,256]{1,0:T(8,128)(2,1)S(1)} %get-tuple-element.32.noted.own), channel_id=1, source_target_pairs={{0,4},{2,6},{4,0},{6,2},{8,12},{10,14},{12,8},{14,10},{1,5},{3,7},... | collective-permute-start | bytes 417800 | tf_op jit(solution)/shard_map/ppermute | solution.py:28
  5.7 1.5 %collective-permute-start.2 = (bf16[272,256]{1,0:T(8,128)(2,1)S(1)}, bf16[272,256]{1,0:T(8,128)(2,1)S(1)}, u32[]{:S(2)}, u32[]{:S(2)}) collective-permute-start(bf16[272,256]{1,0:T(8,128)(2,1)S(1)} %get-tuple-element.32.noted.own), channel_id=1, source_target_pairs={{0,2},{2,0},{4,6},{6,4},{8,10},{10,8},{12,14},{14,12},{1,3},{3,1},... | collective-permute-start | bytes 417800 | tf_op jit(solution)/shard_map/ppermute | solution.py:28
  7.3 2.6 %collective-permute-start.1 = (bf16[256,256]{1,0:T(8,128)(2,1)S(1)}, bf16[256,256]{1,0:T(8,128)(2,1)S(1)}, u32[]{:S(2)}, u32[]{:S(2)}) collective-permute-start(bf16[256,256]{1,0:T(8,128)(2,1)S(1)} %get-tuple-element.34), channel_id=1, source_target_pairs={{0,8},{2,10},{4,12},{6,14},{8,0},{10,2},{12,4},{14,6},{1,9},{3,11}... | collective-permute-start | bytes 393224 | tf_op jit(solution)/shard_map/ppermute | solution.py:28
  10.3 0.7 %copy-done.1 = bf16[256,128]{1,0:T(8,128)(2,1)S(1)} copy-done((bf16[256,128]{1,0:T(8,128)(2,1)S(1)}, bf16[256,128]{1,0:T(8,128)(2,1)}, u32[]{:S(2)}) %copy-start.1) | copy-done | bytes 65560
  11.1 2.6 %weight_map.1 = (bf16[256,1024]{1,0:T(8,128)(2,1)S(1)}, f32[256,128]{1,0:T(8,128)S(1)}, f32[256,128]{1,0:T(8,128)S(1)}) custom-call(s32[256,128]{1,0:T(8,128)S(1)} %copy-done, bf16[256,128]{1,0:T(8,128)(2,1)S(1)} %copy-done.1, f32[256,128]{1,0:T(8,128)S(1)} %broadcast_in_dim.2.plf, bf16[272,256]{1,0:T(8,128)(2,1)S(1)} %get-tuple-element.32.noted.own), custom_call_target="tpu_custom_call" | custom-call | flops 1 | bytes 1 | tf_op jit(solution)/shard_map/weight_map/pallas_call | solution.py:49
  13.7 0.7 %collective-permute-done.4.refs_2_ = bf16[16,256]{1,0:T(8,128)(2,1)S(1)} collective-permute-done((bf16[16,256]{1,0:T(8,128)(2,1)S(1)}, bf16[16,256]{1,0:T(8,128)(2,1)S(1)}, u32[]{:S(2)}, u32[]{:S(2)}) %collective-permute-start.4) | collective-permute-done | bytes 8224 | tf_op jit(solution)/shard_map/ppermute | solution.py:28
  14.4 1.6 %collective-permute-done.1.across = bf16[256,256]{1,0:T(8,128)(2,1)S(1)} collective-permute-done((bf16[256,256]{1,0:T(8,128)(2,1)S(1)}, bf16[256,256]{1,0:T(8,128)(2,1)S(1)}, u32[]{:S(2)}, u32[]{:S(2)}) %collective-permute-start.1) | collective-permute-done | bytes 131104 | tf_op jit(solution)/shard_map/ppermute | solution.py:28
  16.5 1.6 %collective-permute-start.6 = (bf16[128,256]{1,0:T(8,128)(2,1)S(1)}, bf16[128,256]{1,0:T(8,128)(2,1)S(1)}, u32[]{:S(2)}, u32[]{:S(2)}) collective-permute-start(bf16[128,256]{1,0:T(8,128)(2,1)S(1)} %get-tuple-element.39), channel_id=1, source_target_pairs={{0,4},{2,6},{4,0},{6,2},{8,12},{10,14},{12,8},{14,10},{1,5},{3,7},... | collective-permute-start | bytes 196616 | tf_op jit(solution)/shard_map/ppermute | solution.py:28
  18.1 1.5 %collective-permute-start.7 = (bf16[128,256]{1,0:T(8,128)(2,1)S(1)}, bf16[128,256]{1,0:T(8,128)(2,1)S(1)}, u32[]{:S(2)}, u32[]{:S(2)}) collective-permute-start(bf16[128,256]{1,0:T(8,128)(2,1)S(1)} %get-tuple-element.41), channel_id=1, source_target_pairs={{0,2},{2,0},{4,6},{6,4},{8,10},{10,8},{12,14},{14,12},{1,3},{3,1},... | collective-permute-start | bytes 196616 | tf_op jit(solution)/shard_map/ppermute | solution.py:28
  19.9 1.8 %collective-permute-done.6.refs_1_ = bf16[128,256]{1,0:T(8,128)(2,1)S(1)} collective-permute-done((bf16[128,256]{1,0:T(8,128)(2,1)S(1)}, bf16[128,256]{1,0:T(8,128)(2,1)S(1)}, u32[]{:S(2)}, u32[]{:S(2)}) %collective-permute-start.6) | collective-permute-done | bytes 65568 | tf_op jit(solution)/shard_map/ppermute | solution.py:28
  23.0 1.1 %collective-permute-done.8.theirs = f32[1,256]{1,0:T(1,128)S(1)} collective-permute-done((f32[1,256]{1,0:T(1,128)S(1)}, f32[1,256]{1,0:T(1,128)S(1)}, u32[]{:S(2)}, u32[]{:S(2)}) %collective-permute-start.8) | collective-permute-done | bytes 1056 | tf_op jit(solution)/shard_map/ppermute | solution.py:24
  24.2 0.9 %gate.1 = (bf16[256,256]{1,0:T(8,128)(2,1)S(1)}, bf16[128,256]{1,0:T(8,128)(2,1)S(1)}, bf16[128,256]{1,0:T(8,128)(2,1)S(1)}, bf16[128,256]{1,0:T(8,128)(2,1)S(1)}) custom-call(f32[256,256]{1,0:T(8,128)S(1)} %get-tuple-element.44.ratio, f32[256,256]{1,0:T(8,128)S(1)} %get-tuple-element.45.rel, f32[256,128]{1,0:T(8,128)S(1)} %get-tuple-element.43.ratio.own_sum, ...), custom_call_target="tpu_custom_call" | custom-call | flops 1 | bytes 1 | tf_op jit(solution)/shard_map/gate/pallas_call | solution.py:49
  25.0 2.7 %collective-permute-start.9 = (bf16[256,256]{1,0:T(8,128)(2,1)S(1)}, bf16[256,256]{1,0:T(8,128)(2,1)S(1)}, u32[]{:S(2)}, u32[]{:S(2)}) collective-permute-start(bf16[256,256]{1,0:T(8,128)(2,1)S(1)} %get-tuple-element.48.gate), channel_id=1, source_target_pairs={{0,12},{2,14},{4,8},{6,10},{8,4},{10,6},{12,0},{14,2},{1,13},{3,15... | collective-permute-start | bytes 393224 | tf_op jit(solution)/shard_map/ppermute | solution.py:28
  27.8 2.5 %collective-permute-start.11 = (bf16[128,256]{1,0:T(8,128)(2,1)S(1)}, bf16[128,256]{1,0:T(8,128)(2,1)S(1)}, u32[]{:S(2)}, u32[]{:S(2)}) collective-permute-start(bf16[128,256]{1,0:T(8,128)(2,1)S(1)} %get-tuple-element.50), channel_id=1, source_target_pairs={{0,4},{2,6},{4,0},{6,2},{8,12},{10,14},{12,8},{14,10},{1,5},{3,7},... | collective-permute-start | bytes 196616 | tf_op jit(solution)/shard_map/ppermute | solution.py:28
  30.3 1.0 %collective-permute-start.12 = (bf16[128,256]{1,0:T(8,128)(2,1)S(1)}, bf16[128,256]{1,0:T(8,128)(2,1)S(1)}, u32[]{:S(2)}, u32[]{:S(2)}) collective-permute-start(bf16[128,256]{1,0:T(8,128)(2,1)S(1)} %get-tuple-element.51), channel_id=1, source_target_pairs={{0,2},{2,0},{4,6},{6,4},{8,10},{10,8},{12,14},{14,12},{1,3},{3,1},... | collective-permute-start | bytes 196616 | tf_op jit(solution)/shard_map/ppermute | solution.py:28
  31.3 2.0 %collective-permute-done.9.across = bf16[256,256]{1,0:T(8,128)(2,1)S(1)} collective-permute-done((bf16[256,256]{1,0:T(8,128)(2,1)S(1)}, bf16[256,256]{1,0:T(8,128)(2,1)S(1)}, u32[]{:S(2)}, u32[]{:S(2)}) %collective-permute-start.9) | collective-permute-done | bytes 131104 | tf_op jit(solution)/shard_map/ppermute | solution.py:28
  33.3 1.2 %collective-permute-start.13 = (bf16[128,256]{1,0:T(8,128)(2,1)S(1)}, bf16[128,256]{1,0:T(8,128)(2,1)S(1)}, u32[]{:S(2)}, u32[]{:S(2)}) collective-permute-start(bf16[128,256]{1,0:T(8,128)(2,1)S(1)} %get-tuple-element.52), channel_id=1, source_target_pairs={{0,6},{2,4},{4,2},{6,0},{8,14},{10,12},{12,10},{14,8},{1,7},{3,5},... | collective-permute-start | bytes 196616 | tf_op jit(solution)/shard_map/ppermute | solution.py:28
  34.6 0.7 %collective-permute-start.14 = (bf16[128,256]{1,0:T(8,128)(2,1)S(1)}, bf16[128,256]{1,0:T(8,128)(2,1)S(1)}, u32[]{:S(2)}, u32[]{:S(2)}) collective-permute-start(bf16[128,256]{1,0:T(8,128)(2,1)S(1)} %get-tuple-element.53), channel_id=1, source_target_pairs={{0,2},{2,0},{4,6},{6,4},{8,10},{10,8},{12,14},{14,12},{1,3},{3,1},... | collective-permute-start | bytes 196616 | tf_op jit(solution)/shard_map/ppermute | solution.py:28
  35.2 1.7 %collective-permute-start.15 = (bf16[128,256]{1,0:T(8,128)(2,1)S(1)}, bf16[128,256]{1,0:T(8,128)(2,1)S(1)}, u32[]{:S(2)}, u32[]{:S(2)}) collective-permute-start(bf16[128,256]{1,0:T(8,128)(2,1)S(1)} %get-tuple-element.54), channel_id=1, source_target_pairs={{0,4},{2,6},{4,0},{6,2},{8,12},{10,14},{12,8},{14,10},{1,5},{3,7},... | collective-permute-start | bytes 196616 | tf_op jit(solution)/shard_map/ppermute | solution.py:28
  36.9 0.5 %early_moments_two.1.before = f32[3,256,256]{2,1,0:T(8,128)S(1)} custom-call(bf16[256,1024]{1,0:T(8,128)(2,1)S(1)} %get-tuple-element.33.weight, bf16[1024,256]{1,0:T(8,128)(2,1)S(1)} %fill_table.1.table, bf16[256,256]{1,0:T(8,128)(2,1)S(1)} %get-tuple-element.48.gate, bf16[256,256]{1,0:T(8,128)(2,1)S(1)} %collective-permute-done.9.across, ...), custom_call_target="tpu_custom_call" | custom-call | flops 1 | bytes 1 | tf_op jit(solution)/shard_map/early_moments_two/pallas_call | solution.py:49
  37.5 1.6 %collective-permute-done.13.refs_0_ = bf16[128,256]{1,0:T(8,128)(2,1)S(1)} collective-permute-done((bf16[128,256]{1,0:T(8,128)(2,1)S(1)}, bf16[128,256]{1,0:T(8,128)(2,1)S(1)}, u32[]{:S(2)}, u32[]{:S(2)}) %collective-permute-start.13) | collective-permute-done | bytes 65568 | tf_op jit(solution)/shard_map/ppermute | solution.py:28
  40.1 1.1 %collective-permute-done.16.theirs = f32[1,256]{1,0:T(1,128)S(1)} collective-permute-done((f32[1,256]{1,0:T(1,128)S(1)}, f32[1,256]{1,0:T(1,128)S(1)}, u32[]{:S(2)}, u32[]{:S(2)}) %collective-permute-start.16) | collective-permute-done | bytes 1056 | tf_op jit(solution)/shard_map/ppermute | solution.py:24
  41.3 1.5 %copy_number.1 = f32[256,256]{1,0:T(8,128)} custom-call(f32[256,256]{1,0:T(8,128)S(1)} %get-tuple-element.55.ratio, f32[256,256]{1,0:T(8,128)S(1)} %get-tuple-element.56.rel, f32[256,128]{1,0:T(8,128)S(1)} %get-tuple-element.57.own_sum, f32[1,256]{1,0:T(1,128)S(1)} %collective-permute-done.16.theirs, f32[256,128]{1,0:T(8,128)S(1)} %get-tuple-element.47.inverse), custom_call_target="tpu_custom_call" | custom-call | flops 1 | bytes 1 | tf_op jit(solution)/shard_map/copy_number/pallas_call | solution.py:49
  (36 shorter events, 5.6 us)
Async XLA Ops:
  0.0 0.9 %copy-start.2 = (s32[256]{0:T(256)S(1)}, s32[256]{0:T(256)}, u32[]{:S(2)}) copy-start(s32[256]{0:T(256)} %param.9) | copy-start | bytes 3076
  0.9 0.9 %copy-start = (s32[256,128]{1,0:T(8,128)S(1)}, s32[256,128]{1,0:T(8,128)}, u32[]{:S(2)}) copy-start(s32[256,128]{1,0:T(8,128)} %neighbours.3) | copy-start | bytes 393220
  1.1 1.3 %collective-permute-start = (f32[8,384]{1,0:T(8,128)S(1)}, f32[8,384]{1,0:T(8,128)S(1)}, u32[]{:S(2)}, u32[]{:S(2)}) collective-permute-start(f32[8,384]{1,0:T(8,128)S(1)} %bin_sums.1.mine), channel_id=1, source_target_pairs={{0,1},{1,0},{2,3},{3,2},{4,5},{5,4},{6,7},{7,6},{8,9},{9,8},{10,11... | collective-permute-start | bytes 36872 | tf_op jit(solution)/shard_map/ppermute | solution.py:24
  2.7 7.5 %copy-start.3 = (s32[256]{0:T(256)S(1)}, s32[256]{0:T(256)}, u32[]{:S(2)}) copy-start(s32[256]{0:T(256)} %param.8) | copy-start | bytes 3076
  2.7 13.2 %collective-permute-start.3 = (bf16[272,256]{1,0:T(8,128)(2,1)S(1)}, bf16[272,256]{1,0:T(8,128)(2,1)S(1)}, u32[]{:S(2)}, u32[]{:S(2)}) collective-permute-start(bf16[272,256]{1,0:T(8,128)(2,1)S(1)} %get-tuple-element.32.noted.own), channel_id=1, source_target_pairs={{0,4},{2,6},{4,0},{6,2},{8,12},{10,14},{12,8},{14,10},{1,5},{3,7},... | collective-permute-start | bytes 417800 | tf_op jit(solution)/shard_map/ppermute | solution.py:28
  5.7 10.2 %collective-permute-start.2 = (bf16[272,256]{1,0:T(8,128)(2,1)S(1)}, bf16[272,256]{1,0:T(8,128)(2,1)S(1)}, u32[]{:S(2)}, u32[]{:S(2)}) collective-permute-start(bf16[272,256]{1,0:T(8,128)(2,1)S(1)} %get-tuple-element.32.noted.own), channel_id=1, source_target_pairs={{0,2},{2,0},{4,6},{6,4},{8,10},{10,8},{12,14},{14,12},{1,3},{3,1},... | collective-permute-start | bytes 417800 | tf_op jit(solution)/shard_map/ppermute | solution.py:28
  7.3 8.7 %collective-permute-start.1 = (bf16[256,256]{1,0:T(8,128)(2,1)S(1)}, bf16[256,256]{1,0:T(8,128)(2,1)S(1)}, u32[]{:S(2)}, u32[]{:S(2)}) collective-permute-start(bf16[256,256]{1,0:T(8,128)(2,1)S(1)} %get-tuple-element.34), channel_id=1, source_target_pairs={{0,8},{2,10},{4,12},{6,14},{8,0},{10,2},{12,4},{14,6},{1,9},{3,11}... | collective-permute-start | bytes 393224 | tf_op jit(solution)/shard_map/ppermute | solution.py:28
  9.8 4.5 %collective-permute-start.4 = (bf16[16,256]{1,0:T(8,128)(2,1)S(1)}, bf16[16,256]{1,0:T(8,128)(2,1)S(1)}, u32[]{:S(2)}, u32[]{:S(2)}) collective-permute-start(bf16[16,256]{1,0:T(8,128)(2,1)S(1)} %choices.1.ask), channel_id=1, source_target_pairs={{0,6},{2,4},{4,2},{6,0},{8,14},{10,12},{12,10},{14,8},{1,7},{3,5},... | collective-permute-start | bytes 24584 | tf_op jit(solution)/shard_map/ppermute | solution.py:28
  10.2 0.8 %copy-start.1 = (bf16[256,128]{1,0:T(8,128)(2,1)S(1)}, bf16[256,128]{1,0:T(8,128)(2,1)}, u32[]{:S(2)}) copy-start(bf16[256,128]{1,0:T(8,128)(2,1)} %weight.1) | copy-start | bytes 196612
  16.0 6.0 %collective-permute-start.5 = (bf16[256,256]{1,0:T(8,128)(2,1)S(1)}, bf16[256,256]{1,0:T(8,128)(2,1)S(1)}, u32[]{:S(2)}, u32[]{:S(2)}) collective-permute-start(bf16[256,256]{1,0:T(8,128)(2,1)S(1)} %get-tuple-element.38), channel_id=1, source_target_pairs={{0,6},{2,4},{4,2},{6,0},{8,14},{10,12},{12,10},{14,8},{1,7},{3,5},... | collective-permute-start | bytes 393224 | tf_op jit(solution)/shard_map/ppermute | solution.py:28
  16.5 5.2 %collective-permute-start.6 = (bf16[128,256]{1,0:T(8,128)(2,1)S(1)}, bf16[128,256]{1,0:T(8,128)(2,1)S(1)}, u32[]{:S(2)}, u32[]{:S(2)}) collective-permute-start(bf16[128,256]{1,0:T(8,128)(2,1)S(1)} %get-tuple-element.39), channel_id=1, source_target_pairs={{0,4},{2,6},{4,0},{6,2},{8,12},{10,14},{12,8},{14,10},{1,5},{3,7},... | collective-permute-start | bytes 196616 | tf_op jit(solution)/shard_map/ppermute | solution.py:28
  18.1 4.6 %collective-permute-start.7 = (bf16[128,256]{1,0:T(8,128)(2,1)S(1)}, bf16[128,256]{1,0:T(8,128)(2,1)S(1)}, u32[]{:S(2)}, u32[]{:S(2)}) collective-permute-start(bf16[128,256]{1,0:T(8,128)(2,1)S(1)} %get-tuple-element.41), channel_id=1, source_target_pairs={{0,2},{2,0},{4,6},{6,4},{8,10},{10,8},{12,14},{14,12},{1,3},{3,1},... | collective-permute-start | bytes 196616 | tf_op jit(solution)/shard_map/ppermute | solution.py:28
  23.0 1.2 %collective-permute-start.8 = (f32[1,256]{1,0:T(1,128)S(1)}, f32[1,256]{1,0:T(1,128)S(1)}, u32[]{:S(2)}, u32[]{:S(2)}) collective-permute-start(f32[1,256]{1,0:T(1,128)S(1)} %get-tuple-element.46), channel_id=1, source_target_pairs={{0,1},{1,0},{2,3},{3,2},{4,5},{5,4},{6,7},{7,6},{8,9},{9,8},{10,11... | collective-permute-start | bytes 3080 | tf_op jit(solution)/shard_map/ppermute | solution.py:24
  25.0 8.2 %collective-permute-start.9 = (bf16[256,256]{1,0:T(8,128)(2,1)S(1)}, bf16[256,256]{1,0:T(8,128)(2,1)S(1)}, u32[]{:S(2)}, u32[]{:S(2)}) collective-permute-start(bf16[256,256]{1,0:T(8,128)(2,1)S(1)} %get-tuple-element.48.gate), channel_id=1, source_target_pairs={{0,12},{2,14},{4,8},{6,10},{8,4},{10,6},{12,0},{14,2},{1,13},{3,15... | collective-permute-start | bytes 393224 | tf_op jit(solution)/shard_map/ppermute | solution.py:28
  27.8 7.5 %collective-permute-start.10 = (bf16[128,256]{1,0:T(8,128)(2,1)S(1)}, bf16[128,256]{1,0:T(8,128)(2,1)S(1)}, u32[]{:S(2)}, u32[]{:S(2)}) collective-permute-start(bf16[128,256]{1,0:T(8,128)(2,1)S(1)} %get-tuple-element.49), channel_id=1, source_target_pairs={{0,6},{2,4},{4,2},{6,0},{8,14},{10,12},{12,10},{14,8},{1,7},{3,5},... | collective-permute-start | bytes 196616 | tf_op jit(solution)/shard_map/ppermute | solution.py:28
  27.8 9.2 %collective-permute-start.11 = (bf16[128,256]{1,0:T(8,128)(2,1)S(1)}, bf16[128,256]{1,0:T(8,128)(2,1)S(1)}, u32[]{:S(2)}, u32[]{:S(2)}) collective-permute-start(bf16[128,256]{1,0:T(8,128)(2,1)S(1)} %get-tuple-element.50), channel_id=1, source_target_pairs={{0,4},{2,6},{4,0},{6,2},{8,12},{10,14},{12,8},{14,10},{1,5},{3,7},... | collective-permute-start | bytes 196616 | tf_op jit(solution)/shard_map/ppermute | solution.py:28
  30.3 6.7 %collective-permute-start.12 = (bf16[128,256]{1,0:T(8,128)(2,1)S(1)}, bf16[128,256]{1,0:T(8,128)(2,1)S(1)}, u32[]{:S(2)}, u32[]{:S(2)}) collective-permute-start(bf16[128,256]{1,0:T(8,128)(2,1)S(1)} %get-tuple-element.51), channel_id=1, source_target_pairs={{0,2},{2,0},{4,6},{6,4},{8,10},{10,8},{12,14},{14,12},{1,3},{3,1},... | collective-permute-start | bytes 196616 | tf_op jit(solution)/shard_map/ppermute | solution.py:28
  33.3 5.7 %collective-permute-start.13 = (bf16[128,256]{1,0:T(8,128)(2,1)S(1)}, bf16[128,256]{1,0:T(8,128)(2,1)S(1)}, u32[]{:S(2)}, u32[]{:S(2)}) collective-permute-start(bf16[128,256]{1,0:T(8,128)(2,1)S(1)} %get-tuple-element.52), channel_id=1, source_target_pairs={{0,6},{2,4},{4,2},{6,0},{8,14},{10,12},{12,10},{14,8},{1,7},{3,5},... | collective-permute-start | bytes 196616 | tf_op jit(solution)/shard_map/ppermute | solution.py:28
  34.6 4.8 %collective-permute-start.14 = (bf16[128,256]{1,0:T(8,128)(2,1)S(1)}, bf16[128,256]{1,0:T(8,128)(2,1)S(1)}, u32[]{:S(2)}, u32[]{:S(2)}) collective-permute-start(bf16[128,256]{1,0:T(8,128)(2,1)S(1)} %get-tuple-element.53), channel_id=1, source_target_pairs={{0,2},{2,0},{4,6},{6,4},{8,10},{10,8},{12,14},{14,12},{1,3},{3,1},... | collective-permute-start | bytes 196616 | tf_op jit(solution)/shard_map/ppermute | solution.py:28
  35.2 4.5 %collective-permute-start.15 = (bf16[128,256]{1,0:T(8,128)(2,1)S(1)}, bf16[128,256]{1,0:T(8,128)(2,1)S(1)}, u32[]{:S(2)}, u32[]{:S(2)}) collective-permute-start(bf16[128,256]{1,0:T(8,128)(2,1)S(1)} %get-tuple-element.54), channel_id=1, source_target_pairs={{0,4},{2,6},{4,0},{6,2},{8,12},{10,14},{12,8},{14,10},{1,5},{3,7},... | collective-permute-start | bytes 196616 | tf_op jit(solution)/shard_map/ppermute | solution.py:28
  40.1 1.2 %collective-permute-start.16 = (f32[1,256]{1,0:T(1,128)S(1)}, f32[1,256]{1,0:T(1,128)S(1)}, u32[]{:S(2)}, u32[]{:S(2)}) collective-permute-start(f32[1,256]{1,0:T(1,128)S(1)} %get-tuple-element.58), channel_id=1, source_target_pairs={{0,1},{1,0},{2,3},{3,2},{4,5},{5,4},{6,7},{7,6},{8,9},{9,8},{10,11... | collective-permute-start | bytes 3080 | tf_op jit(solution)/shard_map/ppermute | solution.py:24

commit v10 on v7

--- a/solution.py
+++ b/solution.py
@@ -302,18 +302,19 @@
                 finish(here, there, top / (tail + expo[0]))
 
 
-def gate_kernel(order, asked, ratio, rel, own_sum, theirs, inverse, plf, *refs):
-    rows = ratio.shape[0]
-    noted, gate, out = refs[: len(order)], refs[len(order)], refs[len(order) + 1 :]
-
+def gate_kernel(ratio, rel, own_sum, theirs, inverse, plf, gate):
     def finish(here, there, value):
         offset = value - plf[here]
         gate[here, there] = (1.0 / (1.0 + 4.0 * (offset * offset))).astype(BF16)
 
     called(ratio, rel, own_sum, theirs, inverse, finish)
+
+
+def own_gate_kernel(order, asked, gate, *refs):
+    noted, out = refs[: len(order)], refs[len(order) :]
     for k, ref in zip(order, out):
         spot = noted[k - 1].shape[0] - asked + k
-        ref[...] = pick(gate, line(noted[k - 1], spot), rows // RBLK)
+        ref[...] = pick(gate, line(noted[k - 1], spot), gate.shape[0] // RBLK)
 
 
 def pass_gate_kernel(order, asked, across, *refs):
@@ -378,10 +379,13 @@
         weight, total, own, table, partial, *[passed[k - 1] for k in order_of(PASSED, half)],
     )
     order = order_of(OWN_GATES, half)
-    gate, *gates = call(
-        functools.partial(gate_kernel, order, extra), "gate",
-        [((rows, cols), BF16)] + [((RBLK, cols), BF16)] * len(order),
-        ratio, rel, own_sum, swap_tgt(part), inverse, plf, *noted,
+    (gate,) = call(
+        gate_kernel, "gate", [((rows, cols), BF16)],
+        ratio, rel, own_sum, swap_tgt(part), inverse, plf,
+    )
+    gates = call(
+        functools.partial(own_gate_kernel, order, extra), "own_gates",
+        [((RBLK, cols), BF16)] * len(order), gate, *noted,
     )
     far = gate_across(half)
     far_gate = send(gate, far, count)

time: 42.9 us -> 42.9 us (level)
    pallas_call x12 -> x13, Pallas kernels: 7.67 us -> 7.68 us  [call(): pl.pallas_call(body, out_shape=[jax.ShapeDtypeStruct(shape, dtype) for sh...]
where the time goes in v10:
time: 42.9 us; the launch traced here: 42.7 us
  starting transfers between devices  21.5 us (50%)
  waiting for transfers between devices  11.4 us (27%)
  Pallas kernels  7.68 us (18%)
  local copies, waits for them, and re-layouts  2.02 us (5%)
    ppermute x14, starting transfers between devices, send(): return lax.ppermute(value, 'samp', [(i, i ^ step) for i in range(count)])  20.9 us
    ppermute x14, waiting for transfers between devices, send(): return lax.ppermute(value, 'samp', [(i, i ^ step) for i in range(count)])  8.9 us
    pallas_call x13, Pallas kernels, call(): pl.pallas_call(body, out_shape=[jax.ShapeDtypeStruct(shape, dtype) for sh...  7.68 us
    ppermute x3, waiting for transfers between devices, swap_tgt(): return lax.ppermute(value, 'tgt', [(0, 1), (1, 0)])  2.45 us
    unnamed x8, local copies, waits for them, and re-layouts  1 us
    pad x1, local copies, waits for them, and re-layouts, body(): counted = jnp.pad(coverage, ((0, LANE), (0, 0)), constant_values=1)  0.93 us
  transfers between devices with their start and end apart: 17, of which 11 were waited for; matrix products, arithmetic and copies ran while one was open for 0% of the time, Pallas kernels for 9%

profile of v10, /device:TPU:0, one launch (start us, length us, event | category | flops | bytes accessed | tf_op | source)
XLA Modules:
  0.0 42.7 jit_solution(15979849529672605152)
XLA Ops:
  0.0 0.9 %pad.4.coverage = bf16[384,256]{1,0:T(8,128)(2,1)S(1)} pad(bf16[256,256]{1,0:T(8,128)(2,1)} %param.5, bf16[]{:T(256)} %constant.2.clone.1), padding=0_128x0_0 | pad | bytes 327682 | tf_op jit(solution)/shard_map/jit(_pad)/pad | solution.py:343
  2.8 3.0 %collective-permute-start.3 = (bf16[272,256]{1,0:T(8,128)(2,1)S(1)}, bf16[272,256]{1,0:T(8,128)(2,1)S(1)}, u32[]{:S(2)}, u32[]{:S(2)}) collective-permute-start(bf16[272,256]{1,0:T(8,128)(2,1)S(1)} %get-tuple-element.30.noted.own), channel_id=1, source_target_pairs={{0,4},{2,6},{4,0},{6,2},{8,12},{10,14},{12,8},{14,10},{1,5},{3,7},... | collective-permute-start | bytes 417800 | tf_op jit(solution)/shard_map/ppermute | solution.py:28
  5.7 1.5 %collective-permute-start.2 = (bf16[272,256]{1,0:T(8,128)(2,1)S(1)}, bf16[272,256]{1,0:T(8,128)(2,1)S(1)}, u32[]{:S(2)}, u32[]{:S(2)}) collective-permute-start(bf16[272,256]{1,0:T(8,128)(2,1)S(1)} %get-tuple-element.30.noted.own), channel_id=1, source_target_pairs={{0,2},{2,0},{4,6},{6,4},{8,10},{10,8},{12,14},{14,12},{1,3},{3,1},... | collective-permute-start | bytes 417800 | tf_op jit(solution)/shard_map/ppermute | solution.py:28
  7.3 2.6 %collective-permute-start.1 = (bf16[256,256]{1,0:T(8,128)(2,1)S(1)}, bf16[256,256]{1,0:T(8,128)(2,1)S(1)}, u32[]{:S(2)}, u32[]{:S(2)}) collective-permute-start(bf16[256,256]{1,0:T(8,128)(2,1)S(1)} %get-tuple-element.33), channel_id=1, source_target_pairs={{0,8},{2,10},{4,12},{6,14},{8,0},{10,2},{12,4},{14,6},{1,9},{3,11}... | collective-permute-start | bytes 393224 | tf_op jit(solution)/shard_map/ppermute | solution.py:28
  10.3 0.7 %copy-done.1 = bf16[256,128]{1,0:T(8,128)(2,1)S(1)} copy-done((bf16[256,128]{1,0:T(8,128)(2,1)S(1)}, bf16[256,128]{1,0:T(8,128)(2,1)}, u32[]{:S(2)}) %copy-start.1) | copy-done | bytes 65560
  11.1 2.6 %weight_map.1 = (bf16[256,1024]{1,0:T(8,128)(2,1)S(1)}, f32[256,128]{1,0:T(8,128)S(1)}, f32[256,128]{1,0:T(8,128)S(1)}) custom-call(s32[256,128]{1,0:T(8,128)S(1)} %copy-done, bf16[256,128]{1,0:T(8,128)(2,1)S(1)} %copy-done.1, f32[256,128]{1,0:T(8,128)S(1)} %broadcast_in_dim.2.plf, bf16[272,256]{1,0:T(8,128)(2,1)S(1)} %get-tuple-element.30.noted.own), custom_call_target="tpu_custom_call" | custom-call | flops 1 | bytes 1 | tf_op jit(solution)/shard_map/weight_map/pallas_call | solution.py:49
  13.7 0.7 %collective-permute-done.4.refs_2_ = bf16[16,256]{1,0:T(8,128)(2,1)S(1)} collective-permute-done((bf16[16,256]{1,0:T(8,128)(2,1)S(1)}, bf16[16,256]{1,0:T(8,128)(2,1)S(1)}, u32[]{:S(2)}, u32[]{:S(2)}) %collective-permute-start.4) | collective-permute-done | bytes 8224 | tf_op jit(solution)/shard_map/ppermute | solution.py:28
  14.4 1.6 %collective-permute-done.1.across = bf16[256,256]{1,0:T(8,128)(2,1)S(1)} collective-permute-done((bf16[256,256]{1,0:T(8,128)(2,1)S(1)}, bf16[256,256]{1,0:T(8,128)(2,1)S(1)}, u32[]{:S(2)}, u32[]{:S(2)}) %collective-permute-start.1) | collective-permute-done | bytes 131104 | tf_op jit(solution)/shard_map/ppermute | solution.py:28
  16.5 1.6 %collective-permute-start.6 = (bf16[128,256]{1,0:T(8,128)(2,1)S(1)}, bf16[128,256]{1,0:T(8,128)(2,1)S(1)}, u32[]{:S(2)}, u32[]{:S(2)}) collective-permute-start(bf16[128,256]{1,0:T(8,128)(2,1)S(1)} %get-tuple-element.37), channel_id=1, source_target_pairs={{0,4},{2,6},{4,0},{6,2},{8,12},{10,14},{12,8},{14,10},{1,5},{3,7},... | collective-permute-start | bytes 196616 | tf_op jit(solution)/shard_map/ppermute | solution.py:28
  18.1 1.5 %collective-permute-start.7 = (bf16[128,256]{1,0:T(8,128)(2,1)S(1)}, bf16[128,256]{1,0:T(8,128)(2,1)S(1)}, u32[]{:S(2)}, u32[]{:S(2)}) collective-permute-start(bf16[128,256]{1,0:T(8,128)(2,1)S(1)} %get-tuple-element.38), channel_id=1, source_target_pairs={{0,2},{2,0},{4,6},{6,4},{8,10},{10,8},{12,14},{14,12},{1,3},{3,1},... | collective-permute-start | bytes 196616 | tf_op jit(solution)/shard_map/ppermute | solution.py:28
  19.9 1.8 %collective-permute-done.6.refs_1_ = bf16[128,256]{1,0:T(8,128)(2,1)S(1)} collective-permute-done((bf16[128,256]{1,0:T(8,128)(2,1)S(1)}, bf16[128,256]{1,0:T(8,128)(2,1)S(1)}, u32[]{:S(2)}, u32[]{:S(2)}) %collective-permute-start.6) | collective-permute-done | bytes 65568 | tf_op jit(solution)/shard_map/ppermute | solution.py:28
  21.7 0.9 %collective-permute-done.7.refs_2_ = bf16[128,256]{1,0:T(8,128)(2,1)S(1)} collective-permute-done((bf16[128,256]{1,0:T(8,128)(2,1)S(1)}, bf16[128,256]{1,0:T(8,128)(2,1)S(1)}, u32[]{:S(2)}, u32[]{:S(2)}) %collective-permute-start.7) | collective-permute-done | bytes 65568 | tf_op jit(solution)/shard_map/ppermute | solution.py:28
  23.2 1.1 %collective-permute-done.8.theirs = f32[1,256]{1,0:T(1,128)S(1)} collective-permute-done((f32[1,256]{1,0:T(1,128)S(1)}, f32[1,256]{1,0:T(1,128)S(1)}, u32[]{:S(2)}, u32[]{:S(2)}) %collective-permute-start.8) | collective-permute-done | bytes 1056 | tf_op jit(solution)/shard_map/ppermute | solution.py:24
  24.3 0.9 %gate.1 = bf16[256,256]{1,0:T(8,128)(2,1)S(1)} custom-call(f32[256,256]{1,0:T(8,128)S(1)} %get-tuple-element.40.ratio, f32[256,256]{1,0:T(8,128)S(1)} %get-tuple-element.41.rel, f32[256,128]{1,0:T(8,128)S(1)} %get-tuple-element.42.own_sum, f32[1,256]{1,0:T(1,128)S(1)} %collective-permute-done.8.theirs, f32[256,128]{1,0:T(8,128)S(1)} %get-tuple-element.44.inverse, ...), custom_call_target="tpu_custom_call" | custom-call | flops 1 | bytes 1 | tf_op jit(solution)/shard_map/gate/pallas_call | solution.py:49
  25.1 2.7 %collective-permute-start.9 = (bf16[256,256]{1,0:T(8,128)(2,1)S(1)}, bf16[256,256]{1,0:T(8,128)(2,1)S(1)}, u32[]{:S(2)}, u32[]{:S(2)}) collective-permute-start(bf16[256,256]{1,0:T(8,128)(2,1)S(1)} %gate.1), channel_id=1, source_target_pairs={{0,12},{2,14},{4,8},{6,10},{8,4},{10,6},{12,0},{14,2},{1,13},{3,15... | collective-permute-start | bytes 393224 | tf_op jit(solution)/shard_map/ppermute | solution.py:28
  28.0 2.5 %collective-permute-start.11 = (bf16[128,256]{1,0:T(8,128)(2,1)S(1)}, bf16[128,256]{1,0:T(8,128)(2,1)S(1)}, u32[]{:S(2)}, u32[]{:S(2)}) collective-permute-start(bf16[128,256]{1,0:T(8,128)(2,1)S(1)} %get-tuple-element.46), channel_id=1, source_target_pairs={{0,4},{2,6},{4,0},{6,2},{8,12},{10,14},{12,8},{14,10},{1,5},{3,7},... | collective-permute-start | bytes 196616 | tf_op jit(solution)/shard_map/ppermute | solution.py:28
  30.5 1.0 %collective-permute-start.12 = (bf16[128,256]{1,0:T(8,128)(2,1)S(1)}, bf16[128,256]{1,0:T(8,128)(2,1)S(1)}, u32[]{:S(2)}, u32[]{:S(2)}) collective-permute-start(bf16[128,256]{1,0:T(8,128)(2,1)S(1)} %get-tuple-element.47), channel_id=1, source_target_pairs={{0,2},{2,0},{4,6},{6,4},{8,10},{10,8},{12,14},{14,12},{1,3},{3,1},... | collective-permute-start | bytes 196616 | tf_op jit(solution)/shard_map/ppermute | solution.py:28
  31.4 2.0 %collective-permute-done.9.across = bf16[256,256]{1,0:T(8,128)(2,1)S(1)} collective-permute-done((bf16[256,256]{1,0:T(8,128)(2,1)S(1)}, bf16[256,256]{1,0:T(8,128)(2,1)S(1)}, u32[]{:S(2)}, u32[]{:S(2)}) %collective-permute-start.9) | collective-permute-done | bytes 131104 | tf_op jit(solution)/shard_map/ppermute | solution.py:28
  33.4 0.9 %collective-permute-start.13 = (bf16[128,256]{1,0:T(8,128)(2,1)S(1)}, bf16[128,256]{1,0:T(8,128)(2,1)S(1)}, u32[]{:S(2)}, u32[]{:S(2)}) collective-permute-start(bf16[128,256]{1,0:T(8,128)(2,1)S(1)} %get-tuple-element.48), channel_id=1, source_target_pairs={{0,6},{2,4},{4,2},{6,0},{8,14},{10,12},{12,10},{14,8},{1,7},{3,5},... | collective-permute-start | bytes 196616 | tf_op jit(solution)/shard_map/ppermute | solution.py:28
  34.3 0.8 %collective-permute-start.14 = (bf16[128,256]{1,0:T(8,128)(2,1)S(1)}, bf16[128,256]{1,0:T(8,128)(2,1)S(1)}, u32[]{:S(2)}, u32[]{:S(2)}) collective-permute-start(bf16[128,256]{1,0:T(8,128)(2,1)S(1)} %get-tuple-element.49), channel_id=1, source_target_pairs={{0,2},{2,0},{4,6},{6,4},{8,10},{10,8},{12,14},{14,12},{1,3},{3,1},... | collective-permute-start | bytes 196616 | tf_op jit(solution)/shard_map/ppermute | solution.py:28
  35.1 1.9 %collective-permute-start.15 = (bf16[128,256]{1,0:T(8,128)(2,1)S(1)}, bf16[128,256]{1,0:T(8,128)(2,1)S(1)}, u32[]{:S(2)}, u32[]{:S(2)}) collective-permute-start(bf16[128,256]{1,0:T(8,128)(2,1)S(1)} %get-tuple-element.50), channel_id=1, source_target_pairs={{0,4},{2,6},{4,0},{6,2},{8,12},{10,14},{12,8},{14,10},{1,5},{3,7},... | collective-permute-start | bytes 196616 | tf_op jit(solution)/shard_map/ppermute | solution.py:28
  37.5 1.6 %collective-permute-done.13.refs_0_ = bf16[128,256]{1,0:T(8,128)(2,1)S(1)} collective-permute-done((bf16[128,256]{1,0:T(8,128)(2,1)S(1)}, bf16[128,256]{1,0:T(8,128)(2,1)S(1)}, u32[]{:S(2)}, u32[]{:S(2)}) %collective-permute-start.13) | collective-permute-done | bytes 65568 | tf_op jit(solution)/shard_map/ppermute | solution.py:28
  40.0 1.1 %collective-permute-done.16.theirs = f32[1,256]{1,0:T(1,128)S(1)} collective-permute-done((f32[1,256]{1,0:T(1,128)S(1)}, f32[1,256]{1,0:T(1,128)S(1)}, u32[]{:S(2)}, u32[]{:S(2)}) %collective-permute-start.16) | collective-permute-done | bytes 1056 | tf_op jit(solution)/shard_map/ppermute | solution.py:24
  41.2 1.5 %copy_number.1 = f32[256,256]{1,0:T(8,128)} custom-call(f32[256,256]{1,0:T(8,128)S(1)} %get-tuple-element.51.ratio, f32[256,256]{1,0:T(8,128)S(1)} %get-tuple-element.52.rel, f32[256,128]{1,0:T(8,128)S(1)} %get-tuple-element.53.own_sum, f32[1,256]{1,0:T(1,128)S(1)} %collective-permute-done.16.theirs, f32[256,128]{1,0:T(8,128)S(1)} %get-tuple-element.44.inverse), custom_call_target="tpu_custom_call" | custom-call | flops 1 | bytes 1 | tf_op jit(solution)/shard_map/copy_number/pallas_call | solution.py:49
  (34 shorter events, 5.2 us)
Async XLA Ops:
  0.0 0.9 %copy-start.2 = (s32[256]{0:T(256)S(1)}, s32[256]{0:T(256)}, u32[]{:S(2)}) copy-start(s32[256]{0:T(256)} %param.9) | copy-start | bytes 3076
  0.9 0.9 %copy-start = (s32[256,128]{1,0:T(8,128)S(1)}, s32[256,128]{1,0:T(8,128)}, u32[]{:S(2)}) copy-start(s32[256,128]{1,0:T(8,128)} %neighbours.3) | copy-start | bytes 393220
  1.1 1.3 %collective-permute-start = (f32[8,384]{1,0:T(8,128)S(1)}, f32[8,384]{1,0:T(8,128)S(1)}, u32[]{:S(2)}, u32[]{:S(2)}) collective-permute-start(f32[8,384]{1,0:T(8,128)S(1)} %bin_sums.1.mine), channel_id=1, source_target_pairs={{0,1},{1,0},{2,3},{3,2},{4,5},{5,4},{6,7},{7,6},{8,9},{9,8},{10,11... | collective-permute-start | bytes 36872 | tf_op jit(solution)/shard_map/ppermute | solution.py:24
  2.7 7.5 %copy-start.3 = (s32[256]{0:T(256)S(1)}, s32[256]{0:T(256)}, u32[]{:S(2)}) copy-start(s32[256]{0:T(256)} %param.8) | copy-start | bytes 3076
  2.8 13.2 %collective-permute-start.3 = (bf16[272,256]{1,0:T(8,128)(2,1)S(1)}, bf16[272,256]{1,0:T(8,128)(2,1)S(1)}, u32[]{:S(2)}, u32[]{:S(2)}) collective-permute-start(bf16[272,256]{1,0:T(8,128)(2,1)S(1)} %get-tuple-element.30.noted.own), channel_id=1, source_target_pairs={{0,4},{2,6},{4,0},{6,2},{8,12},{10,14},{12,8},{14,10},{1,5},{3,7},... | collective-permute-start | bytes 417800 | tf_op jit(solution)/shard_map/ppermute | solution.py:28
  5.7 10.2 %collective-permute-start.2 = (bf16[272,256]{1,0:T(8,128)(2,1)S(1)}, bf16[272,256]{1,0:T(8,128)(2,1)S(1)}, u32[]{:S(2)}, u32[]{:S(2)}) collective-permute-start(bf16[272,256]{1,0:T(8,128)(2,1)S(1)} %get-tuple-element.30.noted.own), channel_id=1, source_target_pairs={{0,2},{2,0},{4,6},{6,4},{8,10},{10,8},{12,14},{14,12},{1,3},{3,1},... | collective-permute-start | bytes 417800 | tf_op jit(solution)/shard_map/ppermute | solution.py:28
  7.3 8.7 %collective-permute-start.1 = (bf16[256,256]{1,0:T(8,128)(2,1)S(1)}, bf16[256,256]{1,0:T(8,128)(2,1)S(1)}, u32[]{:S(2)}, u32[]{:S(2)}) collective-permute-start(bf16[256,256]{1,0:T(8,128)(2,1)S(1)} %get-tuple-element.33), channel_id=1, source_target_pairs={{0,8},{2,10},{4,12},{6,14},{8,0},{10,2},{12,4},{14,6},{1,9},{3,11}... | collective-permute-start | bytes 393224 | tf_op jit(solution)/shard_map/ppermute | solution.py:28
  9.8 4.5 %collective-permute-start.4 = (bf16[16,256]{1,0:T(8,128)(2,1)S(1)}, bf16[16,256]{1,0:T(8,128)(2,1)S(1)}, u32[]{:S(2)}, u32[]{:S(2)}) collective-permute-start(bf16[16,256]{1,0:T(8,128)(2,1)S(1)} %choices.1.ask), channel_id=1, source_target_pairs={{0,6},{2,4},{4,2},{6,0},{8,14},{10,12},{12,10},{14,8},{1,7},{3,5},... | collective-permute-start | bytes 24584 | tf_op jit(solution)/shard_map/ppermute | solution.py:28
  10.2 0.8 %copy-start.1 = (bf16[256,128]{1,0:T(8,128)(2,1)S(1)}, bf16[256,128]{1,0:T(8,128)(2,1)}, u32[]{:S(2)}) copy-start(bf16[256,128]{1,0:T(8,128)(2,1)} %weight.1) | copy-start | bytes 196612
  16.0 6.6 %collective-permute-start.5 = (bf16[256,256]{1,0:T(8,128)(2,1)S(1)}, bf16[256,256]{1,0:T(8,128)(2,1)S(1)}, u32[]{:S(2)}, u32[]{:S(2)}) collective-permute-start(bf16[256,256]{1,0:T(8,128)(2,1)S(1)} %get-tuple-element.36), channel_id=1, source_target_pairs={{0,6},{2,4},{4,2},{6,0},{8,14},{10,12},{12,10},{14,8},{1,7},{3,5},... | collective-permute-start | bytes 393224 | tf_op jit(solution)/shard_map/ppermute | solution.py:28
  16.5 5.2 %collective-permute-start.6 = (bf16[128,256]{1,0:T(8,128)(2,1)S(1)}, bf16[128,256]{1,0:T(8,128)(2,1)S(1)}, u32[]{:S(2)}, u32[]{:S(2)}) collective-permute-start(bf16[128,256]{1,0:T(8,128)(2,1)S(1)} %get-tuple-element.37), channel_id=1, source_target_pairs={{0,4},{2,6},{4,0},{6,2},{8,12},{10,14},{12,8},{14,10},{1,5},{3,7},... | collective-permute-start | bytes 196616 | tf_op jit(solution)/shard_map/ppermute | solution.py:28
  18.1 4.6 %collective-permute-start.7 = (bf16[128,256]{1,0:T(8,128)(2,1)S(1)}, bf16[128,256]{1,0:T(8,128)(2,1)S(1)}, u32[]{:S(2)}, u32[]{:S(2)}) collective-permute-start(bf16[128,256]{1,0:T(8,128)(2,1)S(1)} %get-tuple-element.38), channel_id=1, source_target_pairs={{0,2},{2,0},{4,6},{6,4},{8,10},{10,8},{12,14},{14,12},{1,3},{3,1},... | collective-permute-start | bytes 196616 | tf_op jit(solution)/shard_map/ppermute | solution.py:28
  23.1 1.2 %collective-permute-start.8 = (f32[1,256]{1,0:T(1,128)S(1)}, f32[1,256]{1,0:T(1,128)S(1)}, u32[]{:S(2)}, u32[]{:S(2)}) collective-permute-start(f32[1,256]{1,0:T(1,128)S(1)} %get-tuple-element.43), channel_id=1, source_target_pairs={{0,1},{1,0},{2,3},{3,2},{4,5},{5,4},{6,7},{7,6},{8,9},{9,8},{10,11... | collective-permute-start | bytes 3080 | tf_op jit(solution)/shard_map/ppermute | solution.py:24
  25.1 8.2 %collective-permute-start.9 = (bf16[256,256]{1,0:T(8,128)(2,1)S(1)}, bf16[256,256]{1,0:T(8,128)(2,1)S(1)}, u32[]{:S(2)}, u32[]{:S(2)}) collective-permute-start(bf16[256,256]{1,0:T(8,128)(2,1)S(1)} %gate.1), channel_id=1, source_target_pairs={{0,12},{2,14},{4,8},{6,10},{8,4},{10,6},{12,0},{14,2},{1,13},{3,15... | collective-permute-start | bytes 393224 | tf_op jit(solution)/shard_map/ppermute | solution.py:28
  27.9 7.2 %collective-permute-start.10 = (bf16[128,256]{1,0:T(8,128)(2,1)S(1)}, bf16[128,256]{1,0:T(8,128)(2,1)S(1)}, u32[]{:S(2)}, u32[]{:S(2)}) collective-permute-start(bf16[128,256]{1,0:T(8,128)(2,1)S(1)} %get-tuple-element.45), channel_id=1, source_target_pairs={{0,6},{2,4},{4,2},{6,0},{8,14},{10,12},{12,10},{14,8},{1,7},{3,5},... | collective-permute-start | bytes 196616 | tf_op jit(solution)/shard_map/ppermute | solution.py:28
  28.0 9.0 %collective-permute-start.11 = (bf16[128,256]{1,0:T(8,128)(2,1)S(1)}, bf16[128,256]{1,0:T(8,128)(2,1)S(1)}, u32[]{:S(2)}, u32[]{:S(2)}) collective-permute-start(bf16[128,256]{1,0:T(8,128)(2,1)S(1)} %get-tuple-element.46), channel_id=1, source_target_pairs={{0,4},{2,6},{4,0},{6,2},{8,12},{10,14},{12,8},{14,10},{1,5},{3,7},... | collective-permute-start | bytes 196616 | tf_op jit(solution)/shard_map/ppermute | solution.py:28
  30.5 6.5 %collective-permute-start.12 = (bf16[128,256]{1,0:T(8,128)(2,1)S(1)}, bf16[128,256]{1,0:T(8,128)(2,1)S(1)}, u32[]{:S(2)}, u32[]{:S(2)}) collective-permute-start(bf16[128,256]{1,0:T(8,128)(2,1)S(1)} %get-tuple-element.47), channel_id=1, source_target_pairs={{0,2},{2,0},{4,6},{6,4},{8,10},{10,8},{12,14},{14,12},{1,3},{3,1},... | collective-permute-start | bytes 196616 | tf_op jit(solution)/shard_map/ppermute | solution.py:28
  33.4 5.7 %collective-permute-start.13 = (bf16[128,256]{1,0:T(8,128)(2,1)S(1)}, bf16[128,256]{1,0:T(8,128)(2,1)S(1)}, u32[]{:S(2)}, u32[]{:S(2)}) collective-permute-start(bf16[128,256]{1,0:T(8,128)(2,1)S(1)} %get-tuple-element.48), channel_id=1, source_target_pairs={{0,6},{2,4},{4,2},{6,0},{8,14},{10,12},{12,10},{14,8},{1,7},{3,5},... | collective-permute-start | bytes 196616 | tf_op jit(solution)/shard_map/ppermute | solution.py:28
  34.3 5.0 %collective-permute-start.14 = (bf16[128,256]{1,0:T(8,128)(2,1)S(1)}, bf16[128,256]{1,0:T(8,128)(2,1)S(1)}, u32[]{:S(2)}, u32[]{:S(2)}) collective-permute-start(bf16[128,256]{1,0:T(8,128)(2,1)S(1)} %get-tuple-element.49), channel_id=1, source_target_pairs={{0,2},{2,0},{4,6},{6,4},{8,10},{10,8},{12,14},{14,12},{1,3},{3,1},... | collective-permute-start | bytes 196616 | tf_op jit(solution)/shard_map/ppermute | solution.py:28
  35.1 4.3 %collective-permute-start.15 = (bf16[128,256]{1,0:T(8,128)(2,1)S(1)}, bf16[128,256]{1,0:T(8,128)(2,1)S(1)}, u32[]{:S(2)}, u32[]{:S(2)}) collective-permute-start(bf16[128,256]{1,0:T(8,128)(2,1)S(1)} %get-tuple-element.50), channel_id=1, source_target_pairs={{0,4},{2,6},{4,0},{6,2},{8,12},{10,14},{12,8},{14,10},{1,5},{3,7},... | collective-permute-start | bytes 196616 | tf_op jit(solution)/shard_map/ppermute | solution.py:28
  40.0 1.2 %collective-permute-start.16 = (f32[1,256]{1,0:T(1,128)S(1)}, f32[1,256]{1,0:T(1,128)S(1)}, u32[]{:S(2)}, u32[]{:S(2)}) collective-permute-start(f32[1,256]{1,0:T(1,128)S(1)} %get-tuple-element.54), channel_id=1, source_target_pairs={{0,1},{1,0},{2,3},{3,2},{4,5},{5,4},{6,7},{7,6},{8,9},{9,8},{10,11... | collective-permute-start | bytes 3080 | tf_op jit(solution)/shard_map/ppermute | solution.py:24
